TPU v7x, 32 devices: a whole 2x2x4 slice. The times are simulated.
32 devices in a mesh: rows: 8 (over y, x, core), chan: 4 (over z).
Axes of the slice: x: 2, y: 2, z: 4, core: 2. Of those that a mesh axis runs over, the one named last changes fastest.
Arguments:
- frame_adjoint: bfloat16 [8, 192, 8, 128], P('rows', 'chan'), may hold values from -6 to 6
- frame_slot: int32 [8], replicated, may hold values from 0 to 7, each once
- inputs: bfloat16 [8, 192, 8, 128], P(None, 'chan', 'rows')
- gain: float32 [192], P('chan'), may hold values from 0.1 to 1.9
- weight: bfloat16 [27, 192, 192], P(None, 'chan'), may hold values from -0.078125 to 0.078125
Outputs:
- input_adjoint: bfloat16 [8, 192, 8, 128], P(None, 'chan', 'rows')
- weight_adjoint: float32 [27, 192, 192], P(None, 'chan')
Inputs may be any that keep to these rules, and one draw needn't show every extreme that they name: `frame_slot`: each frame appears in exactly one slot.
All inputs are finite; a program needn't handle non-finite values.
Results may differ from a plain program's by a relative error of at most 0.003.
Values may be sent and summed in bfloat16 or wider, within the bound.
No kernel may reach another device: no remote copies, remote signals or barrier semaphores. Data moves between devices by JAX's collectives and lax.ppermute only.
A program may use at most 128 MiB of HBM per device.

v0:
```python
import jax
import jax.numpy as jnp
from jax import lax
from jax.sharding import PartitionSpec as P

CHANNELS = 192


epsilon = 1e-06


def extended(block, sides, width):
    for axis, dim in sides:
        count = lax.axis_size(axis)
        forward = [(i, i + 1) for i in range(count - 1)]
        backward = [(target, source) for source, target in forward]
        low = lax.ppermute(
            lax.slice_in_dim(block, block.shape[dim] - width, None, axis=dim), axis, forward
        )
        high = lax.ppermute(lax.slice_in_dim(block, 0, width, axis=dim), axis, backward)
        block = jnp.concatenate([low, block, high], axis=dim)
    return block


def transpose_conv(padded, kernel, frames, rows, width):
    summed = jnp.zeros((frames, kernel.shape[2], rows, width), jnp.float32)
    for frame_off in range(3):
        windows = []
        for row_off in range(3):
            for col_off in range(3):
                windows.append(
                    padded[
                        2 - frame_off : 2 - frame_off + frames,
                        :,
                        2 - row_off : 2 - row_off + rows,
                        2 - col_off : 2 - col_off + width,
                    ]
                )
        stacked = jnp.stack(windows)
        taps = kernel[frame_off * 9 : frame_off * 9 + 9]
        summed = summed + jnp.einsum(
            "kforw,koc->fcrw", stacked, taps, preferred_element_type=jnp.float32
        )
    return summed


def kernel_grad(adjoint, padded, frames, rows, width):
    grad_list = []
    for frame_off in range(3):
        windows = []
        for row_off in range(3):
            for col_off in range(3):
                windows.append(
                    padded[
                        frame_off : frame_off + frames,
                        :,
                        row_off : row_off + rows,
                        col_off : col_off + width,
                    ]
                )
        stacked = jnp.stack(windows)
        grad_list.append(
            jnp.einsum("forw,kfcrw->koc", adjoint, stacked, preferred_element_type=jnp.float32)
        )
    return jnp.concatenate(grad_list, axis=0)


def shards(frame_adjoint, frame_slot, inputs, gain, weight):
    arrived = lax.all_to_all(frame_adjoint, "rows", split_axis=2, concat_axis=0, tiled=True)
    frames = arrived.shape[0]
    rows = arrived.shape[2]
    width = arrived.shape[3]
    onehot = (frame_slot[None, :] == jnp.arange(frames, dtype=jnp.int32)[:, None]).astype(
        jnp.bfloat16
    )
    adjoint = jnp.einsum(
        "tj,jcrw->tcrw", onehot, arrived, preferred_element_type=jnp.float32
    ).astype(jnp.bfloat16)
    values = inputs.astype(jnp.float32)
    squares = lax.psum(jnp.sum(values * values, axis=1), "chan")
    scale = lax.rsqrt(squares / CHANNELS + epsilon)[:, None]
    normed = values * scale * gain[None, :, None, None]
    sigma = jax.nn.sigmoid(normed)
    hidden = (normed * sigma).astype(jnp.bfloat16)
    hidden_rim = extended(hidden, (("rows", 2),), 1)
    hidden_pad = jnp.pad(hidden_rim, ((2, 0), (0, 0), (0, 0), (1, 1)))
    adjoint_rim = extended(adjoint, (("rows", 2),), 1)
    adjoint_pad = jnp.pad(adjoint_rim, ((0, 2), (0, 0), (0, 0), (1, 1)))
    factor = float(frames * rows * lax.axis_size("rows") * width) ** (-0.5)
    local_grad = (
        kernel_grad(
            adjoint, lax.all_gather(hidden_pad, "chan", axis=1, tiled=True), frames, rows, width
        )
        * factor
    )
    partial_sum = transpose_conv(adjoint_pad, weight, frames, rows, width)
    hidden_adjoint = lax.psum_scatter(partial_sum, "chan", scatter_dimension=1, tiled=True)
    weight_adjoint = lax.psum(local_grad, "rows")
    normed_adjoint = (
        hidden_adjoint * sigma * (1.0 + normed * (1.0 - sigma)) * gain[None, :, None, None]
    )
    projection = lax.psum(jnp.sum(normed_adjoint * values, axis=1), "chan")[:, None]
    input_adjoint = scale * normed_adjoint - values * scale * scale * scale * projection / CHANNELS
    return (input_adjoint.astype(jnp.bfloat16), weight_adjoint)


def solution(mesh):
    in_specs = (
        P("rows", "chan", None, None),
        P(),
        P(None, "chan", "rows", None),
        P("chan"),
        P(None, "chan", None),
    )
    out_specs = (P(None, "chan", "rows", None), P(None, "chan", None))
    return jax.shard_map(shards, mesh=mesh, in_specs=in_specs, out_specs=out_specs, check_vma=False)
```

profile of v0, /device:TPU:0, one launch (start us, length us, event | category | flops | bytes accessed | tf_op | source)
XLA Modules:
  0.0 215.6 jit_solution(17038652010754487436)
XLA Ops:
  8.1 10.2 %all_to_all.15 = bf16[1,48,8,128]{3,1,0,2:T(8,128)(2,1)S(1)} all-to-all(bf16[1,48,8,128]{3,1,0,2:T(8,128)(2,1)S(1)} %copy.16), channel_id=1, replica_groups=mesh['rows'=8,'chan'=4] {'rows'}, dimensions={2} | all-to-all | bytes 196608 | tf_op jit(solution)/shard_map/all_to_all | solution.py:69
  19.2 1.3 collective-permute-start.1
  20.5 3.0 %collective-permute-start = (bf16[8,48,1,128]{3,0,1,2:T(8,128)(2,1)S(1)}, bf16[8,48,1,128]{3,0,1,2:T(8,128)(2,1)S(1)}, u32[]{:S(2)}, u32[]{:S(2)}) collective-permute-start(bf16[8,48,1,128]{3,0,1,2:T(8,128)(2,1)S(1)} %bitcast.309), channel_id=1, source_target_pairs={{0,4},{4,8},{8,12},{12,16},{16,20},{20,24},{24,28},{1,5},{5,9},{9,... | collective-permute-start | bytes 294920 | tf_op jit(solution)/shard_map/ppermute | solution.py:17
  27.2 1.3 fusion.18
  28.6 12.1 %psum.21 = f32[8,1,128]{2,0,1:T(8,128)S(1)} all-reduce(f32[8,1,128]{2,0,1:T(8,128)S(1)} %bitcast.314), channel_id=1, replica_groups=mesh['rows'=8,'chan'=4] {'chan'}, use_global_device_ids=true, to_apply=%region_1.0 | all-reduce | flops 1024 | bytes 8192 | tf_op jit(solution)/shard_map/psum | solution.py:80
  40.7 15.1 %reduce-scatter.2.cloned.1.call-done = f32[8,48,1,128]{3,1,0,2:T(8,128)} async-done(((f32[8,192,1,128]{3,1,0,2:T(8,128)}), f32[8,48,1,128]{3,1,0,2:T(8,128)}) %reduce-scatter.2.cloned.1.call-update) | async-done | bytes 196624 | tf_op jit(solution)/shard_map/reduce_scatter | solution.py:97
  57.0 1.3 collective-permute-start.3
  58.3 3.0 %collective-permute-start.2 = (bf16[8,48,1,128]{3,1,0,2:T(8,128)(2,1)S(1)}, bf16[8,48,1,128]{3,1,0,2:T(8,128)(2,1)S(1)}, u32[]{:S(2)}, u32[]{:S(2)}) collective-permute-start(bf16[8,48,1,128]{3,1,0,2:T(8,128)(2,1)S(1)} %get-tuple-element.56), channel_id=1, source_target_pairs={{0,4},{4,8},{8,12},{12,16},{16,20},{20,24},{24,28},{1,5},{5,9},{9,... | collective-permute-start | bytes 294920 | tf_op jit(solution)/shard_map/ppermute | solution.py:17
  63.4 62.8 %all-gather.2.cloned.1.call-done = bf16[10,192,3,130]{3,1,0,2:T(8,128)(2,1)} async-done(((bf16[10,48,3,130]{3,1,0,2:T(8,128)(2,1)}), bf16[10,192,3,130]{3,1,0,2:T(8,128)(2,1)}) %all-gather.2.cloned.1.call-update) | async-done | bytes 1497616 | tf_op jit(solution)/shard_map/all_gather | solution.py:92
  126.2 1.5 fusion.67
  127.7 2.3 %fusion.66 = (bf16[9,8,192,1,128]{4,2,1,3,0:T(8,128)(2,1)S(1)}, bf16[9,8,192,1,128]{4,2,1,3,0:T(8,128)(2,1)S(1)}, bf16[9,8,192,1,128]{4,2,1,3,0:T(8,128)(2,1)S(1)}) fusion(bf16[9,8,192,1,128]{4,2,1,3,0:T(8,128)(2,1)S(1)} %get-tuple-element.30, bf16[10,192,3,130]{3,1,0,2:T(8,128)(2,1)} %all-gather.2.cloned.1.call-done, ...), kind=kLoop, calls=%fused_computation.97 | loop fusion | bytes 2359296
  130.1 2.3 %fusion.65 = (bf16[9,8,192,1,128]{4,2,1,3,0:T(8,128)(2,1)S(1)}, bf16[9,8,192,1,128]{4,2,1,3,0:T(8,128)(2,1)S(1)}, bf16[9,8,192,1,128]{4,2,1,3,0:T(8,128)(2,1)S(1)}) fusion(bf16[9,8,192,1,128]{4,2,1,3,0:T(8,128)(2,1)S(1)} %get-tuple-element.27, bf16[10,192,3,130]{3,1,0,2:T(8,128)(2,1)} %all-gather.2.cloned.1.call-done, ...), kind=kLoop, calls=%fused_computation.95 | loop fusion | bytes 2359296
  132.4 1.5 fusion.64
  133.9 2.5 %fusion.63 = (bf16[9,8,192,1,128]{4,2,1,3,0:T(8,128)(2,1)S(1)}, bf16[9,8,192,1,128]{4,2,1,3,0:T(8,128)(2,1)S(1)}, bf16[9,8,192,1,128]{4,2,1,3,0:T(8,128)(2,1)S(1)}) fusion(bf16[9,8,192,1,128]{4,2,1,3,0:T(8,128)(2,1)S(1)} %get-tuple-element.21, bf16[10,192,3,130]{3,1,0,2:T(8,128)(2,1)} %all-gather.2.cloned.1.call-done, ...), kind=kLoop, calls=%fused_computation.91 | loop fusion | bytes 2359296
  136.4 2.5 %fusion.62 = (bf16[9,8,192,1,128]{4,2,1,3,0:T(8,128)(2,1)S(1)}, bf16[9,8,192,1,128]{4,2,1,3,0:T(8,128)(2,1)S(1)}, bf16[9,8,192,1,128]{4,2,1,3,0:T(8,128)(2,1)S(1)}) fusion(bf16[9,8,192,1,128]{4,2,1,3,0:T(8,128)(2,1)S(1)} %get-tuple-element.18, bf16[10,192,3,130]{3,1,0,2:T(8,128)(2,1)} %all-gather.2.cloned.1.call-done, ...), kind=kLoop, calls=%fused_computation.89 | loop fusion | bytes 2359296
  138.8 1.4 fusion.61
  140.3 2.3 %fusion.60 = (bf16[9,8,192,1,128]{4,2,1,3,0:T(8,128)(2,1)S(1)}, bf16[9,8,192,1,128]{4,2,1,3,0:T(8,128)(2,1)S(1)}, bf16[9,8,192,1,128]{4,2,1,3,0:T(8,128)(2,1)S(1)}) fusion(bf16[9,8,192,1,128]{4,2,1,3,0:T(8,128)(2,1)S(1)} %get-tuple-element.12, bf16[10,192,3,130]{3,1,0,2:T(8,128)(2,1)} %all-gather.2.cloned.1.call-done, ...), kind=kLoop, calls=%fused_computation.85 | loop fusion | bytes 2359296
  142.6 2.3 %fusion.59 = (bf16[9,8,192,1,128]{4,2,1,3,0:T(8,128)(2,1)S(1)}, bf16[9,8,192,1,128]{4,2,1,3,0:T(8,128)(2,1)S(1)}, bf16[9,8,192,1,128]{4,2,1,3,0:T(8,128)(2,1)S(1)}) fusion(bf16[9,8,192,1,128]{4,2,1,3,0:T(8,128)(2,1)S(1)} %get-tuple-element.9, bf16[10,192,3,130]{3,1,0,2:T(8,128)(2,1)} %all-gather.2.cloned.1.call-done, ...), kind=kLoop, calls=%fused_computation.83 | loop fusion | bytes 2359296 | tf_op jit(solution)/shard_map/stack | solution.py:61
  146.1 1.2 fusion.25
  147.3 1.2 fusion.22
  148.5 1.2 maximum_multiply_fusion
  149.8 9.2 %psum.22 = f32[8,128]{1,0:T(8,128)S(1)} all-reduce(f32[8,128]{1,0:T(8,128)S(1)} %get-tuple-element.57), channel_id=1, replica_groups=mesh['rows'=8,'chan'=4] {'chan'}, use_global_device_ids=true, to_apply=%region_4.5 | all-reduce | flops 1024 | bytes 8192 | tf_op jit(solution)/shard_map/psum | solution.py:102
  159.7 46.8 %all-reduce.4.cloned.1.call-done = f32[27,48,192]{2,1,0:T(8,128)} async-done(((f32[27,48,192]{2,1,0:T(8,128)}), f32[27,48,192]{2,1,0:T(8,128)}) %all-reduce.4.cloned.1.call-update) | async-done | bytes 995344 | tf_op jit(solution)/shard_map/psum | solution.py:98
  206.6 2.5 %copy.102 = f32[27,48,192]{2,1,0:T(8,128)} copy(f32[27,48,192]{2,1,0:T(8,128)} %all-reduce.4.cloned.1.call-done) | data formatting | bytes 1990656
  (42 shorter events, 10.8 us)
Async XLA Ops:
  7.2 48.7 %reduce-scatter.2.cloned.1.call-start = ((), (), s32[]{:S(2)}) async-start(), calls=%async_computation.2 | async-start | bytes 983040 | tf_op jit(solution)/shard_map/reduce_scatter | solution.py:97
  18.3 8.1 %copy-start.2 = (bf16[27,48,192]{2,1,0:T(8,128)(2,1)S(1)}, bf16[27,48,192]{2,1,0:T(8,128)(2,1)}, u32[]{:S(2)}) copy-start(bf16[27,48,192]{2,1,0:T(8,128)(2,1)} %param.9) | copy-start | bytes 1492996
  19.2 4.3 %collective-permute-start.1 = (bf16[8,48,1,128]{3,0,1,2:T(8,128)(2,1)S(1)}, bf16[8,48,1,128]{3,0,1,2:T(8,128)(2,1)S(1)}, u32[]{:S(2)}, u32[]{:S(2)}) collective-permute-start(bf16[8,48,1,128]{3,0,1,2:T(8,128)(2,1)S(1)} %bitcast.308), channel_id=1, source_target_pairs={{4,0},{8,4},{12,8},{16,12},{20,16},{24,20},{28,24},{5,1},{9,5},{13... | collective-permute-start | bytes 294920 | tf_op jit(solution)/shard_map/ppermute | solution.py:20
  20.5 4.0 %collective-permute-start = (bf16[8,48,1,128]{3,0,1,2:T(8,128)(2,1)S(1)}, bf16[8,48,1,128]{3,0,1,2:T(8,128)(2,1)S(1)}, u32[]{:S(2)}, u32[]{:S(2)}) collective-permute-start(bf16[8,48,1,128]{3,0,1,2:T(8,128)(2,1)S(1)} %bitcast.309), channel_id=1, source_target_pairs={{0,4},{4,8},{8,12},{12,16},{16,20},{20,24},{24,28},{1,5},{5,9},{9,... | collective-permute-start | bytes 294920 | tf_op jit(solution)/shard_map/ppermute | solution.py:17
  26.8 1.8 copy-start
  26.8 29.0 %copy-start.3 = (f32[48]{0:T(128)S(1)}, f32[48]{0:T(128)}, u32[]{:S(2)}) copy-start(f32[48]{0:T(128)} %param.8) | copy-start | bytes 580
  28.5 97.7 %all-gather.2.cloned.1.call-start = ((), (), s32[]{:S(2)}) async-start(), calls=%async_computation.3 | async-start | bytes 3686400 | tf_op jit(solution)/shard_map/all_gather | solution.py:92
  57.0 4.3 %collective-permute-start.3 = (bf16[8,48,1,128]{3,1,0,2:T(8,128)(2,1)S(1)}, bf16[8,48,1,128]{3,1,0,2:T(8,128)(2,1)S(1)}, u32[]{:S(2)}, u32[]{:S(2)}) collective-permute-start(bf16[8,48,1,128]{3,1,0,2:T(8,128)(2,1)S(1)} %get-tuple-element.56), channel_id=1, source_target_pairs={{4,0},{8,4},{12,8},{16,12},{20,16},{24,20},{28,24},{5,1},{9,5},{13... | collective-permute-start | bytes 294920 | tf_op jit(solution)/shard_map/ppermute | solution.py:20
  58.3 4.0 %collective-permute-start.2 = (bf16[8,48,1,128]{3,1,0,2:T(8,128)(2,1)S(1)}, bf16[8,48,1,128]{3,1,0,2:T(8,128)(2,1)S(1)}, u32[]{:S(2)}, u32[]{:S(2)}) collective-permute-start(bf16[8,48,1,128]{3,1,0,2:T(8,128)(2,1)S(1)} %get-tuple-element.56), channel_id=1, source_target_pairs={{0,4},{4,8},{8,12},{12,16},{16,20},{20,24},{24,28},{1,5},{5,9},{9,... | collective-permute-start | bytes 294920 | tf_op jit(solution)/shard_map/ppermute | solution.py:17
  63.4 143.2 %all-reduce.4.cloned.1.call-start = ((), (), s32[]{:S(2)}) async-start(), calls=%async_computation.4 | async-start | bytes 2654208 | tf_op jit(solution)/shard_map/psum | solution.py:98
  147.3 11.6 %copy-start.1 = (f32[8,48,1,128]{3,1,0,2:T(8,128)S(1)}, f32[8,48,1,128]{3,1,0,2:T(8,128)}, u32[]{:S(2)}) copy-start(f32[8,48,1,128]{3,1,0,2:T(8,128)} %reduce-scatter.2.cloned.1.call-done) | copy-start | bytes 589828
Sparse Core Ops, SparseCore 0:
  28.7 27.1 reduce-scatter.1
  63.5 62.6 all-gather.1
  149.9 56.6 all-reduce.3
where the time goes:
time: 216 us
  waiting for transfers between devices  127 us (59%)
  blocking collectives  31.4 us (15%)
  local copies, waits for them, and re-layouts  23.6 us (11%)
  between operations  14 us (6%)
  starting transfers between devices  8.77 us (4%)
  matrix products  6.6 us (3%)
  other arithmetic  4.63 us (2%)
    all_gather x1, waiting for transfers between devices, shards(): lax.all_gather(hidden_pad, 'chan', axis=1, tiled=True)  62.8 us
    psum x1, waiting for transfers between devices, shards(): weight_adjoint = lax.psum(local_grad, 'rows')  46.8 us
    unnamed x29, local copies, waits for them, and re-layouts  21.2 us
    reduce_scatter x1, waiting for transfers between devices, shards(): lax.psum_scatter(partial_sum, 'chan', scatter_dimension=1, tiled=True)  15.1 us
    psum x1, blocking collectives, shards(): squares = lax.psum(jnp.sum(values * values, axis=1), 'chan')  12.1 us
    all_to_all x1, blocking collectives, shards(): lax.all_to_all(frame_adjoint, 'rows', split_axis=2, concat_axis=0, tiled=...  10.2 us
    psum x1, blocking collectives, shards(): lax.psum(jnp.sum(normed_adjoint * values, axis=1), 'chan')[:, None]  9.15 us
    ppermute x2, starting transfers between devices, extended(): lax.ppermute(lax.slice_in_dim(block, block.shape[dim] - width, None, axis...  6.07 us
  transfers between devices with their start and end apart: 7, of which 5 were waited for; matrix products, arithmetic and copies ran while one was open for 0% of the time, Pallas kernels for 0%

commit v1 on v0

v1 whole, which is shorter than its diff:
```python
import functools

import jax
import jax.numpy as jnp
from jax import lax
from jax.experimental import pallas as pl
from jax.experimental.pallas import tpu as pltpu
from jax.sharding import PartitionSpec as P

CHANNELS = 192
EPSILON = 1e-06
MIB = 1024 * 1024


def round_up(value, unit):
    return -(-value // unit) * unit


def packing(taps_out, ins, count):
    blocks, rest = divmod(ins, 128)
    half = round_up(-(-taps_out // 2), 16) if rest else 0
    return blocks, rest, half, round_up(blocks * taps_out + half, 16 * count)


def vmem():
    return pl.BlockSpec(memory_space=pltpu.VMEM)


def smem():
    return pl.BlockSpec(memory_space=pltpu.SMEM)


def limit(taps_out, pixels):
    return pltpu.CompilerParams(vmem_limit_bytes=10 * MIB + 6 * taps_out * pixels)


def cost(rows, columns, depth):
    return pl.CostEstimate(
        flops=2 * rows * columns * depth,
        bytes_accessed=2 * (rows * depth + columns * depth),
        transcendentals=columns * depth,
    )


def gains(x_refs, start, group):
    found = []
    for ref in x_refs:
        rows = ref[pl.ds(start, 16), :].astype(jnp.float32)
        gain = rows[0:1] + rows[1:2] + rows[2:3]
        found.append(jnp.transpose(jnp.broadcast_to(gain, (128, 128)))[:group])
    return found


def norm(x_refs, t, group):
    values = [ref[pl.ds(t * group, group), :].astype(jnp.float32) for ref in x_refs]
    squares = sum(jnp.sum(value * value, axis=0, keepdims=True) for value in values)
    scale = lax.rsqrt(squares / CHANNELS + EPSILON)
    return scale, [value * scale for value in values]


def prepare_kernel(adjoint_ref, x_ref, gain_ref, strips_ref, payload_ref, lines, gain_rows):
    channels, height, width = adjoint_ref.shape
    frames = x_ref.shape[0]
    group = strips_ref.shape[2]
    lines[...] = adjoint_ref[...].astype(jnp.float32).reshape(channels * height, width)
    nothing = jnp.zeros((group, width), jnp.bfloat16)
    strips_ref[0, 0] = nothing
    strips_ref[height - 1, 2] = nothing
    for r in range(height):
        row = lines[pl.ds(r, channels, stride=height), :]
        if group > channels:
            row = jnp.concatenate(
                [row, jnp.zeros((group - channels, width), jnp.float32)], axis=0
            )
        row = row.astype(jnp.bfloat16)
        for k in range(3):
            if 0 <= r + 1 - k < height:
                strips_ref[r + 1 - k, k] = row
    for t in range(frames):
        values = x_ref[t]
        if group > channels:
            values = jnp.concatenate(
                [
                    values.astype(jnp.float32),
                    jnp.zeros((group - channels, width), jnp.float32),
                ],
                axis=0,
            ).astype(jnp.bfloat16)
        payload_ref[pl.ds(t * group, group), :] = values
    gain = gain_ref[...]
    high = gain.astype(jnp.bfloat16).astype(jnp.float32)
    middle = (gain - high).astype(jnp.bfloat16).astype(jnp.float32)
    gain_rows[...] = jnp.zeros_like(gain_rows)
    gain_rows[pl.ds(0, 1), pl.ds(0, channels)] = high
    gain_rows[pl.ds(1, 1), pl.ds(0, channels)] = middle
    gain_rows[pl.ds(2, 1), pl.ds(0, channels)] = gain - high - middle
    payload_ref[pl.ds(frames * group, 16), :] = gain_rows[...].astype(jnp.bfloat16)


def window_kernel(frames, group, slot_ref, adjoint_ref, windows, place):
    width = adjoint_ref.shape[-1]
    for slot in range(frames):
        place[slot_ref[slot]] = slot

    lane = lax.broadcasted_iota(jnp.int32, (group, width), 1)
    nothing = jnp.zeros((group, width), jnp.bfloat16)
    for a in range(2):
        for inner in range(9):
            for t in range(frames - 2 + a, frames):
                windows[pl.ds((a * 9 + inner) * group, group), pl.ds(t * width, width)] = nothing
    for frame in range(frames):
        slot = place[frame]
        for b in range(3):
            row = adjoint_ref[slot, 2 - b].astype(jnp.float32)
            after = jnp.where(lane == width - 1, 0.0, pltpu.roll(row, width - 1, 1))
            before = jnp.where(lane == 0, 0.0, pltpu.roll(row, 1, 1))
            for c, shifted in enumerate((after, row, before)):
                shifted = shifted.astype(jnp.bfloat16)
                for a in range(3):
                    t = frame + a - 2
                    if t >= 0:
                        windows[
                            pl.ds((a * 9 + b * 3 + c) * group, group), pl.ds(t * width, width)
                        ] = shifted

def grad_kernel(frames, group, factor, at_ref, windows, *refs):
    groups = len(refs) - 2
    x_refs = refs[:groups]
    grad_ref, hidden = refs[groups:]
    ins = groups * group
    width = windows.shape[1] // frames
    gain = gains(x_refs, frames * group, group)
    for t in range(frames):
        scale, scaled = norm(x_refs, t, group)
        for s in range(groups):
            normed = scaled[s] * gain[s]
            value = (normed * jax.nn.sigmoid(normed)).astype(jnp.bfloat16)
            start = pl.multiple_of(lax.rem(at_ref[0] + groups - s, groups) * group, 16)
            hidden[pl.ds(start, group), pl.ds(t * width, width)] = value

    grad = lax.dot_general(
        windows[...], hidden[...], (((1,), (1,)), ((), ())), preferred_element_type=jnp.float32
    )
    grad = grad * factor
    taps_out = grad.shape[0]
    blocks, rest, half, rows = packing(taps_out, ins, 1)
    for block in range(blocks):
        grad_ref[pl.ds(block * taps_out, taps_out), :] = grad[
            :, block * 128 : block * 128 + 128
        ].astype(jnp.bfloat16)
    base = blocks * taps_out
    if rest:
        left = grad[:half, blocks * 128 :]
        right = grad[half:, blocks * 128 :]
        right = jnp.concatenate(
            [right, jnp.zeros((2 * half - taps_out, rest), jnp.float32)], axis=0
        )
        grad_ref[pl.ds(base, half), :] = jnp.concatenate([left, right], axis=1).astype(
            jnp.bfloat16
        )
        base = base + half
    tail = grad_ref.shape[0] - base
    if tail:
        grad_ref[pl.ds(base, tail), :] = jnp.zeros((tail, 128), jnp.bfloat16)


def part_kernel(frames, group, at_ref, weight_ref, windows, *refs):
    groups = (len(refs) - 3) // 2
    x_refs = refs[:groups]
    part_refs = refs[groups : 2 * groups]
    scale_ref, own_share_ref, product = refs[2 * groups :]
    width = scale_ref.shape[-1]
    product[...] = jnp.dot(weight_ref[...], windows[...], preferred_element_type=jnp.float32)
    gain = gains(x_refs, frames * group, group)
    shares = []
    for t in range(frames):
        scale, scaled = norm(x_refs, t, group)
        scale_ref[pl.ds(t, 1), :] = scale
        share = jnp.zeros((1, width), jnp.float32)
        for s in range(groups):
            normed = scaled[s] * gain[s]
            sigma = jax.nn.sigmoid(normed)
            slope = sigma * (1.0 + normed * (1.0 - sigma)) * gain[s]
            start = pl.multiple_of(lax.rem(at_ref[0] + groups - s, groups) * group, 16)
            term = product[pl.ds(start, group), pl.ds(t * width, width)] * slope * scale
            part_refs[s][pl.ds(t * group, group), :] = term.astype(part_refs[s].dtype)
            share = share + jnp.sum(term * scaled[s], axis=0, keepdims=True)
        shares.append(share)
    share = jnp.concatenate(shares, axis=0)
    own_share_ref[...] = share
    high = share.astype(jnp.bfloat16).astype(jnp.float32)
    both = [high, share - high]
    unused = round_up(2 * frames, 16) - 2 * frames
    if unused:
        both.append(jnp.zeros((unused, width), jnp.float32))
    both = jnp.concatenate(both, axis=0).astype(jnp.bfloat16)
    for s in range(1, groups):
        part_refs[s][pl.ds(frames * group, both.shape[0]), :] = both


def finish_kernel(frames, group, packed_ref, x_ref, scale_ref, share_ref, *refs):
    own_ref, others, (out_ref, grad_ref) = refs[0], refs[1:-2], refs[-2:]
    taps_out, ins = grad_ref.shape
    blocks, rest, half, rows = packing(taps_out, ins, 1)
    for block in range(blocks):
        grad_ref[:, pl.ds(block * 128, 128)] = packed_ref[
            pl.ds(block * taps_out, taps_out), :
        ].astype(jnp.float32)
    if rest:
        both = packed_ref[pl.ds(blocks * taps_out, half), :].astype(jnp.float32)
        grad_ref[pl.ds(0, half), pl.ds(blocks * 128, rest)] = both[:, :rest]
        grad_ref[pl.ds(half, taps_out - half), pl.ds(blocks * 128, rest)] = both[
            : taps_out - half, rest:
        ]

    share = share_ref[...]
    for ref in others:
        both = ref[pl.ds(frames * group, round_up(2 * frames, 16)), :].astype(jnp.float32)
        share = share + both[:frames] + both[frames : 2 * frames]
    share = share / CHANNELS
    for t in range(frames):
        term = own_ref[pl.ds(t * group, group), :]
        for ref in others:
            term = term + ref[pl.ds(t * group, group), :].astype(jnp.float32)
        scaled = x_ref[pl.ds(t * group, group), :].astype(jnp.float32) * scale_ref[pl.ds(t, 1), :]
        out_ref[t] = (term - scaled * share[t : t + 1]).astype(jnp.bfloat16)


def shards(frame_adjoint, frame_slot, inputs, gain, weight):
    count = lax.axis_size("rows")
    groups = lax.axis_size("chan")
    frames, channels, _, width = inputs.shape
    group = round_up(channels, 16)
    spare = group - channels
    ins = groups * group

    taps_out = 27 * group
    pixels = frames * width
    strips, payload = pl.pallas_call(
        prepare_kernel,
        out_shape=(
            jax.ShapeDtypeStruct((count, 3, group, width), jnp.bfloat16),
            jax.ShapeDtypeStruct((frames * group + 16, width), jnp.bfloat16),
        ),
        in_specs=[vmem(), vmem(), vmem()],
        out_specs=(vmem(), vmem()),
        scratch_shapes=[
            pltpu.VMEM((channels * count, width), jnp.float32),
            pltpu.VMEM((16, width), jnp.float32),
        ],
        compiler_params=limit(taps_out, pixels),
        name="prepare_kernel",
    )(frame_adjoint[0], inputs[:, :, 0], gain.reshape(1, channels))
    strips = lax.all_to_all(strips, "rows", split_axis=0, concat_axis=0, tiled=True)

    shifts = [[(z, (z + s) % groups) for z in range(groups)] for s in range(groups)]
    everything = [payload] + [lax.ppermute(payload, "chan", shifts[s]) for s in range(1, groups)]
    at = lax.axis_index("chan").astype(jnp.int32).reshape(1)

    kernel = weight.reshape(27, channels, groups, channels)
    kernel = jnp.pad(kernel, ((0, 0), (0, spare), (0, 0), (0, spare)))
    kernel = kernel.reshape(27 * group, ins).T

    packed_rows = packing(taps_out, ins, count)[3]
    factor = float(frames * count * width) ** (-0.5)
    windows = pl.pallas_call(
        functools.partial(window_kernel, frames, group),
        out_shape=jax.ShapeDtypeStruct((taps_out, pixels), jnp.bfloat16),
        in_specs=[smem(), vmem()],
        out_specs=vmem(),
        scratch_shapes=[pltpu.SMEM((frames,), jnp.int32)],
        compiler_params=limit(taps_out, pixels),
        name="window_kernel",
    )(frame_slot, strips)
    packed = pl.pallas_call(
        functools.partial(grad_kernel, frames, group, factor),
        out_shape=jax.ShapeDtypeStruct((packed_rows, 128), jnp.bfloat16),
        in_specs=[smem(), vmem()] + [vmem()] * groups,
        out_specs=vmem(),
        scratch_shapes=[pltpu.VMEM((ins, pixels), jnp.bfloat16)],
        compiler_params=limit(taps_out, pixels),
        cost_estimate=cost(taps_out, ins, pixels),
        name="grad_kernel",
    )(at, windows, *everything)

    pieces = lax.all_to_all(
        packed.reshape(count, packed_rows // count, 128),
        "rows", split_axis=0, concat_axis=0, tiled=True,
    )

    sent = frames * group + round_up(2 * frames, 16)
    *parts, scale, share = pl.pallas_call(
        functools.partial(part_kernel, frames, group),
        out_shape=tuple(
            [jax.ShapeDtypeStruct((frames * group, width), jnp.float32)]
            + [jax.ShapeDtypeStruct((sent, width), jnp.bfloat16)] * (groups - 1)
            + [jax.ShapeDtypeStruct((frames, width), jnp.float32)] * 2
        ),
        in_specs=[smem(), vmem(), vmem()] + [vmem()] * groups,
        out_specs=(vmem(),) * (groups + 2),
        scratch_shapes=[pltpu.VMEM((ins, pixels), jnp.float32)],
        compiler_params=limit(taps_out, pixels),
        cost_estimate=cost(taps_out, ins, pixels),
        name="part_kernel",
    )(at, kernel, windows, *everything)

    arrived = [
        lax.ppermute(parts[s], "chan", shifts[groups - s]) for s in range(1, groups)
    ]
    summed = jnp.sum(pieces.astype(jnp.float32), axis=0).astype(jnp.bfloat16)
    whole = lax.all_gather(summed, "rows", axis=0, tiled=True)
    input_adjoint, grad = pl.pallas_call(
        functools.partial(finish_kernel, frames, group),
        out_shape=(
            jax.ShapeDtypeStruct((frames, group, width), jnp.bfloat16),
            jax.ShapeDtypeStruct((taps_out, ins), jnp.float32),
        ),
        in_specs=[vmem()] * (groups + 4),
        out_specs=(vmem(), vmem()),
        compiler_params=limit(taps_out, pixels),
        name="finish_kernel",
    )(whole, payload, scale, share, parts[0], *arrived)
    grad = grad.reshape(27, group, groups, group)[:, :channels, :, :channels]
    return (
        input_adjoint[:, :channels, None, :],
        grad.reshape(27, channels, groups * channels),
    )


def solution(mesh):
    in_specs = (
        P("rows", "chan", None, None),
        P(),
        P(None, "chan", "rows", None),
        P("chan"),
        P(None, "chan", None),
    )
    out_specs = (P(None, "chan", "rows", None), P(None, "chan", None))
    return jax.shard_map(shards, mesh=mesh, in_specs=in_specs, out_specs=out_specs, check_vma=False)
```

time: 216 us -> 51.9 us (0.24)
  waiting for transfers between devices: 127 us -> 8.39 us
  blocking collectives: 31.4 us -> 9.35 us
  local copies, waits for them, and re-layouts: 23.6 us -> 6.98 us
  between operations: 14 us -> 0.71 us
  starting transfers between devices: 8.77 us -> 17.9 us
  Pallas kernels: 0 us -> 6.82 us
  matrix products: 6.6 us -> 0 us
  other arithmetic: 4.63 us -> 1.12 us
    all_gather x1 -> x0, waiting for transfers between devices: 62.8 us -> none  [shards(): lax.all_gather(hidden_pad, 'chan', axis=1, tiled=True)]
    psum x1 -> x0, waiting for transfers between devices: 46.8 us -> none  [shards(): weight_adjoint = lax.psum(local_grad, 'rows')]
    psum x2 -> x0, blocking collectives: 21.2 us -> none  [the longest x1 12.1 us: shards(): squares = lax.psum(jnp.sum(values * values, axis=1), 'chan')]
    unnamed x29 -> x16, local copies, waits for them, and re-layouts: 21.2 us -> 5.6 us
    reduce_scatter x1 -> x0, waiting for transfers between devices: 15.1 us -> none  [shards(): lax.psum_scatter(partial_sum, 'chan', scatter_dimension=1, tiled=True)]
    all_to_all x1 -> x0, blocking collectives: 10.2 us -> none  [shards(): lax.all_to_all(frame_adjoint, 'rows', split_axis=2, concat_axis=0, tiled=...]
    all_gather x0 -> x1, blocking collectives: none -> 9.35 us  [shards(): whole = lax.all_gather(summed, 'rows', axis=0, tiled=True)]
    all_to_all x0 -> x2, starting transfers between devices: none -> 9.33 us  [the longest x1 5.17 us: shards(): lax.all_to_all(strips, 'rows', split_axis=0, concat_axis=0, tiled=True)]
  transfers between devices with their start and end apart: 7 -> 8, of which waited for: 5 -> 3; matrix products, arithmetic and copies ran while one was open for 0% -> 5% of each run, Pallas kernels for 0% -> 5%
where the time goes in v1:
time: 51.9 us; the launch traced here: 51.3 us
  starting transfers between devices  17.9 us (34%)
  blocking collectives  9.35 us (18%)
  waiting for transfers between devices  8.39 us (16%)
  local copies, waits for them, and re-layouts  6.98 us (13%)
  Pallas kernels  6.82 us (13%)
  other arithmetic  1.12 us (2%)
  between operations  0.71 us (1%)
    all_gather x1, blocking collectives, shards(): whole = lax.all_gather(summed, 'rows', axis=0, tiled=True)  9.35 us
    unnamed x16, local copies, waits for them, and re-layouts  5.6 us
    all_to_all x1, starting transfers between devices, shards(): lax.all_to_all(strips, 'rows', split_axis=0, concat_axis=0, tiled=True)  5.17 us
    ppermute x3, waiting for transfers between devices, shards(): lax.ppermute(payload, 'chan', shifts[s])  4.83 us
    ppermute x3, starting transfers between devices, shards(): lax.ppermute(payload, 'chan', shifts[s])  4.61 us
    all_to_all x1, starting transfers between devices, shards(): lax.all_to_all(packed.reshape(count, packed_rows // count, 128), 'rows',...  4.16 us
    ppermute x3, starting transfers between devices, shards(): lax.ppermute(parts[s], 'chan', shifts[groups - s])  4 us
    all_to_all x1, waiting for transfers between devices, shards(): lax.all_to_all(strips, 'rows', split_axis=0, concat_axis=0, tiled=True)  2.67 us
  transfers between devices with their start and end apart: 8, of which 3 were waited for; matrix products, arithmetic and copies ran while one was open for 5% of the time, Pallas kernels for 5%

profile of v1, /device:TPU:0, one launch (start us, length us, event | category | flops | bytes accessed | tf_op | source)
XLA Modules:
  0.0 51.3 jit_solution(9853703439924309988)
XLA Ops:
  0.6 0.9 %copy-done.4 = bf16[1,48,8,128]{3,2,1,0:T(8,128)(2,1)S(1)} copy-done((bf16[1,48,8,128]{3,2,1,0:T(8,128)(2,1)S(1)}, bf16[1,48,8,128]{3,2,1,0:T(8,128)(2,1)}, u32[]{:S(2)}) %copy-start.4) | copy-done | bytes 98328
  1.5 0.9 %copy-done.5 = bf16[8,48,1,128]{3,1,2,0:T(8,128)(2,1)S(1)} copy-done((bf16[8,48,1,128]{3,1,2,0:T(8,128)(2,1)S(1)}, bf16[8,48,1,128]{3,1,2,0:T(8,128)(2,1)}, u32[]{:S(2)}) %copy-start.5) | copy-done | bytes 98328
  2.4 0.7 %copy-done.6 = f32[48]{0:T(128)S(1)} copy-done((f32[48]{0:T(128)S(1)}, f32[48]{0:T(128)}, u32[]{:S(2)}) %copy-start.6) | copy-done | bytes 216
  3.1 0.8 %prepare_kernel.1 = (bf16[8,3,48,128]{3,2,1,0:T(8,128)(2,1)}, bf16[400,128]{1,0:T(8,128)(2,1)S(1)}) custom-call(bf16[48,8,128]{2,1,0:T(8,128)(2,1)S(1)} %bitcast.12, bf16[8,48,128]{2,1,0:T(8,128)(2,1)S(1)} %bitcast.13, f32[1,48]{1,0:T(1,128)S(1)} %bitcast.14), custom_call_target="tpu_custom_call" | custom-call | tf_op jit(solution)/shard_map/prepare_kernel/pallas_call | solution.py:239
  3.8 5.2 %all-to-all-start = ((bf16[8,3,48,128]{3,2,1,0:T(8,128)(2,1)}), bf16[8,3,48,128]{3,2,1,0:T(8,128)(2,1)S(1)}, u32[]{:S(2)}, u32[]{:S(2)}) async-start(bf16[8,3,48,128]{3,2,1,0:T(8,128)(2,1)} %get-tuple-element.12), calls=%async_computation | async-start | bytes 589824 | tf_op jit(solution)/shard_map/all_to_all | solution.py:254
  9.0 3.6 %collective-permute-start.2 = (bf16[400,128]{1,0:T(8,128)(2,1)S(1)}, bf16[400,128]{1,0:T(8,128)(2,1)S(1)}, u32[]{:S(2)}, u32[]{:S(2)}) collective-permute-start(bf16[400,128]{1,0:T(8,128)(2,1)S(1)} %get-tuple-element.13.refs_0_.x_ref), channel_id=1, source_target_pairs={{0,3},{1,0},{2,1},{3,2},{4,7},{5,4},{6,5},{7,6},{8,11},{9,8},{10,9... | collective-permute-start | bytes 307208 | tf_op jit(solution)/shard_map/ppermute | solution.py:257
  12.6 1.0 %collective-permute-start = (bf16[400,128]{1,0:T(8,128)(2,1)S(1)}, bf16[400,128]{1,0:T(8,128)(2,1)S(1)}, u32[]{:S(2)}, u32[]{:S(2)}) collective-permute-start(bf16[400,128]{1,0:T(8,128)(2,1)S(1)} %get-tuple-element.13.refs_0_.x_ref), channel_id=1, source_target_pairs={{0,1},{1,2},{2,3},{3,0},{4,5},{5,6},{6,7},{7,4},{8,9},{9,10},{10,1... | collective-permute-start | bytes 307208 | tf_op jit(solution)/shard_map/ppermute | solution.py:257
  13.6 2.7 %all-to-all-done.adjoint_ref = bf16[8,3,48,128]{3,2,1,0:T(8,128)(2,1)S(1)} async-done(((bf16[8,3,48,128]{3,2,1,0:T(8,128)(2,1)}), bf16[8,3,48,128]{3,2,1,0:T(8,128)(2,1)S(1)}, u32[]{:S(2)}, u32[]{:S(2)}) %all-to-all-start) | async-done | bytes 294944 | tf_op jit(solution)/shard_map/all_to_all | solution.py:254
  16.3 0.7 %copy-done.7 = s32[8]{0:T(128)S(1)} copy-done((s32[8]{0:T(128)S(1)}, s32[8]{0:T(128)}, u32[]{:S(2)}) %copy-start.7) | copy-done | bytes 56
  17.0 0.9 %window_kernel.1.windows = bf16[1296,1024]{1,0:T(8,128)(2,1)S(1)} custom-call(s32[8]{0:T(128)S(1)} %copy-done.7, bf16[8,3,48,128]{3,2,1,0:T(8,128)(2,1)S(1)} %all-to-all-done.adjoint_ref), custom_call_target="tpu_custom_call" | custom-call | tf_op jit(solution)/shard_map/window_kernel/pallas_call | solution.py:266
  17.9 4.8 %collective-permute-done.1.refs_2_ = bf16[400,128]{1,0:T(8,128)(2,1)S(1)} collective-permute-done((bf16[400,128]{1,0:T(8,128)(2,1)S(1)}, bf16[400,128]{1,0:T(8,128)(2,1)S(1)}, u32[]{:S(2)}, u32[]{:S(2)}) %collective-permute-start.1) | collective-permute-done | bytes 102432 | tf_op jit(solution)/shard_map/ppermute | solution.py:257
  22.7 2.0 %grad_kernel.1 = bf16[2048,128]{1,0:T(8,128)(2,1)} custom-call(s32[1]{0:T(128)} %bitcast.at_ref, bf16[1296,1024]{1,0:T(8,128)(2,1)S(1)} %window_kernel.1.windows, bf16[400,128]{1,0:T(8,128)(2,1)S(1)} %get-tuple-element.13.refs_0_.x_ref, bf16[400,128]{1,0:T(8,128)(2,1)S(1)} %collective-permute-done.refs_1_, ...), custom_call_target="tpu_custom_call" | custom-call | flops 509607936 | bytes 3047424 | tf_op jit(solution)/shard_map/grad_kernel/pallas_call | solution.py:275
  24.8 4.2 %all-to-all-start.1 = ((bf16[8,256,128]{2,1,0:T(8,128)(2,1)}), bf16[8,256,128]{2,1,0:T(8,128)(2,1)}, u32[]{:S(2)}, u32[]{:S(2)}) async-start(bf16[8,256,128]{2,1,0:T(8,128)(2,1)} %bitcast.4), calls=%async_computation.1 | async-start | bytes 1048576 | tf_op jit(solution)/shard_map/all_to_all | solution.py:286
  28.9 1.4 %copy.9 = bf16[1296,192]{0,1:T(8,128)(2,1)S(1)} copy(bf16[1296,192]{1,0:T(8,128)(2,1)} %bitcast.15) | data formatting | bytes 995328 | tf_op jit(solution)/shard_map/reshape | solution.py:262
  30.3 0.9 %copy-done.1 = bf16[400,128]{1,0:T(8,128)(2,1)S(1)} copy-done((bf16[400,128]{1,0:T(8,128)(2,1)S(1)}, bf16[400,128]{1,0:T(8,128)(2,1)}, u32[]{:S(2)}) %copy-start.1) | copy-done | bytes 102424
  31.2 1.9 %part_kernel.1 = (f32[384,128]{1,0:T(8,128)S(1)}, bf16[400,128]{1,0:T(8,128)(2,1)}, bf16[400,128]{1,0:T(8,128)(2,1)}, bf16[400,128]{1,0:T(8,128)(2,1)}, f32[8,128]{1,0:T(8,128)S(1)}, /*index=5*/f32[8,128]{1,0:T(8,128)S(1)}) custom-call(s32[1]{0:T(128)} %bitcast.at_ref, bf16[192,1296]{1,0:T(8,128)(2,1)S(1)} %bitcast.11, ...), custom_call_target="tpu_custom_call" | custom-call | flops 509607936 | bytes 3047424 | tf_op jit(solution)/shard_map/part_kernel/pallas_call | solution.py:292
  33.1 0.7 %copy-done.2 = f32[384,128]{1,0:T(8,128)} copy-done((f32[384,128]{1,0:T(8,128)}, f32[384,128]{1,0:T(8,128)S(1)}, u32[]{:S(2)}) %copy-start.2) | copy-done | bytes 196632
  33.8 1.4 %collective-permute-start.3 = (bf16[400,128]{1,0:T(8,128)(2,1)}, bf16[400,128]{1,0:T(8,128)(2,1)S(1)}, u32[]{:S(2)}, u32[]{:S(2)}) collective-permute-start(bf16[400,128]{1,0:T(8,128)(2,1)} %get-tuple-element.17), channel_id=1, source_target_pairs={{0,3},{1,0},{2,1},{3,2},{4,7},{5,4},{6,5},{7,6},{8,11},{9,8},{10,9... | collective-permute-start | bytes 307208 | tf_op jit(solution)/shard_map/ppermute | solution.py:308
  35.8 2.0 %collective-permute-start.5 = (bf16[400,128]{1,0:T(8,128)(2,1)}, bf16[400,128]{1,0:T(8,128)(2,1)S(1)}, u32[]{:S(2)}, u32[]{:S(2)}) collective-permute-start(bf16[400,128]{1,0:T(8,128)(2,1)} %get-tuple-element.19), channel_id=1, source_target_pairs={{0,1},{1,2},{2,3},{3,0},{4,5},{5,6},{6,7},{7,4},{8,9},{9,10},{10,1... | collective-permute-start | bytes 307208 | tf_op jit(solution)/shard_map/ppermute | solution.py:308
  37.8 0.9 %all-to-all-done.1 = bf16[8,256,128]{2,1,0:T(8,128)(2,1)} async-done(((bf16[8,256,128]{2,1,0:T(8,128)(2,1)}), bf16[8,256,128]{2,1,0:T(8,128)(2,1)}, u32[]{:S(2)}, u32[]{:S(2)}) %all-to-all-start.1) | async-done | bytes 524320 | tf_op jit(solution)/shard_map/all_to_all | solution.py:286
  38.7 1.1 %reduce_sum.12 = bf16[256,128]{1,0:T(8,128)(2,1)S(1)} reduce(bf16[8,256,128]{2,1,0:T(8,128)(2,1)} %all-to-all-done.1, bf16[]{:T(256)} %constant.3.clone.1), dimensions={0}, to_apply=%region_0.1 | reduce | flops 229376 | bytes 589826 | tf_op jit(solution)/shard_map/reduce_sum | solution.py:310
  39.8 9.3 %all_gather.3.packed_ref = bf16[2048,128]{1,0:T(8,128)(2,1)S(1)} all-gather(bf16[256,128]{1,0:T(8,128)(2,1)S(1)} %reduce_sum.12), channel_id=1, replica_groups=mesh['rows'=8,'chan'=4] {'rows'}, dimensions={0}, use_global_device_ids=true | all-gather | bytes 589824 | tf_op jit(solution)/shard_map/all_gather | solution.py:311
  49.2 0.9 %copy-done.3 = f32[384,128]{1,0:T(8,128)S(1)} copy-done((f32[384,128]{1,0:T(8,128)S(1)}, f32[384,128]{1,0:T(8,128)}, u32[]{:S(2)}) %copy-start.3) | copy-done | bytes 196632
  50.1 1.2 %finish_kernel.1 = (bf16[8,48,128]{2,1,0:T(8,128)(2,1)}, f32[1296,192]{1,0:T(8,128)}) custom-call(bf16[2048,128]{1,0:T(8,128)(2,1)S(1)} %all_gather.3.packed_ref, bf16[400,128]{1,0:T(8,128)(2,1)S(1)} %get-tuple-element.13.refs_0_.x_ref, f32[8,128]{1,0:T(8,128)S(1)} %get-tuple-element.14.scale_ref, f32[8,128]{1,0:T(8,128)S(1)} %get-tuple-element.15.share_ref, ...), custom_call_target="tpu_custom_call" | custom-call | tf_op jit(solution)/shard_map/finish_kernel/pallas_call | solution.py:312
  (16 shorter events, 0.6 us)
Async XLA Ops:
  0.6 0.9 %copy-start.4 = (bf16[1,48,8,128]{3,2,1,0:T(8,128)(2,1)S(1)}, bf16[1,48,8,128]{3,2,1,0:T(8,128)(2,1)}, u32[]{:S(2)}) copy-start(bf16[1,48,8,128]{3,2,1,0:T(8,128)(2,1)} %param.5) | copy-start | bytes 294916
  1.5 0.9 %copy-start.5 = (bf16[8,48,1,128]{3,1,2,0:T(8,128)(2,1)S(1)}, bf16[8,48,1,128]{3,1,2,0:T(8,128)(2,1)}, u32[]{:S(2)}) copy-start(bf16[8,48,1,128]{3,1,2,0:T(8,128)(2,1)} %param.7) | copy-start | bytes 294916
  2.4 0.7 %copy-start.6 = (f32[48]{0:T(128)S(1)}, f32[48]{0:T(128)}, u32[]{:S(2)}) copy-start(f32[48]{0:T(128)} %param.8) | copy-start | bytes 580
  3.8 12.5 %all-to-all-start = ((bf16[8,3,48,128]{3,2,1,0:T(8,128)(2,1)}), bf16[8,3,48,128]{3,2,1,0:T(8,128)(2,1)S(1)}, u32[]{:S(2)}, u32[]{:S(2)}) async-start(bf16[8,3,48,128]{3,2,1,0:T(8,128)(2,1)} %get-tuple-element.12), calls=%async_computation | async-start | bytes 589824 | tf_op jit(solution)/shard_map/all_to_all | solution.py:254
  9.0 8.9 %collective-permute-start.2 = (bf16[400,128]{1,0:T(8,128)(2,1)S(1)}, bf16[400,128]{1,0:T(8,128)(2,1)S(1)}, u32[]{:S(2)}, u32[]{:S(2)}) collective-permute-start(bf16[400,128]{1,0:T(8,128)(2,1)S(1)} %get-tuple-element.13.refs_0_.x_ref), channel_id=1, source_target_pairs={{0,3},{1,0},{2,1},{3,2},{4,7},{5,4},{6,5},{7,6},{8,11},{9,8},{10,9... | collective-permute-start | bytes 307208 | tf_op jit(solution)/shard_map/ppermute | solution.py:257
  12.6 10.1 %collective-permute-start.1 = (bf16[400,128]{1,0:T(8,128)(2,1)S(1)}, bf16[400,128]{1,0:T(8,128)(2,1)S(1)}, u32[]{:S(2)}, u32[]{:S(2)}) collective-permute-start(bf16[400,128]{1,0:T(8,128)(2,1)S(1)} %get-tuple-element.13.refs_0_.x_ref), channel_id=1, source_target_pairs={{0,2},{1,3},{2,0},{3,1},{4,6},{5,7},{6,4},{7,5},{8,10},{9,11},{10,... | collective-permute-start | bytes 307208 | tf_op jit(solution)/shard_map/ppermute | solution.py:257
  12.6 10.1 %collective-permute-start = (bf16[400,128]{1,0:T(8,128)(2,1)S(1)}, bf16[400,128]{1,0:T(8,128)(2,1)S(1)}, u32[]{:S(2)}, u32[]{:S(2)}) collective-permute-start(bf16[400,128]{1,0:T(8,128)(2,1)S(1)} %get-tuple-element.13.refs_0_.x_ref), channel_id=1, source_target_pairs={{0,1},{1,2},{2,3},{3,0},{4,5},{5,6},{6,7},{7,4},{8,9},{9,10},{10,1... | collective-permute-start | bytes 307208 | tf_op jit(solution)/shard_map/ppermute | solution.py:257
  16.3 0.7 %copy-start.7 = (s32[8]{0:T(128)S(1)}, s32[8]{0:T(128)}, u32[]{:S(2)}) copy-start(s32[8]{0:T(128)} %slot_ref.1) | copy-start | bytes 100
  22.7 6.2 %copy-start = (bf16[400,128]{1,0:T(8,128)(2,1)}, bf16[400,128]{1,0:T(8,128)(2,1)S(1)}, u32[]{:S(2)}) copy-start(bf16[400,128]{1,0:T(8,128)(2,1)S(1)} %collective-permute-done.refs_1_) | copy-start | bytes 307204
  24.8 13.9 %all-to-all-start.1 = ((bf16[8,256,128]{2,1,0:T(8,128)(2,1)}), bf16[8,256,128]{2,1,0:T(8,128)(2,1)}, u32[]{:S(2)}, u32[]{:S(2)}) async-start(bf16[8,256,128]{2,1,0:T(8,128)(2,1)} %bitcast.4), calls=%async_computation.1 | async-start | bytes 1048576 | tf_op jit(solution)/shard_map/all_to_all | solution.py:286
  30.3 0.9 %copy-start.1 = (bf16[400,128]{1,0:T(8,128)(2,1)S(1)}, bf16[400,128]{1,0:T(8,128)(2,1)}, u32[]{:S(2)}) copy-start(bf16[400,128]{1,0:T(8,128)(2,1)} %copy-done) | copy-start | bytes 307204
  33.1 0.7 %copy-start.2 = (f32[384,128]{1,0:T(8,128)}, f32[384,128]{1,0:T(8,128)S(1)}, u32[]{:S(2)}) copy-start(f32[384,128]{1,0:T(8,128)S(1)} %get-tuple-element.16.refs_0_) | copy-start | bytes 589828
  33.8 15.4 %collective-permute-start.3 = (bf16[400,128]{1,0:T(8,128)(2,1)}, bf16[400,128]{1,0:T(8,128)(2,1)S(1)}, u32[]{:S(2)}, u32[]{:S(2)}) collective-permute-start(bf16[400,128]{1,0:T(8,128)(2,1)} %get-tuple-element.17), channel_id=1, source_target_pairs={{0,3},{1,0},{2,1},{3,2},{4,7},{5,4},{6,5},{7,6},{8,11},{9,8},{10,9... | collective-permute-start | bytes 307208 | tf_op jit(solution)/shard_map/ppermute | solution.py:308
  35.2 14.0 %collective-permute-start.4 = (bf16[400,128]{1,0:T(8,128)(2,1)}, bf16[400,128]{1,0:T(8,128)(2,1)S(1)}, u32[]{:S(2)}, u32[]{:S(2)}) collective-permute-start(bf16[400,128]{1,0:T(8,128)(2,1)} %get-tuple-element.18), channel_id=1, source_target_pairs={{0,2},{1,3},{2,0},{3,1},{4,6},{5,7},{6,4},{7,5},{8,10},{9,11},{10,... | collective-permute-start | bytes 307208 | tf_op jit(solution)/shard_map/ppermute | solution.py:308
  35.8 13.4 %collective-permute-start.5 = (bf16[400,128]{1,0:T(8,128)(2,1)}, bf16[400,128]{1,0:T(8,128)(2,1)S(1)}, u32[]{:S(2)}, u32[]{:S(2)}) collective-permute-start(bf16[400,128]{1,0:T(8,128)(2,1)} %get-tuple-element.19), channel_id=1, source_target_pairs={{0,1},{1,2},{2,3},{3,0},{4,5},{5,6},{6,7},{7,4},{8,9},{9,10},{10,1... | collective-permute-start | bytes 307208 | tf_op jit(solution)/shard_map/ppermute | solution.py:308
  49.1 0.9 %copy-start.3 = (f32[384,128]{1,0:T(8,128)S(1)}, f32[384,128]{1,0:T(8,128)}, u32[]{:S(2)}) copy-start(f32[384,128]{1,0:T(8,128)} %copy-done.2) | copy-start | bytes 589828

commit v2 on v1

--- a/solution.py
+++ b/solution.py
@@ -24,6 +24,10 @@
 
 def vmem():
     return pl.BlockSpec(memory_space=pltpu.VMEM)
+
+
+def copied():
+    return pl.BlockSpec()
 
 
 def smem():
@@ -242,19 +246,23 @@
             jax.ShapeDtypeStruct((count, 3, group, width), jnp.bfloat16),
             jax.ShapeDtypeStruct((frames * group + 16, width), jnp.bfloat16),
         ),
-        in_specs=[vmem(), vmem(), vmem()],
+        in_specs=[copied(), copied(), copied()],
         out_specs=(vmem(), vmem()),
         scratch_shapes=[
             pltpu.VMEM((channels * count, width), jnp.float32),
             pltpu.VMEM((16, width), jnp.float32),
         ],
-        compiler_params=limit(taps_out, pixels),
+        compiler_params=pltpu.CompilerParams(vmem_limit_bytes=60 * MIB),
         name="prepare_kernel",
     )(frame_adjoint[0], inputs[:, :, 0], gain.reshape(1, channels))
     strips = lax.all_to_all(strips, "rows", split_axis=0, concat_axis=0, tiled=True)
 
     shifts = [[(z, (z + s) % groups) for z in range(groups)] for s in range(groups)]
-    everything = [payload] + [lax.ppermute(payload, "chan", shifts[s]) for s in range(1, groups)]
+    everything = [payload] * groups
+    for s in range(1, groups // 2 + 1):
+        everything[s] = lax.ppermute(everything[s - 1], "chan", shifts[1])
+    for s in range(groups - 1, groups // 2, -1):
+        everything[s] = lax.ppermute(everything[(s + 1) % groups], "chan", shifts[groups - 1])
     at = lax.axis_index("chan").astype(jnp.int32).reshape(1)
 
     kernel = weight.reshape(27, channels, groups, channels)
@@ -266,7 +274,7 @@
     windows = pl.pallas_call(
         functools.partial(window_kernel, frames, group),
         out_shape=jax.ShapeDtypeStruct((taps_out, pixels), jnp.bfloat16),
-        in_specs=[smem(), vmem()],
+        in_specs=[smem(), copied()],
         out_specs=vmem(),
         scratch_shapes=[pltpu.SMEM((frames,), jnp.int32)],
         compiler_params=limit(taps_out, pixels),
@@ -275,7 +283,7 @@
     packed = pl.pallas_call(
         functools.partial(grad_kernel, frames, group, factor),
         out_shape=jax.ShapeDtypeStruct((packed_rows, 128), jnp.bfloat16),
-        in_specs=[smem(), vmem()] + [vmem()] * groups,
+        in_specs=[smem(), vmem()] + [copied()] * groups,
         out_specs=vmem(),
         scratch_shapes=[pltpu.VMEM((ins, pixels), jnp.bfloat16)],
         compiler_params=limit(taps_out, pixels),
@@ -296,7 +304,7 @@
             + [jax.ShapeDtypeStruct((sent, width), jnp.bfloat16)] * (groups - 1)
             + [jax.ShapeDtypeStruct((frames, width), jnp.float32)] * 2
         ),
-        in_specs=[smem(), vmem(), vmem()] + [vmem()] * groups,
+        in_specs=[smem(), vmem(), vmem()] + [copied()] * groups,
         out_specs=(vmem(),) * (groups + 2),
         scratch_shapes=[pltpu.VMEM((ins, pixels), jnp.float32)],
         compiler_params=limit(taps_out, pixels),
@@ -315,7 +323,7 @@
             jax.ShapeDtypeStruct((frames, group, width), jnp.bfloat16),
             jax.ShapeDtypeStruct((taps_out, ins), jnp.float32),
         ),
-        in_specs=[vmem()] * (groups + 4),
+        in_specs=[copied()] * (groups + 4),
         out_specs=(vmem(), vmem()),
         compiler_params=limit(taps_out, pixels),
         name="finish_kernel",

time: 51.9 us -> 50.7 us (0.977)
  waiting for transfers between devices: 8.39 us -> 11 us
  local copies, waits for them, and re-layouts: 6.98 us -> 4.52 us
  starting transfers between devices: 17.9 us -> 16.1 us
  Pallas kernels: 6.82 us -> 7.81 us
    ppermute x3, waiting for transfers between devices: 4.83 us -> 8.71 us  [the longest x2 8.7 us: shards(): everything[s] = lax.ppermute(everything[s - 1], 'chan', shifts[1])]
    all_to_all x1, waiting for transfers between devices: 2.67 us -> 0.01 us  [shards(): lax.all_to_all(strips, 'rows', split_axis=0, concat_axis=0, tiled=True)]
    unnamed x16 -> x12, local copies, waits for them, and re-layouts: 5.6 us -> 3.14 us
    all_to_all x1, waiting for transfers between devices: 0.89 us -> 2.24 us  [shards(): lax.all_to_all(packed.reshape(count, packed_rows // count, 128), 'rows',...]
    ppermute x3, starting transfers between devices: 4 us -> 2.77 us  [shards(): lax.ppermute(parts[s], 'chan', shifts[groups - s])]
    pallas_call x1, Pallas kernels: 0.77 us -> 1.76 us  [shards(): pl.pallas_call(prepare_kernel, out_shape=(jax.ShapeDtypeStruct((count, 3,...]
    ppermute x3, starting transfers between devices: 4.61 us -> 3.83 us  [the longest x1 2.25 us: shards(): lax.ppermute(everything[(s + 1) % groups], 'chan', shifts[groups - 1])]
  transfers between devices with their start and end apart: 8 -> 8, of which waited for: 3 -> 3; matrix products, arithmetic and copies ran while one was open for 5% -> 5% of each run, Pallas kernels for 5% -> 6%
where the time goes in v2:
time: 50.7 us; the launch traced here: 50.1 us
  starting transfers between devices  16.1 us (32%)
  waiting for transfers between devices  11 us (22%)
  blocking collectives  8.91 us (18%)
  Pallas kernels  7.81 us (15%)
  local copies, waits for them, and re-layouts  4.52 us (9%)
  other arithmetic  1.12 us (2%)
  between operations  0.69 us (1%)
    all_gather x1, blocking collectives, shards(): whole = lax.all_gather(summed, 'rows', axis=0, tiled=True)  8.91 us
    ppermute x2, waiting for transfers between devices, shards(): everything[s] = lax.ppermute(everything[s - 1], 'chan', shifts[1])  8.7 us
    all_to_all x1, starting transfers between devices, shards(): lax.all_to_all(strips, 'rows', split_axis=0, concat_axis=0, tiled=True)  5.3 us
    all_to_all x1, starting transfers between devices, shards(): lax.all_to_all(packed.reshape(count, packed_rows // count, 128), 'rows',...  4.25 us
    unnamed x12, local copies, waits for them, and re-layouts  3.14 us
    ppermute x3, starting transfers between devices, shards(): lax.ppermute(parts[s], 'chan', shifts[groups - s])  2.77 us
    ppermute x1, starting transfers between devices, shards(): lax.ppermute(everything[(s + 1) % groups], 'chan', shifts[groups - 1])  2.25 us
    all_to_all x1, waiting for transfers between devices, shards(): lax.all_to_all(packed.reshape(count, packed_rows // count, 128), 'rows',...  2.24 us
  transfers between devices with their start and end apart: 8, of which 3 were waited for; matrix products, arithmetic and copies ran while one was open for 5% of the time, Pallas kernels for 6%

profile of v2, /device:TPU:0, one launch (start us, length us, event | category | flops | bytes accessed | tf_op | source)
XLA Modules:
  0.0 50.1 jit_solution(18194891948631018888)
XLA Ops:
  0.6 1.8 %prepare_kernel.1 = (bf16[8,3,48,128]{3,2,1,0:T(8,128)(2,1)}, bf16[400,128]{1,0:T(8,128)(2,1)}) custom-call(bf16[48,8,128]{2,1,0:T(8,128)(2,1)} %bitcast.13, bf16[8,48,128]{2,1,0:T(8,128)(2,1)} %bitcast.14, f32[1,48]{1,0:T(1,128)} %bitcast.15), custom_call_target="tpu_custom_call" | custom-call | tf_op jit(solution)/shard_map/prepare_kernel/pallas_call | solution.py:243
  2.4 5.3 %all-to-all-start = ((bf16[8,3,48,128]{3,2,1,0:T(8,128)(2,1)}), bf16[8,3,48,128]{3,2,1,0:T(8,128)(2,1)S(1)}, u32[]{:S(2)}, u32[]{:S(2)}) async-start(bf16[8,3,48,128]{3,2,1,0:T(8,128)(2,1)} %get-tuple-element.12), calls=%async_computation | async-start | bytes 589824 | tf_op jit(solution)/shard_map/all_to_all | solution.py:258
  7.7 1.6 %collective-permute-start = (bf16[400,128]{1,0:T(8,128)(2,1)}, bf16[400,128]{1,0:T(8,128)(2,1)S(1)}, u32[]{:S(2)}, u32[]{:S(2)}) collective-permute-start(bf16[400,128]{1,0:T(8,128)(2,1)} %get-tuple-element.13.refs_0_.x_ref), channel_id=1, source_target_pairs={{0,1},{1,2},{2,3},{3,0},{4,5},{5,6},{6,7},{7,4},{8,9},{9,10},{10,1... | collective-permute-start | bytes 307208 | tf_op jit(solution)/shard_map/ppermute | solution.py:263
  9.3 2.2 %collective-permute-start.2 = (bf16[400,128]{1,0:T(8,128)(2,1)}, bf16[400,128]{1,0:T(8,128)(2,1)S(1)}, u32[]{:S(2)}, u32[]{:S(2)}) collective-permute-start(bf16[400,128]{1,0:T(8,128)(2,1)} %get-tuple-element.13.refs_0_.x_ref), channel_id=1, source_target_pairs={{0,3},{1,0},{2,1},{3,2},{4,7},{5,4},{6,5},{7,6},{8,11},{9,8},{10,9... | collective-permute-start | bytes 307208 | tf_op jit(solution)/shard_map/ppermute | solution.py:265
  11.5 3.9 %collective-permute-done.refs_1_ = bf16[400,128]{1,0:T(8,128)(2,1)S(1)} collective-permute-done((bf16[400,128]{1,0:T(8,128)(2,1)}, bf16[400,128]{1,0:T(8,128)(2,1)S(1)}, u32[]{:S(2)}, u32[]{:S(2)}) %collective-permute-start) | collective-permute-done | bytes 102432 | tf_op jit(solution)/shard_map/ppermute | solution.py:263
  15.4 0.0 collective-permute-start.1
  15.4 0.0 all-to-all-done.adjoint_ref
  15.4 0.7 %copy-done.5 = s32[8]{0:T(128)S(1)} copy-done((s32[8]{0:T(128)S(1)}, s32[8]{0:T(128)}, u32[]{:S(2)}) %copy-start.5) | copy-done | bytes 56
  16.0 0.9 %window_kernel.1.windows = bf16[1296,1024]{1,0:T(8,128)(2,1)S(1)} custom-call(s32[8]{0:T(128)S(1)} %copy-done.5, bf16[8,3,48,128]{3,2,1,0:T(8,128)(2,1)S(1)} %all-to-all-done.adjoint_ref), custom_call_target="tpu_custom_call" | custom-call | tf_op jit(solution)/shard_map/window_kernel/pallas_call | solution.py:274
  17.0 4.8 %collective-permute-done.1.refs_2_ = bf16[400,128]{1,0:T(8,128)(2,1)S(1)} collective-permute-done((bf16[400,128]{1,0:T(8,128)(2,1)S(1)}, bf16[400,128]{1,0:T(8,128)(2,1)S(1)}, u32[]{:S(2)}, u32[]{:S(2)}) %collective-permute-start.1) | collective-permute-done | bytes 102432 | tf_op jit(solution)/shard_map/ppermute | solution.py:263
  21.8 2.0 %grad_kernel.1 = bf16[2048,128]{1,0:T(8,128)(2,1)} custom-call(s32[1]{0:T(128)} %bitcast.at_ref, bf16[1296,1024]{1,0:T(8,128)(2,1)S(1)} %window_kernel.1.windows, bf16[400,128]{1,0:T(8,128)(2,1)S(1)} %copy-done, bf16[400,128]{1,0:T(8,128)(2,1)S(1)} %collective-permute-done.refs_1_, bf16[400,128]{1,0:T(8,128)(2,1)S(1)} %collective-permute-done.1.refs_2_, ...), custom_call_target="tpu_custom_call" | custom-call | flops 509607936 | bytes 3047424 | tf_op jit(solution)/shard_map/grad_kernel/pallas_call | solution.py:283
  23.8 4.2 %all-to-all-start.1 = ((bf16[8,256,128]{2,1,0:T(8,128)(2,1)}), bf16[8,256,128]{2,1,0:T(8,128)(2,1)}, u32[]{:S(2)}, u32[]{:S(2)}) async-start(bf16[8,256,128]{2,1,0:T(8,128)(2,1)} %bitcast.4), calls=%async_computation.1 | async-start | bytes 1048576 | tf_op jit(solution)/shard_map/all_to_all | solution.py:294
  28.1 1.4 %copy.9 = bf16[1296,192]{0,1:T(8,128)(2,1)S(1)} copy(bf16[1296,192]{1,0:T(8,128)(2,1)} %bitcast.12) | data formatting | bytes 995328 | tf_op jit(solution)/shard_map/reshape | solution.py:270
  29.5 0.9 %copy-done.2 = bf16[400,128]{1,0:T(8,128)(2,1)S(1)} copy-done((bf16[400,128]{1,0:T(8,128)(2,1)S(1)}, bf16[400,128]{1,0:T(8,128)(2,1)}, u32[]{:S(2)}) %copy-start.2) | copy-done | bytes 102424
  30.4 1.9 %part_kernel.1 = (f32[384,128]{1,0:T(8,128)S(1)}, bf16[400,128]{1,0:T(8,128)(2,1)}, bf16[400,128]{1,0:T(8,128)(2,1)}, bf16[400,128]{1,0:T(8,128)(2,1)}, f32[8,128]{1,0:T(8,128)S(1)}, /*index=5*/f32[8,128]{1,0:T(8,128)S(1)}) custom-call(s32[1]{0:T(128)} %bitcast.at_ref, bf16[192,1296]{1,0:T(8,128)(2,1)S(1)} %bitcast.11, ...), custom_call_target="tpu_custom_call" | custom-call | flops 509607936 | bytes 3047424 | tf_op jit(solution)/shard_map/part_kernel/pallas_call | solution.py:300
  32.3 0.7 %copy-done.3 = f32[384,128]{1,0:T(8,128)} copy-done((f32[384,128]{1,0:T(8,128)}, f32[384,128]{1,0:T(8,128)S(1)}, u32[]{:S(2)}) %copy-start.3) | copy-done | bytes 196632
  32.9 1.8 %collective-permute-start.3 = (bf16[400,128]{1,0:T(8,128)(2,1)}, bf16[400,128]{1,0:T(8,128)(2,1)S(1)}, u32[]{:S(2)}, u32[]{:S(2)}) collective-permute-start(bf16[400,128]{1,0:T(8,128)(2,1)} %get-tuple-element.17), channel_id=1, source_target_pairs={{0,3},{1,0},{2,1},{3,2},{4,7},{5,4},{6,5},{7,6},{8,11},{9,8},{10,9... | collective-permute-start | bytes 307208 | tf_op jit(solution)/shard_map/ppermute | solution.py:316
  34.7 1.0 %collective-permute-start.5 = (bf16[400,128]{1,0:T(8,128)(2,1)}, bf16[400,128]{1,0:T(8,128)(2,1)S(1)}, u32[]{:S(2)}, u32[]{:S(2)}) collective-permute-start(bf16[400,128]{1,0:T(8,128)(2,1)} %get-tuple-element.19), channel_id=1, source_target_pairs={{0,1},{1,2},{2,3},{3,0},{4,5},{5,6},{6,7},{7,4},{8,9},{9,10},{10,1... | collective-permute-start | bytes 307208 | tf_op jit(solution)/shard_map/ppermute | solution.py:316
  35.7 2.2 %all-to-all-done.1 = bf16[8,256,128]{2,1,0:T(8,128)(2,1)} async-done(((bf16[8,256,128]{2,1,0:T(8,128)(2,1)}), bf16[8,256,128]{2,1,0:T(8,128)(2,1)}, u32[]{:S(2)}, u32[]{:S(2)}) %all-to-all-start.1) | async-done | bytes 524320 | tf_op jit(solution)/shard_map/all_to_all | solution.py:294
  37.9 1.1 %reduce_sum.12 = bf16[256,128]{1,0:T(8,128)(2,1)S(1)} reduce(bf16[8,256,128]{2,1,0:T(8,128)(2,1)} %all-to-all-done.1, bf16[]{:T(256)} %constant.3.clone.1), dimensions={0}, to_apply=%region_0.1 | reduce | flops 229376 | bytes 589826 | tf_op jit(solution)/shard_map/reduce_sum | solution.py:318
  39.1 8.9 %all_gather.3.packed_ref = bf16[2048,128]{1,0:T(8,128)(2,1)S(1)} all-gather(bf16[256,128]{1,0:T(8,128)(2,1)S(1)} %reduce_sum.12), channel_id=1, replica_groups=mesh['rows'=8,'chan'=4] {'rows'}, dimensions={0}, use_global_device_ids=true | all-gather | bytes 589824 | tf_op jit(solution)/shard_map/all_gather | solution.py:319
  48.0 0.0 collective-permute-done.5.refs_3_
  48.0 0.9 %copy-done.4 = f32[384,128]{1,0:T(8,128)S(1)} copy-done((f32[384,128]{1,0:T(8,128)S(1)}, f32[384,128]{1,0:T(8,128)}, u32[]{:S(2)}) %copy-start.4) | copy-done | bytes 196632
  48.9 1.2 %finish_kernel.1 = (bf16[8,48,128]{2,1,0:T(8,128)(2,1)}, f32[1296,192]{1,0:T(8,128)}) custom-call(bf16[2048,128]{1,0:T(8,128)(2,1)S(1)} %all_gather.3.packed_ref, bf16[400,128]{1,0:T(8,128)(2,1)S(1)} %copy-done, f32[8,128]{1,0:T(8,128)S(1)} %get-tuple-element.14.scale_ref, f32[8,128]{1,0:T(8,128)S(1)} %get-tuple-element.15.share_ref, ...), custom_call_target="tpu_custom_call" | custom-call | tf_op jit(solution)/shard_map/finish_kernel/pallas_call | solution.py:320
  (12 shorter events, 0.0 us)
Async XLA Ops:
  2.4 19.4 %copy-start = (bf16[400,128]{1,0:T(8,128)(2,1)S(1)}, bf16[400,128]{1,0:T(8,128)(2,1)}, u32[]{:S(2)}) copy-start(bf16[400,128]{1,0:T(8,128)(2,1)} %get-tuple-element.13.refs_0_.x_ref) | copy-start | bytes 307204
  2.4 13.0 %all-to-all-start = ((bf16[8,3,48,128]{3,2,1,0:T(8,128)(2,1)}), bf16[8,3,48,128]{3,2,1,0:T(8,128)(2,1)S(1)}, u32[]{:S(2)}, u32[]{:S(2)}) async-start(bf16[8,3,48,128]{3,2,1,0:T(8,128)(2,1)} %get-tuple-element.12), calls=%async_computation | async-start | bytes 589824 | tf_op jit(solution)/shard_map/all_to_all | solution.py:258
  7.7 7.7 %collective-permute-start = (bf16[400,128]{1,0:T(8,128)(2,1)}, bf16[400,128]{1,0:T(8,128)(2,1)S(1)}, u32[]{:S(2)}, u32[]{:S(2)}) collective-permute-start(bf16[400,128]{1,0:T(8,128)(2,1)} %get-tuple-element.13.refs_0_.x_ref), channel_id=1, source_target_pairs={{0,1},{1,2},{2,3},{3,0},{4,5},{5,6},{6,7},{7,4},{8,9},{9,10},{10,1... | collective-permute-start | bytes 307208 | tf_op jit(solution)/shard_map/ppermute | solution.py:263
  9.3 7.7 %collective-permute-start.2 = (bf16[400,128]{1,0:T(8,128)(2,1)}, bf16[400,128]{1,0:T(8,128)(2,1)S(1)}, u32[]{:S(2)}, u32[]{:S(2)}) collective-permute-start(bf16[400,128]{1,0:T(8,128)(2,1)} %get-tuple-element.13.refs_0_.x_ref), channel_id=1, source_target_pairs={{0,3},{1,0},{2,1},{3,2},{4,7},{5,4},{6,5},{7,6},{8,11},{9,8},{10,9... | collective-permute-start | bytes 307208 | tf_op jit(solution)/shard_map/ppermute | solution.py:265
  15.4 6.5 %collective-permute-start.1 = (bf16[400,128]{1,0:T(8,128)(2,1)S(1)}, bf16[400,128]{1,0:T(8,128)(2,1)S(1)}, u32[]{:S(2)}, u32[]{:S(2)}) collective-permute-start(bf16[400,128]{1,0:T(8,128)(2,1)S(1)} %collective-permute-done.refs_1_), channel_id=1, source_target_pairs={{0,1},{1,2},{2,3},{3,0},{4,5},{5,6},{6,7},{7,4},{8,9},{9,10},{10,1... | collective-permute-start | bytes 307208 | tf_op jit(solution)/shard_map/ppermute | solution.py:263
  15.4 0.7 %copy-start.5 = (s32[8]{0:T(128)S(1)}, s32[8]{0:T(128)}, u32[]{:S(2)}) copy-start(s32[8]{0:T(128)} %slot_ref.1) | copy-start | bytes 100
  21.8 6.3 %copy-start.1 = (bf16[400,128]{1,0:T(8,128)(2,1)}, bf16[400,128]{1,0:T(8,128)(2,1)S(1)}, u32[]{:S(2)}) copy-start(bf16[400,128]{1,0:T(8,128)(2,1)S(1)} %collective-permute-done.1.refs_2_) | copy-start | bytes 307204
  23.8 14.1 %all-to-all-start.1 = ((bf16[8,256,128]{2,1,0:T(8,128)(2,1)}), bf16[8,256,128]{2,1,0:T(8,128)(2,1)}, u32[]{:S(2)}, u32[]{:S(2)}) async-start(bf16[8,256,128]{2,1,0:T(8,128)(2,1)} %bitcast.4), calls=%async_computation.1 | async-start | bytes 1048576 | tf_op jit(solution)/shard_map/all_to_all | solution.py:294
  29.5 0.9 %copy-start.2 = (bf16[400,128]{1,0:T(8,128)(2,1)S(1)}, bf16[400,128]{1,0:T(8,128)(2,1)}, u32[]{:S(2)}) copy-start(bf16[400,128]{1,0:T(8,128)(2,1)} %copy-done.1) | copy-start | bytes 307204
  32.3 0.7 %copy-start.3 = (f32[384,128]{1,0:T(8,128)}, f32[384,128]{1,0:T(8,128)S(1)}, u32[]{:S(2)}) copy-start(f32[384,128]{1,0:T(8,128)S(1)} %get-tuple-element.16.refs_0_) | copy-start | bytes 589828
  32.9 15.0 %collective-permute-start.3 = (bf16[400,128]{1,0:T(8,128)(2,1)}, bf16[400,128]{1,0:T(8,128)(2,1)S(1)}, u32[]{:S(2)}, u32[]{:S(2)}) collective-permute-start(bf16[400,128]{1,0:T(8,128)(2,1)} %get-tuple-element.17), channel_id=1, source_target_pairs={{0,3},{1,0},{2,1},{3,2},{4,7},{5,4},{6,5},{7,6},{8,11},{9,8},{10,9... | collective-permute-start | bytes 307208 | tf_op jit(solution)/shard_map/ppermute | solution.py:316
  34.7 13.3 %collective-permute-start.4 = (bf16[400,128]{1,0:T(8,128)(2,1)}, bf16[400,128]{1,0:T(8,128)(2,1)S(1)}, u32[]{:S(2)}, u32[]{:S(2)}) collective-permute-start(bf16[400,128]{1,0:T(8,128)(2,1)} %get-tuple-element.18), channel_id=1, source_target_pairs={{0,2},{1,3},{2,0},{3,1},{4,6},{5,7},{6,4},{7,5},{8,10},{9,11},{10,... | collective-permute-start | bytes 307208 | tf_op jit(solution)/shard_map/ppermute | solution.py:316
  34.7 13.3 %collective-permute-start.5 = (bf16[400,128]{1,0:T(8,128)(2,1)}, bf16[400,128]{1,0:T(8,128)(2,1)S(1)}, u32[]{:S(2)}, u32[]{:S(2)}) collective-permute-start(bf16[400,128]{1,0:T(8,128)(2,1)} %get-tuple-element.19), channel_id=1, source_target_pairs={{0,1},{1,2},{2,3},{3,0},{4,5},{5,6},{6,7},{7,4},{8,9},{9,10},{10,1... | collective-permute-start | bytes 307208 | tf_op jit(solution)/shard_map/ppermute | solution.py:316
  48.0 0.9 %copy-start.4 = (f32[384,128]{1,0:T(8,128)S(1)}, f32[384,128]{1,0:T(8,128)}, u32[]{:S(2)}) copy-start(f32[384,128]{1,0:T(8,128)} %copy-done.3) | copy-start | bytes 589828

commit v3 on v2

--- a/solution.py
+++ b/solution.py
@@ -28,6 +28,10 @@
 
 def copied():
     return pl.BlockSpec()
+
+
+def anywhere():
+    return pl.BlockSpec(memory_space=pl.ANY)
 
 
 def smem():
@@ -101,6 +105,10 @@
     payload_ref[pl.ds(frames * group, 16), :] = gain_rows[...].astype(jnp.bfloat16)
 
 
+def after_kernel(strips_ref, arrived_ref, out_ref):
+    pass
+
+
 def window_kernel(frames, group, slot_ref, adjoint_ref, windows, place):
     width = adjoint_ref.shape[-1]
     for slot in range(frames):
@@ -139,7 +147,7 @@
         for s in range(groups):
             normed = scaled[s] * gain[s]
             value = (normed * jax.nn.sigmoid(normed)).astype(jnp.bfloat16)
-            start = pl.multiple_of(lax.rem(at_ref[0] + groups - s, groups) * group, 16)
+            start = pl.multiple_of((at_ref[0] ^ s) * group, 16)
             hidden[pl.ds(start, group), pl.ds(t * width, width)] = value
 
     grad = lax.dot_general(
@@ -169,29 +177,31 @@
 
 
 def part_kernel(frames, group, at_ref, weight_ref, windows, *refs):
-    groups = (len(refs) - 3) // 2
+    groups = (len(refs) - 1) // 2
     x_refs = refs[:groups]
     part_refs = refs[groups : 2 * groups]
-    scale_ref, own_share_ref, product = refs[2 * groups :]
-    width = scale_ref.shape[-1]
-    product[...] = jnp.dot(weight_ref[...], windows[...], preferred_element_type=jnp.float32)
+    product = refs[2 * groups]
+    width = part_refs[0].shape[-1]
+    product[...] = lax.dot_general(
+        weight_ref[...], windows[...], (((0,), (0,)), ((), ())), preferred_element_type=jnp.float32
+    )
     gain = gains(x_refs, frames * group, group)
     shares = []
     for t in range(frames):
         scale, scaled = norm(x_refs, t, group)
-        scale_ref[pl.ds(t, 1), :] = scale
+        part_refs[0][pl.ds(frames * group + t, 1), :] = scale
         share = jnp.zeros((1, width), jnp.float32)
         for s in range(groups):
             normed = scaled[s] * gain[s]
             sigma = jax.nn.sigmoid(normed)
             slope = sigma * (1.0 + normed * (1.0 - sigma)) * gain[s]
-            start = pl.multiple_of(lax.rem(at_ref[0] + groups - s, groups) * group, 16)
+            start = pl.multiple_of((at_ref[0] ^ s) * group, 16)
             term = product[pl.ds(start, group), pl.ds(t * width, width)] * slope * scale
             part_refs[s][pl.ds(t * group, group), :] = term.astype(part_refs[s].dtype)
             share = share + jnp.sum(term * scaled[s], axis=0, keepdims=True)
         shares.append(share)
     share = jnp.concatenate(shares, axis=0)
-    own_share_ref[...] = share
+    part_refs[0][pl.ds(frames * group + frames, frames), :] = share
     high = share.astype(jnp.bfloat16).astype(jnp.float32)
     both = [high, share - high]
     unused = round_up(2 * frames, 16) - 2 * frames
@@ -202,7 +212,7 @@
         part_refs[s][pl.ds(frames * group, both.shape[0]), :] = both
 
 
-def finish_kernel(frames, group, packed_ref, x_ref, scale_ref, share_ref, *refs):
+def finish_kernel(frames, group, packed_ref, x_ref, *refs):
     own_ref, others, (out_ref, grad_ref) = refs[0], refs[1:-2], refs[-2:]
     taps_out, ins = grad_ref.shape
     blocks, rest, half, rows = packing(taps_out, ins, 1)
@@ -217,7 +227,7 @@
             : taps_out - half, rest:
         ]
 
-    share = share_ref[...]
+    share = own_ref[pl.ds(frames * group + frames, frames), :]
     for ref in others:
         both = ref[pl.ds(frames * group, round_up(2 * frames, 16)), :].astype(jnp.float32)
         share = share + both[:frames] + both[frames : 2 * frames]
@@ -226,7 +236,8 @@
         term = own_ref[pl.ds(t * group, group), :]
         for ref in others:
             term = term + ref[pl.ds(t * group, group), :].astype(jnp.float32)
-        scaled = x_ref[pl.ds(t * group, group), :].astype(jnp.float32) * scale_ref[pl.ds(t, 1), :]
+        scale = own_ref[pl.ds(frames * group + t, 1), :]
+        scaled = x_ref[pl.ds(t * group, group), :].astype(jnp.float32) * scale
         out_ref[t] = (term - scaled * share[t : t + 1]).astype(jnp.bfloat16)
 
 
@@ -255,19 +266,24 @@
         compiler_params=pltpu.CompilerParams(vmem_limit_bytes=60 * MIB),
         name="prepare_kernel",
     )(frame_adjoint[0], inputs[:, :, 0], gain.reshape(1, channels))
+    partners = [[(z, z ^ s) for z in range(groups)] for s in range(groups)]
+    everything = [payload] + [
+        lax.ppermute(payload, "chan", partners[s]) for s in range(1, groups)
+    ]
+    strips = pl.pallas_call(
+        after_kernel,
+        out_shape=jax.ShapeDtypeStruct(strips.shape, strips.dtype),
+        in_specs=[anywhere(), anywhere()],
+        out_specs=anywhere(),
+        input_output_aliases={0: 0},
+        name="after_kernel",
+    )(strips, everything[1])
     strips = lax.all_to_all(strips, "rows", split_axis=0, concat_axis=0, tiled=True)
-
-    shifts = [[(z, (z + s) % groups) for z in range(groups)] for s in range(groups)]
-    everything = [payload] * groups
-    for s in range(1, groups // 2 + 1):
-        everything[s] = lax.ppermute(everything[s - 1], "chan", shifts[1])
-    for s in range(groups - 1, groups // 2, -1):
-        everything[s] = lax.ppermute(everything[(s + 1) % groups], "chan", shifts[groups - 1])
     at = lax.axis_index("chan").astype(jnp.int32).reshape(1)
 
     kernel = weight.reshape(27, channels, groups, channels)
     kernel = jnp.pad(kernel, ((0, 0), (0, spare), (0, 0), (0, spare)))
-    kernel = kernel.reshape(27 * group, ins).T
+    kernel = kernel.reshape(27 * group, ins)
 
     packed_rows = packing(taps_out, ins, count)[3]
     factor = float(frames * count * width) ** (-0.5)
@@ -297,24 +313,21 @@
     )
 
     sent = frames * group + round_up(2 * frames, 16)
-    *parts, scale, share = pl.pallas_call(
+    parts = pl.pallas_call(
         functools.partial(part_kernel, frames, group),
         out_shape=tuple(
-            [jax.ShapeDtypeStruct((frames * group, width), jnp.float32)]
+            [jax.ShapeDtypeStruct((frames * (group + 2), width), jnp.float32)]
             + [jax.ShapeDtypeStruct((sent, width), jnp.bfloat16)] * (groups - 1)
-            + [jax.ShapeDtypeStruct((frames, width), jnp.float32)] * 2
         ),
         in_specs=[smem(), vmem(), vmem()] + [copied()] * groups,
-        out_specs=(vmem(),) * (groups + 2),
+        out_specs=(vmem(),) * groups,
         scratch_shapes=[pltpu.VMEM((ins, pixels), jnp.float32)],
         compiler_params=limit(taps_out, pixels),
         cost_estimate=cost(taps_out, ins, pixels),
         name="part_kernel",
     )(at, kernel, windows, *everything)
 
-    arrived = [
-        lax.ppermute(parts[s], "chan", shifts[groups - s]) for s in range(1, groups)
-    ]
+    arrived = [lax.ppermute(parts[s], "chan", partners[s]) for s in range(1, groups)]
     summed = jnp.sum(pieces.astype(jnp.float32), axis=0).astype(jnp.bfloat16)
     whole = lax.all_gather(summed, "rows", axis=0, tiled=True)
     input_adjoint, grad = pl.pallas_call(
@@ -323,11 +336,11 @@
             jax.ShapeDtypeStruct((frames, group, width), jnp.bfloat16),
             jax.ShapeDtypeStruct((taps_out, ins), jnp.float32),
         ),
-        in_specs=[copied()] * (groups + 4),
+        in_specs=[copied()] * (groups + 2),
         out_specs=(vmem(), vmem()),
         compiler_params=limit(taps_out, pixels),
         name="finish_kernel",
-    )(whole, payload, scale, share, parts[0], *arrived)
+    )(whole, payload, parts[0], *arrived)
     grad = grad.reshape(27, group, groups, group)[:, :channels, :, :channels]
     return (
         input_adjoint[:, :channels, None, :],

time: 50.7 us -> 53 us (1.045)
  starting transfers between devices: 16.1 us -> 21 us
  local copies, waits for them, and re-layouts: 4.52 us -> 2.39 us
  waiting for transfers between devices: 11 us -> 9.88 us
    ppermute x6, starting transfers between devices: 6.6 us -> 12.7 us  [the longest x3 6.96 us: shards(): lax.ppermute(payload, 'chan', partners[s])]
    all_to_all x1, waiting for transfers between devices: 0.01 us -> 3.35 us  [shards(): lax.all_to_all(strips, 'rows', split_axis=0, concat_axis=0, tiled=True)]
    ppermute x6, waiting for transfers between devices: 8.71 us -> 5.47 us  [the longest x3 5.46 us: shards(): lax.ppermute(payload, 'chan', partners[s])]
    reshape x1 -> x0, local copies, waits for them, and re-layouts: 1.38 us -> none  [shards(): kernel = kernel.reshape(27 * group, ins).T]
    all_to_all x1, starting transfers between devices: 5.3 us -> 3.99 us  [shards(): lax.all_to_all(strips, 'rows', split_axis=0, concat_axis=0, tiled=True)]
    all_to_all x1, waiting for transfers between devices: 2.24 us -> 1.06 us  [shards(): lax.all_to_all(packed.reshape(count, packed_rows // count, 128), 'rows',...]
    unnamed x12 -> x10, local copies, waits for them, and re-layouts: 3.14 us -> 2.39 us
  transfers between devices with their start and end apart: 8 -> 8, of which waited for: 3 -> 4; matrix products, arithmetic and copies ran while one was open for 5% -> 2% of each run, Pallas kernels for 6% -> 5%
where the time goes in v3:
time: 53 us; the launch traced here: 52.1 us
  starting transfers between devices  21 us (40%)
  waiting for transfers between devices  9.88 us (19%)
  blocking collectives  9.16 us (17%)
  Pallas kernels  7.88 us (15%)
  local copies, waits for them, and re-layouts  2.39 us (5%)
  other arithmetic  1.12 us (2%)
  between operations  0.66 us (1%)
    all_gather x1, blocking collectives, shards(): whole = lax.all_gather(summed, 'rows', axis=0, tiled=True)  9.16 us
    ppermute x3, starting transfers between devices, shards(): lax.ppermute(payload, 'chan', partners[s])  6.96 us
    ppermute x3, starting transfers between devices, shards(): lax.ppermute(parts[s], 'chan', partners[s])  5.79 us
    ppermute x3, waiting for transfers between devices, shards(): lax.ppermute(payload, 'chan', partners[s])  5.46 us
    all_to_all x1, starting transfers between devices, shards(): lax.all_to_all(packed.reshape(count, packed_rows // count, 128), 'rows',...  4.25 us
    all_to_all x1, starting transfers between devices, shards(): lax.all_to_all(strips, 'rows', split_axis=0, concat_axis=0, tiled=True)  3.99 us
    all_to_all x1, waiting for transfers between devices, shards(): lax.all_to_all(strips, 'rows', split_axis=0, concat_axis=0, tiled=True)  3.35 us
    unnamed x10, local copies, waits for them, and re-layouts  2.39 us
  transfers between devices with their start and end apart: 8, of which 4 were waited for; matrix products, arithmetic and copies ran while one was open for 2% of the time, Pallas kernels for 5%

profile of v3, /device:TPU:0, one launch (start us, length us, event | category | flops | bytes accessed | tf_op | source)
XLA Modules:
  0.0 52.1 jit_solution(11140251468592194033)
XLA Ops:
  0.6 1.7 %prepare_kernel.1 = (bf16[8,3,48,128]{3,2,1,0:T(8,128)(2,1)}, bf16[400,128]{1,0:T(8,128)(2,1)}) custom-call(bf16[48,8,128]{2,1,0:T(8,128)(2,1)} %bitcast.11, bf16[8,48,128]{2,1,0:T(8,128)(2,1)} %bitcast.12, f32[1,48]{1,0:T(1,128)} %bitcast.13), custom_call_target="tpu_custom_call" | custom-call | tf_op jit(solution)/shard_map/prepare_kernel/pallas_call | solution.py:254
  2.4 3.0 %collective-permute-start = (bf16[400,128]{1,0:T(8,128)(2,1)}, bf16[400,128]{1,0:T(8,128)(2,1)S(1)}, u32[]{:S(2)}, u32[]{:S(2)}) collective-permute-start(bf16[400,128]{1,0:T(8,128)(2,1)} %get-tuple-element.11.refs_0_.x_ref), channel_id=1, source_target_pairs={{0,1},{1,0},{2,3},{3,2},{4,5},{5,4},{6,7},{7,6},{8,9},{9,8},{10,11... | collective-permute-start | bytes 307208 | tf_op jit(solution)/shard_map/ppermute | solution.py:271
  5.4 3.2 %collective-permute-done.arrived_ref.refs_1_ = bf16[400,128]{1,0:T(8,128)(2,1)S(1)} collective-permute-done((bf16[400,128]{1,0:T(8,128)(2,1)}, bf16[400,128]{1,0:T(8,128)(2,1)S(1)}, u32[]{:S(2)}, u32[]{:S(2)}) %collective-permute-start) | collective-permute-done | bytes 102432 | tf_op jit(solution)/shard_map/ppermute | solution.py:271
  8.6 0.6 %copy-done.1 = bf16[400,128]{1,0:T(8,128)(2,1)} copy-done((bf16[400,128]{1,0:T(8,128)(2,1)}, bf16[400,128]{1,0:T(8,128)(2,1)S(1)}, u32[]{:S(2)}) %copy-start.1) | copy-done | bytes 102424
  9.2 4.0 %all-to-all-start = ((bf16[8,3,48,128]{3,2,1,0:T(8,128)(2,1)}), bf16[8,3,48,128]{3,2,1,0:T(8,128)(2,1)S(1)}, u32[]{:S(2)}, u32[]{:S(2)}) async-start(bf16[8,3,48,128]{3,2,1,0:T(8,128)(2,1)} %after_kernel.1), calls=%async_computation | async-start | bytes 589824 | tf_op jit(solution)/shard_map/all_to_all | solution.py:281
  13.2 2.6 %collective-permute-start.1 = (bf16[400,128]{1,0:T(8,128)(2,1)}, bf16[400,128]{1,0:T(8,128)(2,1)S(1)}, u32[]{:S(2)}, u32[]{:S(2)}) collective-permute-start(bf16[400,128]{1,0:T(8,128)(2,1)} %get-tuple-element.11.refs_0_.x_ref), channel_id=1, source_target_pairs={{0,2},{1,3},{2,0},{3,1},{4,6},{5,7},{6,4},{7,5},{8,10},{9,11},{10,... | collective-permute-start | bytes 307208 | tf_op jit(solution)/shard_map/ppermute | solution.py:271
  15.8 1.3 %collective-permute-start.2 = (bf16[400,128]{1,0:T(8,128)(2,1)}, bf16[400,128]{1,0:T(8,128)(2,1)S(1)}, u32[]{:S(2)}, u32[]{:S(2)}) collective-permute-start(bf16[400,128]{1,0:T(8,128)(2,1)} %get-tuple-element.11.refs_0_.x_ref), channel_id=1, source_target_pairs={{0,3},{1,2},{2,1},{3,0},{4,7},{5,6},{6,5},{7,4},{8,11},{9,10},{10,... | collective-permute-start | bytes 307208 | tf_op jit(solution)/shard_map/ppermute | solution.py:271
  17.1 3.3 %all-to-all-done.adjoint_ref = bf16[8,3,48,128]{3,2,1,0:T(8,128)(2,1)S(1)} async-done(((bf16[8,3,48,128]{3,2,1,0:T(8,128)(2,1)}), bf16[8,3,48,128]{3,2,1,0:T(8,128)(2,1)S(1)}, u32[]{:S(2)}, u32[]{:S(2)}) %all-to-all-start) | async-done | bytes 294944 | tf_op jit(solution)/shard_map/all_to_all | solution.py:281
  20.5 0.7 %copy-done.4 = s32[8]{0:T(128)S(1)} copy-done((s32[8]{0:T(128)S(1)}, s32[8]{0:T(128)}, u32[]{:S(2)}) %copy-start.4) | copy-done | bytes 56
  21.1 0.9 %window_kernel.1.windows = bf16[1296,1024]{1,0:T(8,128)(2,1)S(1)} custom-call(s32[8]{0:T(128)S(1)} %copy-done.4, bf16[8,3,48,128]{3,2,1,0:T(8,128)(2,1)S(1)} %all-to-all-done.adjoint_ref), custom_call_target="tpu_custom_call" | custom-call | tf_op jit(solution)/shard_map/window_kernel/pallas_call | solution.py:290
  22.1 2.3 %collective-permute-done.1.refs_2_ = bf16[400,128]{1,0:T(8,128)(2,1)S(1)} collective-permute-done((bf16[400,128]{1,0:T(8,128)(2,1)}, bf16[400,128]{1,0:T(8,128)(2,1)S(1)}, u32[]{:S(2)}, u32[]{:S(2)}) %collective-permute-start.1) | collective-permute-done | bytes 102432 | tf_op jit(solution)/shard_map/ppermute | solution.py:271
  24.4 0.0 collective-permute-done.2.refs_3_
  24.4 2.1 %grad_kernel.1 = bf16[2048,128]{1,0:T(8,128)(2,1)} custom-call(s32[1]{0:T(128)} %bitcast.at_ref, bf16[1296,1024]{1,0:T(8,128)(2,1)S(1)} %window_kernel.1.windows, bf16[400,128]{1,0:T(8,128)(2,1)S(1)} %copy-done, bf16[400,128]{1,0:T(8,128)(2,1)S(1)} %copy-done.2, bf16[400,128]{1,0:T(8,128)(2,1)S(1)} %collective-permute-done.1.refs_2_, ...), custom_call_target="tpu_custom_call" | custom-call | flops 509607936 | bytes 3047424 | tf_op jit(solution)/shard_map/grad_kernel/pallas_call | solution.py:299
  26.5 4.2 %all-to-all-start.1 = ((bf16[8,256,128]{2,1,0:T(8,128)(2,1)}), bf16[8,256,128]{2,1,0:T(8,128)(2,1)}, u32[]{:S(2)}, u32[]{:S(2)}) async-start(bf16[8,256,128]{2,1,0:T(8,128)(2,1)} %bitcast.4), calls=%async_computation.1 | async-start | bytes 1048576 | tf_op jit(solution)/shard_map/all_to_all | solution.py:310
  30.7 1.1 %copy-done.3 = bf16[27,48,192]{2,1,0:T(8,128)(2,1)S(1)} copy-done((bf16[27,48,192]{2,1,0:T(8,128)(2,1)S(1)}, bf16[27,48,192]{2,1,0:T(8,128)(2,1)}, u32[]{:S(2)}) %copy-start.3) | copy-done | bytes 497688
  31.8 1.9 %part_kernel.1 = (f32[400,128]{1,0:T(8,128)S(1)}, bf16[400,128]{1,0:T(8,128)(2,1)}, bf16[400,128]{1,0:T(8,128)(2,1)}, bf16[400,128]{1,0:T(8,128)(2,1)S(1)}) custom-call(s32[1]{0:T(128)} %bitcast.at_ref, bf16[1296,192]{1,0:T(8,128)(2,1)S(1)} %bitcast.10, bf16[1296,1024]{1,0:T(8,128)(2,1)S(1)} %window_kernel.1.windows, bf16[400,128]{1,0:T(8,128)(2,1)S(1)} %copy-done, ...), custom_call_target="tpu_custom_call" | custom-call | flops 509607936 | bytes 3047424 | tf_op jit(solution)/shard_map/part_kernel/pallas_call | solution.py:316
  33.7 2.5 %collective-permute-start.3 = (bf16[400,128]{1,0:T(8,128)(2,1)}, bf16[400,128]{1,0:T(8,128)(2,1)S(1)}, u32[]{:S(2)}, u32[]{:S(2)}) collective-permute-start(bf16[400,128]{1,0:T(8,128)(2,1)} %get-tuple-element.13), channel_id=1, source_target_pairs={{0,1},{1,0},{2,3},{3,2},{4,5},{5,4},{6,7},{7,6},{8,9},{9,8},{10,11... | collective-permute-start | bytes 307208 | tf_op jit(solution)/shard_map/ppermute | solution.py:330
  36.2 1.8 %collective-permute-start.4 = (bf16[400,128]{1,0:T(8,128)(2,1)}, bf16[400,128]{1,0:T(8,128)(2,1)S(1)}, u32[]{:S(2)}, u32[]{:S(2)}) collective-permute-start(bf16[400,128]{1,0:T(8,128)(2,1)} %get-tuple-element.14), channel_id=1, source_target_pairs={{0,2},{1,3},{2,0},{3,1},{4,6},{5,7},{6,4},{7,5},{8,10},{9,11},{10,... | collective-permute-start | bytes 307208 | tf_op jit(solution)/shard_map/ppermute | solution.py:330
  38.0 1.5 %collective-permute-start.5 = (bf16[400,128]{1,0:T(8,128)(2,1)S(1)}, bf16[400,128]{1,0:T(8,128)(2,1)S(1)}, u32[]{:S(2)}, u32[]{:S(2)}) collective-permute-start(bf16[400,128]{1,0:T(8,128)(2,1)S(1)} %get-tuple-element.15), channel_id=1, source_target_pairs={{0,3},{1,2},{2,1},{3,0},{4,7},{5,6},{6,5},{7,4},{8,11},{9,10},{10,... | collective-permute-start | bytes 307208 | tf_op jit(solution)/shard_map/ppermute | solution.py:330
  39.5 1.1 %all-to-all-done.1 = bf16[8,256,128]{2,1,0:T(8,128)(2,1)} async-done(((bf16[8,256,128]{2,1,0:T(8,128)(2,1)}), bf16[8,256,128]{2,1,0:T(8,128)(2,1)}, u32[]{:S(2)}, u32[]{:S(2)}) %all-to-all-start.1) | async-done | bytes 524320 | tf_op jit(solution)/shard_map/all_to_all | solution.py:310
  40.6 1.1 %reduce_sum.12 = bf16[256,128]{1,0:T(8,128)(2,1)S(1)} reduce(bf16[8,256,128]{2,1,0:T(8,128)(2,1)} %all-to-all-done.1, bf16[]{:T(256)} %constant.3.clone.1), dimensions={0}, to_apply=%region_0.1 | reduce | flops 229376 | bytes 589826 | tf_op jit(solution)/shard_map/reduce_sum | solution.py:331
  41.7 9.2 %all_gather.3.packed_ref = bf16[2048,128]{1,0:T(8,128)(2,1)S(1)} all-gather(bf16[256,128]{1,0:T(8,128)(2,1)S(1)} %reduce_sum.12), channel_id=1, replica_groups=mesh['rows'=8,'chan'=4] {'rows'}, dimensions={0}, use_global_device_ids=true | all-gather | bytes 589824 | tf_op jit(solution)/shard_map/all_gather | solution.py:332
  50.8 0.0 collective-permute-done.3.refs_1_
  50.8 1.2 %finish_kernel.1 = (bf16[8,48,128]{2,1,0:T(8,128)(2,1)}, f32[1296,192]{1,0:T(8,128)}) custom-call(bf16[2048,128]{1,0:T(8,128)(2,1)S(1)} %all_gather.3.packed_ref, bf16[400,128]{1,0:T(8,128)(2,1)S(1)} %copy-done, f32[400,128]{1,0:T(8,128)S(1)} %get-tuple-element.12.refs_0_, bf16[400,128]{1,0:T(8,128)(2,1)S(1)} %collective-permute-done.3.refs_1_, ...), custom_call_target="tpu_custom_call" | custom-call | tf_op jit(solution)/shard_map/finish_kernel/pallas_call | solution.py:333
  (10 shorter events, 0.0 us)
Async XLA Ops:
  2.4 22.0 %copy-start = (bf16[400,128]{1,0:T(8,128)(2,1)S(1)}, bf16[400,128]{1,0:T(8,128)(2,1)}, u32[]{:S(2)}) copy-start(bf16[400,128]{1,0:T(8,128)(2,1)} %get-tuple-element.11.refs_0_.x_ref) | copy-start | bytes 307204
  2.4 6.2 %collective-permute-start = (bf16[400,128]{1,0:T(8,128)(2,1)}, bf16[400,128]{1,0:T(8,128)(2,1)S(1)}, u32[]{:S(2)}, u32[]{:S(2)}) collective-permute-start(bf16[400,128]{1,0:T(8,128)(2,1)} %get-tuple-element.11.refs_0_.x_ref), channel_id=1, source_target_pairs={{0,1},{1,0},{2,3},{3,2},{4,5},{5,4},{6,7},{7,6},{8,9},{9,8},{10,11... | collective-permute-start | bytes 307208 | tf_op jit(solution)/shard_map/ppermute | solution.py:271
  8.6 0.6 %copy-start.1 = (bf16[400,128]{1,0:T(8,128)(2,1)}, bf16[400,128]{1,0:T(8,128)(2,1)S(1)}, u32[]{:S(2)}) copy-start(bf16[400,128]{1,0:T(8,128)(2,1)S(1)} %collective-permute-done.arrived_ref.refs_1_) | copy-start | bytes 307204
  9.2 15.2 %copy-start.2 = (bf16[400,128]{1,0:T(8,128)(2,1)S(1)}, bf16[400,128]{1,0:T(8,128)(2,1)}, u32[]{:S(2)}) copy-start(bf16[400,128]{1,0:T(8,128)(2,1)} %copy-done.1) | copy-start | bytes 307204
  9.2 11.3 %all-to-all-start = ((bf16[8,3,48,128]{3,2,1,0:T(8,128)(2,1)}), bf16[8,3,48,128]{3,2,1,0:T(8,128)(2,1)S(1)}, u32[]{:S(2)}, u32[]{:S(2)}) async-start(bf16[8,3,48,128]{3,2,1,0:T(8,128)(2,1)} %after_kernel.1), calls=%async_computation | async-start | bytes 589824 | tf_op jit(solution)/shard_map/all_to_all | solution.py:281
  13.2 11.2 %collective-permute-start.1 = (bf16[400,128]{1,0:T(8,128)(2,1)}, bf16[400,128]{1,0:T(8,128)(2,1)S(1)}, u32[]{:S(2)}, u32[]{:S(2)}) collective-permute-start(bf16[400,128]{1,0:T(8,128)(2,1)} %get-tuple-element.11.refs_0_.x_ref), channel_id=1, source_target_pairs={{0,2},{1,3},{2,0},{3,1},{4,6},{5,7},{6,4},{7,5},{8,10},{9,11},{10,... | collective-permute-start | bytes 307208 | tf_op jit(solution)/shard_map/ppermute | solution.py:271
  15.8 8.6 %collective-permute-start.2 = (bf16[400,128]{1,0:T(8,128)(2,1)}, bf16[400,128]{1,0:T(8,128)(2,1)S(1)}, u32[]{:S(2)}, u32[]{:S(2)}) collective-permute-start(bf16[400,128]{1,0:T(8,128)(2,1)} %get-tuple-element.11.refs_0_.x_ref), channel_id=1, source_target_pairs={{0,3},{1,2},{2,1},{3,0},{4,7},{5,6},{6,5},{7,4},{8,11},{9,10},{10,... | collective-permute-start | bytes 307208 | tf_op jit(solution)/shard_map/ppermute | solution.py:271
  20.5 0.7 %copy-start.4 = (s32[8]{0:T(128)S(1)}, s32[8]{0:T(128)}, u32[]{:S(2)}) copy-start(s32[8]{0:T(128)} %slot_ref.1) | copy-start | bytes 100
  26.5 14.1 %all-to-all-start.1 = ((bf16[8,256,128]{2,1,0:T(8,128)(2,1)}), bf16[8,256,128]{2,1,0:T(8,128)(2,1)}, u32[]{:S(2)}, u32[]{:S(2)}) async-start(bf16[8,256,128]{2,1,0:T(8,128)(2,1)} %bitcast.4), calls=%async_computation.1 | async-start | bytes 1048576 | tf_op jit(solution)/shard_map/all_to_all | solution.py:310
  30.7 1.1 %copy-start.3 = (bf16[27,48,192]{2,1,0:T(8,128)(2,1)S(1)}, bf16[27,48,192]{2,1,0:T(8,128)(2,1)}, u32[]{:S(2)}) copy-start(bf16[27,48,192]{2,1,0:T(8,128)(2,1)} %param.9) | copy-start | bytes 1492996
  33.7 17.1 %collective-permute-start.3 = (bf16[400,128]{1,0:T(8,128)(2,1)}, bf16[400,128]{1,0:T(8,128)(2,1)S(1)}, u32[]{:S(2)}, u32[]{:S(2)}) collective-permute-start(bf16[400,128]{1,0:T(8,128)(2,1)} %get-tuple-element.13), channel_id=1, source_target_pairs={{0,1},{1,0},{2,3},{3,2},{4,5},{5,4},{6,7},{7,6},{8,9},{9,8},{10,11... | collective-permute-start | bytes 307208 | tf_op jit(solution)/shard_map/ppermute | solution.py:330
  36.2 14.6 %collective-permute-start.4 = (bf16[400,128]{1,0:T(8,128)(2,1)}, bf16[400,128]{1,0:T(8,128)(2,1)S(1)}, u32[]{:S(2)}, u32[]{:S(2)}) collective-permute-start(bf16[400,128]{1,0:T(8,128)(2,1)} %get-tuple-element.14), channel_id=1, source_target_pairs={{0,2},{1,3},{2,0},{3,1},{4,6},{5,7},{6,4},{7,5},{8,10},{9,11},{10,... | collective-permute-start | bytes 307208 | tf_op jit(solution)/shard_map/ppermute | solution.py:330
  38.0 12.8 %collective-permute-start.5 = (bf16[400,128]{1,0:T(8,128)(2,1)S(1)}, bf16[400,128]{1,0:T(8,128)(2,1)S(1)}, u32[]{:S(2)}, u32[]{:S(2)}) collective-permute-start(bf16[400,128]{1,0:T(8,128)(2,1)S(1)} %get-tuple-element.15), channel_id=1, source_target_pairs={{0,3},{1,2},{2,1},{3,0},{4,7},{5,6},{6,5},{7,4},{8,11},{9,10},{10,... | collective-permute-start | bytes 307208 | tf_op jit(solution)/shard_map/ppermute | solution.py:330

commit v4 on v3

--- a/solution.py
+++ b/solution.py
@@ -105,11 +105,22 @@
     payload_ref[pl.ds(frames * group, 16), :] = gain_rows[...].astype(jnp.bfloat16)
 
 
-def after_kernel(strips_ref, arrived_ref, out_ref):
-    pass
-
-
-def window_kernel(frames, group, slot_ref, adjoint_ref, windows, place):
+def hidden_kernel(frames, group, at_ref, *refs):
+    x_refs, hidden = refs[:-1], refs[-1]
+    groups = len(x_refs)
+    width = hidden.shape[1] // frames
+    gain = gains(x_refs, frames * group, group)
+    for t in range(frames):
+        scale, scaled = norm(x_refs, t, group)
+        for s in range(groups):
+            normed = scaled[s] * gain[s]
+            value = (normed * jax.nn.sigmoid(normed)).astype(jnp.bfloat16)
+            start = pl.multiple_of((at_ref[0] ^ s) * group, 16)
+            hidden[pl.ds(start, group), pl.ds(t * width, width)] = value
+
+
+def grad_kernel(frames, factor, slot_ref, adjoint_ref, hidden, grad_ref, windows, place):
+    group, ins = adjoint_ref.shape[2], hidden.shape[0]
     width = adjoint_ref.shape[-1]
     for slot in range(frames):
         place[slot_ref[slot]] = slot
@@ -134,21 +145,6 @@
                         windows[
                             pl.ds((a * 9 + b * 3 + c) * group, group), pl.ds(t * width, width)
                         ] = shifted
-
-def grad_kernel(frames, group, factor, at_ref, windows, *refs):
-    groups = len(refs) - 2
-    x_refs = refs[:groups]
-    grad_ref, hidden = refs[groups:]
-    ins = groups * group
-    width = windows.shape[1] // frames
-    gain = gains(x_refs, frames * group, group)
-    for t in range(frames):
-        scale, scaled = norm(x_refs, t, group)
-        for s in range(groups):
-            normed = scaled[s] * gain[s]
-            value = (normed * jax.nn.sigmoid(normed)).astype(jnp.bfloat16)
-            start = pl.multiple_of((at_ref[0] ^ s) * group, 16)
-            hidden[pl.ds(start, group), pl.ds(t * width, width)] = value
 
     grad = lax.dot_general(
         windows[...], hidden[...], (((1,), (1,)), ((), ())), preferred_element_type=jnp.float32
@@ -270,14 +266,6 @@
     everything = [payload] + [
         lax.ppermute(payload, "chan", partners[s]) for s in range(1, groups)
     ]
-    strips = pl.pallas_call(
-        after_kernel,
-        out_shape=jax.ShapeDtypeStruct(strips.shape, strips.dtype),
-        in_specs=[anywhere(), anywhere()],
-        out_specs=anywhere(),
-        input_output_aliases={0: 0},
-        name="after_kernel",
-    )(strips, everything[1])
     strips = lax.all_to_all(strips, "rows", split_axis=0, concat_axis=0, tiled=True)
     at = lax.axis_index("chan").astype(jnp.int32).reshape(1)
 
@@ -287,25 +275,30 @@
 
     packed_rows = packing(taps_out, ins, count)[3]
     factor = float(frames * count * width) ** (-0.5)
-    windows = pl.pallas_call(
-        functools.partial(window_kernel, frames, group),
-        out_shape=jax.ShapeDtypeStruct((taps_out, pixels), jnp.bfloat16),
-        in_specs=[smem(), copied()],
+    hidden = pl.pallas_call(
+        functools.partial(hidden_kernel, frames, group),
+        out_shape=jax.ShapeDtypeStruct((ins, pixels), jnp.bfloat16),
+        in_specs=[smem()] + [copied()] * groups,
         out_specs=vmem(),
+        compiler_params=limit(taps_out, pixels),
+        cost_estimate=pl.CostEstimate(
+            flops=16 * ins * pixels, bytes_accessed=32 * ins * pixels, transcendentals=ins * pixels
+        ),
+        name="hidden_kernel",
+    )(at, *everything)
+    packed, windows = pl.pallas_call(
+        functools.partial(grad_kernel, frames, factor),
+        out_shape=(
+            jax.ShapeDtypeStruct((packed_rows, 128), jnp.bfloat16),
+            jax.ShapeDtypeStruct((taps_out, pixels), jnp.bfloat16),
+        ),
+        in_specs=[smem(), copied(), vmem()],
+        out_specs=(vmem(), vmem()),
         scratch_shapes=[pltpu.SMEM((frames,), jnp.int32)],
-        compiler_params=limit(taps_out, pixels),
-        name="window_kernel",
-    )(frame_slot, strips)
-    packed = pl.pallas_call(
-        functools.partial(grad_kernel, frames, group, factor),
-        out_shape=jax.ShapeDtypeStruct((packed_rows, 128), jnp.bfloat16),
-        in_specs=[smem(), vmem()] + [copied()] * groups,
-        out_specs=vmem(),
-        scratch_shapes=[pltpu.VMEM((ins, pixels), jnp.bfloat16)],
         compiler_params=limit(taps_out, pixels),
         cost_estimate=cost(taps_out, ins, pixels),
         name="grad_kernel",
-    )(at, windows, *everything)
+    )(frame_slot, strips, hidden)
 
     pieces = lax.all_to_all(
         packed.reshape(count, packed_rows // count, 128),

time: 53 us -> 55.9 us (1.055)
  local copies, waits for them, and re-layouts: 2.39 us -> 9.22 us
  starting transfers between devices: 21 us -> 18.2 us
  Pallas kernels: 7.88 us -> 6.99 us
    unnamed x10 -> x30, local copies, waits for them, and re-layouts: 2.39 us -> 9.22 us
    all_to_all x1, waiting for transfers between devices: 3.35 us -> 0.01 us  [shards(): lax.all_to_all(strips, 'rows', split_axis=0, concat_axis=0, tiled=True)]
    ppermute x3, waiting for transfers between devices: 5.46 us -> 8.71 us  [shards(): lax.ppermute(payload, 'chan', partners[s])]
    ppermute x3, starting transfers between devices: 6.96 us -> 4.39 us  [shards(): lax.ppermute(payload, 'chan', partners[s])]
    ppermute x3, starting transfers between devices: 5.79 us -> 4.4 us  [shards(): lax.ppermute(parts[s], 'chan', partners[s])]
    all_to_all x1, starting transfers between devices: 3.99 us -> 5.3 us  [shards(): lax.all_to_all(strips, 'rows', split_axis=0, concat_axis=0, tiled=True)]
    pallas_call x3 -> x2, Pallas kernels: 3 us -> 1.99 us  [the longest x1 1.68 us: shards(): pl.pallas_call(functools.partial(grad_kernel, frames, factor), out_shape=...]
  transfers between devices with their start and end apart: 8 -> 8, of which waited for: 4 -> 3; matrix products, arithmetic and copies ran while one was open for 2% -> 2% of each run, Pallas kernels for 5% -> 4%
where the time goes in v4:
time: 55.9 us; the launch traced here: 55.3 us
  starting transfers between devices  18.2 us (33%)
  waiting for transfers between devices  9.64 us (17%)
  blocking collectives  9.33 us (17%)
  local copies, waits for them, and re-layouts  9.22 us (16%)
  Pallas kernels  6.99 us (13%)
  other arithmetic  1.12 us (2%)
  between operations  0.75 us (1%)
    all_gather x1, blocking collectives, shards(): whole = lax.all_gather(summed, 'rows', axis=0, tiled=True)  9.33 us
    unnamed x30, local copies, waits for them, and re-layouts  9.22 us
    ppermute x3, waiting for transfers between devices, shards(): lax.ppermute(payload, 'chan', partners[s])  8.71 us
    all_to_all x1, starting transfers between devices, shards(): lax.all_to_all(strips, 'rows', split_axis=0, concat_axis=0, tiled=True)  5.3 us
    ppermute x3, starting transfers between devices, shards(): lax.ppermute(parts[s], 'chan', partners[s])  4.4 us
    ppermute x3, starting transfers between devices, shards(): lax.ppermute(payload, 'chan', partners[s])  4.39 us
    all_to_all x1, starting transfers between devices, shards(): lax.all_to_all(packed.reshape(count, packed_rows // count, 128), 'rows',...  4.16 us
    pallas_call x1, Pallas kernels, shards(): pl.pallas_call(functools.partial(part_kernel, frames, group), out_shape=t...  1.94 us
  transfers between devices with their start and end apart: 8, of which 3 were waited for; matrix products, arithmetic and copies ran while one was open for 2% of the time, Pallas kernels for 4%

profile of v4, /device:TPU:0, one launch (start us, length us, event | category | flops | bytes accessed | tf_op | source)
XLA Modules:
  0.0 55.3 jit_solution(5819457304180229250)
XLA Ops:
  0.6 1.8 %prepare_kernel.1 = (bf16[8,3,48,128]{3,2,1,0:T(8,128)(2,1)}, bf16[400,128]{1,0:T(8,128)(2,1)}) custom-call(bf16[48,8,128]{2,1,0:T(8,128)(2,1)} %bitcast.12, bf16[8,48,128]{2,1,0:T(8,128)(2,1)} %bitcast.13, f32[1,48]{1,0:T(1,128)} %bitcast.14), custom_call_target="tpu_custom_call" | custom-call | tf_op jit(solution)/shard_map/prepare_kernel/pallas_call | solution.py:250
  2.5 5.3 %all-to-all-start = ((bf16[8,3,48,128]{3,2,1,0:T(8,128)(2,1)}), bf16[8,3,48,128]{3,2,1,0:T(8,128)(2,1)S(1)}, u32[]{:S(2)}, u32[]{:S(2)}) async-start(bf16[8,3,48,128]{3,2,1,0:T(8,128)(2,1)} %get-tuple-element.12), calls=%async_computation | async-start | bytes 589824 | tf_op jit(solution)/shard_map/all_to_all | solution.py:269
  7.8 3.6 %collective-permute-start.2 = (bf16[400,128]{1,0:T(8,128)(2,1)}, bf16[400,128]{1,0:T(8,128)(2,1)S(1)}, u32[]{:S(2)}, u32[]{:S(2)}) collective-permute-start(bf16[400,128]{1,0:T(8,128)(2,1)} %get-tuple-element.13.refs_0_.x_ref), channel_id=1, source_target_pairs={{0,3},{1,2},{2,1},{3,0},{4,7},{5,6},{6,5},{7,4},{8,11},{9,10},{10,... | collective-permute-start | bytes 307208 | tf_op jit(solution)/shard_map/ppermute | solution.py:267
  11.4 0.8 %collective-permute-start = (bf16[400,128]{1,0:T(8,128)(2,1)}, bf16[400,128]{1,0:T(8,128)(2,1)S(1)}, u32[]{:S(2)}, u32[]{:S(2)}) collective-permute-start(bf16[400,128]{1,0:T(8,128)(2,1)} %get-tuple-element.13.refs_0_.x_ref), channel_id=1, source_target_pairs={{0,1},{1,0},{2,3},{3,2},{4,5},{5,4},{6,7},{7,6},{8,9},{9,8},{10,11... | collective-permute-start | bytes 307208 | tf_op jit(solution)/shard_map/ppermute | solution.py:267
  12.2 3.4 %collective-permute-done.2.refs_3_ = bf16[400,128]{1,0:T(8,128)(2,1)S(1)} collective-permute-done((bf16[400,128]{1,0:T(8,128)(2,1)}, bf16[400,128]{1,0:T(8,128)(2,1)S(1)}, u32[]{:S(2)}, u32[]{:S(2)}) %collective-permute-start.2) | collective-permute-done | bytes 102432 | tf_op jit(solution)/shard_map/ppermute | solution.py:267
  15.6 5.3 %collective-permute-done.1.refs_2_ = bf16[400,128]{1,0:T(8,128)(2,1)S(1)} collective-permute-done((bf16[400,128]{1,0:T(8,128)(2,1)}, bf16[400,128]{1,0:T(8,128)(2,1)S(1)}, u32[]{:S(2)}, u32[]{:S(2)}) %collective-permute-start.1) | collective-permute-done | bytes 102432 | tf_op jit(solution)/shard_map/ppermute | solution.py:267
  20.9 1.0 %copy-done = bf16[400,128]{1,0:T(8,128)(2,1)S(1)} copy-done((bf16[400,128]{1,0:T(8,128)(2,1)S(1)}, bf16[400,128]{1,0:T(8,128)(2,1)}, u32[]{:S(2)}) %copy-start) | copy-done | bytes 102424
  22.2 0.7 %copy-done.8 = bf16[192,1024]{1,0:T(8,128)(2,1)} copy-done((bf16[192,1024]{1,0:T(8,128)(2,1)}, bf16[192,1024]{1,0:T(8,128)(2,1)S(1)}, u32[]{:S(2)}) %copy-start.8) | copy-done | bytes 393240
  23.0 0.7 %copy-done.10 = bf16[8,3,48,128]{3,2,1,0:T(8,128)(2,1)} copy-done((bf16[8,3,48,128]{3,2,1,0:T(8,128)(2,1)}, bf16[8,3,48,128]{3,2,1,0:T(8,128)(2,1)S(1)}, u32[]{:S(2)}) %copy-start.10) | copy-done | bytes 294936
  23.7 1.0 %copy-done.9 = bf16[192,1024]{1,0:T(8,128)(2,1)S(1)} copy-done((bf16[192,1024]{1,0:T(8,128)(2,1)S(1)}, bf16[192,1024]{1,0:T(8,128)(2,1)}, u32[]{:S(2)}) %copy-start.9) | copy-done | bytes 393240
  24.7 1.0 %copy-done.11 = bf16[8,3,48,128]{3,2,1,0:T(8,128)(2,1)S(1)} copy-done((bf16[8,3,48,128]{3,2,1,0:T(8,128)(2,1)S(1)}, bf16[8,3,48,128]{3,2,1,0:T(8,128)(2,1)}, u32[]{:S(2)}) %copy-start.11) | copy-done | bytes 294936
  26.3 1.7 %grad_kernel.1 = (bf16[2048,128]{1,0:T(8,128)(2,1)S(1)}, bf16[1296,1024]{1,0:T(8,128)(2,1)S(1)}) custom-call(s32[8]{0:T(128)S(1)} %copy-done.14, bf16[8,3,48,128]{3,2,1,0:T(8,128)(2,1)S(1)} %copy-done.11, bf16[192,1024]{1,0:T(8,128)(2,1)S(1)} %copy-done.9), custom_call_target="tpu_custom_call" | custom-call | flops 509607936 | bytes 3047424 | tf_op jit(solution)/shard_map/grad_kernel/pallas_call | solution.py:289
  28.0 0.8 %copy-done.3 = bf16[2048,128]{1,0:T(8,128)(2,1)} copy-done((bf16[2048,128]{1,0:T(8,128)(2,1)}, bf16[2048,128]{1,0:T(8,128)(2,1)S(1)}, u32[]{:S(2)}) %copy-start.3) | copy-done | bytes 524312
  28.8 4.2 %all-to-all-start.1 = ((bf16[8,256,128]{2,1,0:T(8,128)(2,1)}), bf16[8,256,128]{2,1,0:T(8,128)(2,1)}, u32[]{:S(2)}, u32[]{:S(2)}) async-start(bf16[8,256,128]{2,1,0:T(8,128)(2,1)} %bitcast.11), calls=%async_computation.1 | async-start | bytes 1048576 | tf_op jit(solution)/shard_map/all_to_all | solution.py:303
  32.9 0.9 %copy-done.5 = bf16[400,128]{1,0:T(8,128)(2,1)S(1)} copy-done((bf16[400,128]{1,0:T(8,128)(2,1)S(1)}, bf16[400,128]{1,0:T(8,128)(2,1)}, u32[]{:S(2)}) %copy-start.5) | copy-done | bytes 102424
  33.8 0.9 %copy-done.7 = bf16[400,128]{1,0:T(8,128)(2,1)S(1)} copy-done((bf16[400,128]{1,0:T(8,128)(2,1)S(1)}, bf16[400,128]{1,0:T(8,128)(2,1)}, u32[]{:S(2)}) %copy-start.7) | copy-done | bytes 102424
  34.7 1.9 %part_kernel.1 = (f32[400,128]{1,0:T(8,128)S(1)}, bf16[400,128]{1,0:T(8,128)(2,1)}, bf16[400,128]{1,0:T(8,128)(2,1)}, bf16[400,128]{1,0:T(8,128)(2,1)}) custom-call(s32[1]{0:T(128)} %bitcast.3.at_ref, bf16[1296,192]{1,0:T(8,128)(2,1)S(1)} %bitcast.10, bf16[1296,1024]{1,0:T(8,128)(2,1)S(1)} %get-tuple-element.15.windows, bf16[400,128]{1,0:T(8,128)(2,1)S(1)} %copy-done.1, ...), custom_call_target="tpu_custom_call" | custom-call | flops 509607936 | bytes 3047424 | tf_op jit(solution)/shard_map/part_kernel/pallas_call | solution.py:309
  37.8 2.6 %collective-permute-start.4 = (bf16[400,128]{1,0:T(8,128)(2,1)}, bf16[400,128]{1,0:T(8,128)(2,1)S(1)}, u32[]{:S(2)}, u32[]{:S(2)}) collective-permute-start(bf16[400,128]{1,0:T(8,128)(2,1)} %get-tuple-element.18), channel_id=1, source_target_pairs={{0,2},{1,3},{2,0},{3,1},{4,6},{5,7},{6,4},{7,5},{8,10},{9,11},{10,... | collective-permute-start | bytes 307208 | tf_op jit(solution)/shard_map/ppermute | solution.py:323
  40.4 1.3 %collective-permute-start.5 = (bf16[400,128]{1,0:T(8,128)(2,1)}, bf16[400,128]{1,0:T(8,128)(2,1)S(1)}, u32[]{:S(2)}, u32[]{:S(2)}) collective-permute-start(bf16[400,128]{1,0:T(8,128)(2,1)} %get-tuple-element.19), channel_id=1, source_target_pairs={{0,3},{1,2},{2,1},{3,0},{4,7},{5,6},{6,5},{7,4},{8,11},{9,10},{10,... | collective-permute-start | bytes 307208 | tf_op jit(solution)/shard_map/ppermute | solution.py:323
  41.8 0.9 %all-to-all-done.1 = bf16[8,256,128]{2,1,0:T(8,128)(2,1)} async-done(((bf16[8,256,128]{2,1,0:T(8,128)(2,1)}), bf16[8,256,128]{2,1,0:T(8,128)(2,1)}, u32[]{:S(2)}, u32[]{:S(2)}) %all-to-all-start.1) | async-done | bytes 524320 | tf_op jit(solution)/shard_map/all_to_all | solution.py:303
  42.7 1.1 %reduce_sum.12 = bf16[256,128]{1,0:T(8,128)(2,1)S(1)} reduce(bf16[8,256,128]{2,1,0:T(8,128)(2,1)} %all-to-all-done.1, bf16[]{:T(256)} %constant.3.clone.1), dimensions={0}, to_apply=%region_0.1 | reduce | flops 229376 | bytes 589826 | tf_op jit(solution)/shard_map/reduce_sum | solution.py:324
  43.8 9.3 %all_gather.3.packed_ref = bf16[2048,128]{1,0:T(8,128)(2,1)S(1)} all-gather(bf16[256,128]{1,0:T(8,128)(2,1)S(1)} %reduce_sum.12), channel_id=1, replica_groups=mesh['rows'=8,'chan'=4] {'rows'}, dimensions={0}, use_global_device_ids=true | all-gather | bytes 589824 | tf_op jit(solution)/shard_map/all_gather | solution.py:325
  53.1 0.9 %copy-done.13 = f32[400,128]{1,0:T(8,128)S(1)} copy-done((f32[400,128]{1,0:T(8,128)S(1)}, f32[400,128]{1,0:T(8,128)}, u32[]{:S(2)}) %copy-start.13) | copy-done | bytes 204824
  54.1 1.2 %finish_kernel.1 = (bf16[8,48,128]{2,1,0:T(8,128)(2,1)}, f32[1296,192]{1,0:T(8,128)}) custom-call(bf16[2048,128]{1,0:T(8,128)(2,1)S(1)} %all_gather.3.packed_ref, bf16[400,128]{1,0:T(8,128)(2,1)S(1)} %copy-done.1, f32[400,128]{1,0:T(8,128)S(1)} %copy-done.13, bf16[400,128]{1,0:T(8,128)(2,1)S(1)} %collective-permute-done.3.refs_1_, ...), custom_call_target="tpu_custom_call" | custom-call | tf_op jit(solution)/shard_map/finish_kernel/pallas_call | solution.py:326
  (29 shorter events, 2.1 us)
Async XLA Ops:
  0.6 32.3 %copy-start.2 = (bf16[27,48,192]{2,1,0:T(8,128)(2,1)S(1)}, bf16[27,48,192]{2,1,0:T(8,128)(2,1)}, u32[]{:S(2)}) copy-start(bf16[27,48,192]{2,1,0:T(8,128)(2,1)} %param.9) | copy-start | bytes 1492996
  2.5 30.5 %copy-start.1 = (bf16[400,128]{1,0:T(8,128)(2,1)S(1)}, bf16[400,128]{1,0:T(8,128)(2,1)}, u32[]{:S(2)}) copy-start(bf16[400,128]{1,0:T(8,128)(2,1)} %get-tuple-element.13.refs_0_.x_ref) | copy-start | bytes 307204
  2.5 20.5 %all-to-all-start = ((bf16[8,3,48,128]{3,2,1,0:T(8,128)(2,1)}), bf16[8,3,48,128]{3,2,1,0:T(8,128)(2,1)S(1)}, u32[]{:S(2)}, u32[]{:S(2)}) async-start(bf16[8,3,48,128]{3,2,1,0:T(8,128)(2,1)} %get-tuple-element.12), calls=%async_computation | async-start | bytes 589824 | tf_op jit(solution)/shard_map/all_to_all | solution.py:269
  7.8 7.8 %collective-permute-start.2 = (bf16[400,128]{1,0:T(8,128)(2,1)}, bf16[400,128]{1,0:T(8,128)(2,1)S(1)}, u32[]{:S(2)}, u32[]{:S(2)}) collective-permute-start(bf16[400,128]{1,0:T(8,128)(2,1)} %get-tuple-element.13.refs_0_.x_ref), channel_id=1, source_target_pairs={{0,3},{1,2},{2,1},{3,0},{4,7},{5,6},{6,5},{7,4},{8,11},{9,10},{10,... | collective-permute-start | bytes 307208 | tf_op jit(solution)/shard_map/ppermute | solution.py:267
  11.4 9.5 %collective-permute-start.1 = (bf16[400,128]{1,0:T(8,128)(2,1)}, bf16[400,128]{1,0:T(8,128)(2,1)S(1)}, u32[]{:S(2)}, u32[]{:S(2)}) collective-permute-start(bf16[400,128]{1,0:T(8,128)(2,1)} %get-tuple-element.13.refs_0_.x_ref), channel_id=1, source_target_pairs={{0,2},{1,3},{2,0},{3,1},{4,6},{5,7},{6,4},{7,5},{8,10},{9,11},{10,... | collective-permute-start | bytes 307208 | tf_op jit(solution)/shard_map/ppermute | solution.py:267
  11.4 9.5 %collective-permute-start = (bf16[400,128]{1,0:T(8,128)(2,1)}, bf16[400,128]{1,0:T(8,128)(2,1)S(1)}, u32[]{:S(2)}, u32[]{:S(2)}) collective-permute-start(bf16[400,128]{1,0:T(8,128)(2,1)} %get-tuple-element.13.refs_0_.x_ref), channel_id=1, source_target_pairs={{0,1},{1,0},{2,3},{3,2},{4,5},{5,4},{6,7},{7,6},{8,9},{9,8},{10,11... | collective-permute-start | bytes 307208 | tf_op jit(solution)/shard_map/ppermute | solution.py:267
  20.9 1.3 %copy-start.4 = (bf16[400,128]{1,0:T(8,128)(2,1)}, bf16[400,128]{1,0:T(8,128)(2,1)S(1)}, u32[]{:S(2)}) copy-start(bf16[400,128]{1,0:T(8,128)(2,1)S(1)} %collective-permute-done.1.refs_2_) | copy-start | bytes 307204
  20.9 1.3 %copy-start.6 = (bf16[400,128]{1,0:T(8,128)(2,1)}, bf16[400,128]{1,0:T(8,128)(2,1)S(1)}, u32[]{:S(2)}) copy-start(bf16[400,128]{1,0:T(8,128)(2,1)S(1)} %collective-permute-done.refs_1_) | copy-start | bytes 307204
  20.9 1.0 %copy-start = (bf16[400,128]{1,0:T(8,128)(2,1)S(1)}, bf16[400,128]{1,0:T(8,128)(2,1)}, u32[]{:S(2)}) copy-start(bf16[400,128]{1,0:T(8,128)(2,1)} %get-tuple-element.13.refs_0_.x_ref) | copy-start | bytes 307204
  22.2 0.7 %copy-start.8 = (bf16[192,1024]{1,0:T(8,128)(2,1)}, bf16[192,1024]{1,0:T(8,128)(2,1)S(1)}, u32[]{:S(2)}) copy-start(bf16[192,1024]{1,0:T(8,128)(2,1)S(1)} %hidden_kernel.1.hidden) | copy-start | bytes 1179652
  23.0 0.7 %copy-start.10 = (bf16[8,3,48,128]{3,2,1,0:T(8,128)(2,1)}, bf16[8,3,48,128]{3,2,1,0:T(8,128)(2,1)S(1)}, u32[]{:S(2)}) copy-start(bf16[8,3,48,128]{3,2,1,0:T(8,128)(2,1)S(1)} %all-to-all-done.adjoint_ref) | copy-start | bytes 884740
  23.7 1.0 %copy-start.9 = (bf16[192,1024]{1,0:T(8,128)(2,1)S(1)}, bf16[192,1024]{1,0:T(8,128)(2,1)}, u32[]{:S(2)}) copy-start(bf16[192,1024]{1,0:T(8,128)(2,1)} %copy-done.8) | copy-start | bytes 1179652
  24.7 1.0 %copy-start.11 = (bf16[8,3,48,128]{3,2,1,0:T(8,128)(2,1)S(1)}, bf16[8,3,48,128]{3,2,1,0:T(8,128)(2,1)}, u32[]{:S(2)}) copy-start(bf16[8,3,48,128]{3,2,1,0:T(8,128)(2,1)} %copy-done.10) | copy-start | bytes 884740
  25.6 0.7 %copy-start.14 = (s32[8]{0:T(128)S(1)}, s32[8]{0:T(128)}, u32[]{:S(2)}) copy-start(s32[8]{0:T(128)} %slot_ref.1) | copy-start | bytes 100
  28.0 0.8 %copy-start.3 = (bf16[2048,128]{1,0:T(8,128)(2,1)}, bf16[2048,128]{1,0:T(8,128)(2,1)S(1)}, u32[]{:S(2)}) copy-start(bf16[2048,128]{1,0:T(8,128)(2,1)S(1)} %get-tuple-element.14) | copy-start | bytes 1572868
  28.8 13.9 %all-to-all-start.1 = ((bf16[8,256,128]{2,1,0:T(8,128)(2,1)}), bf16[8,256,128]{2,1,0:T(8,128)(2,1)}, u32[]{:S(2)}, u32[]{:S(2)}) async-start(bf16[8,256,128]{2,1,0:T(8,128)(2,1)} %bitcast.11), calls=%async_computation.1 | async-start | bytes 1048576 | tf_op jit(solution)/shard_map/all_to_all | solution.py:303
  32.9 0.9 %copy-start.5 = (bf16[400,128]{1,0:T(8,128)(2,1)S(1)}, bf16[400,128]{1,0:T(8,128)(2,1)}, u32[]{:S(2)}) copy-start(bf16[400,128]{1,0:T(8,128)(2,1)} %copy-done.4) | copy-start | bytes 307204
  33.8 0.9 %copy-start.7 = (bf16[400,128]{1,0:T(8,128)(2,1)S(1)}, bf16[400,128]{1,0:T(8,128)(2,1)}, u32[]{:S(2)}) copy-start(bf16[400,128]{1,0:T(8,128)(2,1)} %copy-done.6) | copy-start | bytes 307204
  36.7 0.7 %copy-start.12 = (f32[400,128]{1,0:T(8,128)}, f32[400,128]{1,0:T(8,128)S(1)}, u32[]{:S(2)}) copy-start(f32[400,128]{1,0:T(8,128)S(1)} %get-tuple-element.16.refs_0_) | copy-start | bytes 614404
  37.3 15.8 %collective-permute-start.3 = (bf16[400,128]{1,0:T(8,128)(2,1)}, bf16[400,128]{1,0:T(8,128)(2,1)S(1)}, u32[]{:S(2)}, u32[]{:S(2)}) collective-permute-start(bf16[400,128]{1,0:T(8,128)(2,1)} %get-tuple-element.17), channel_id=1, source_target_pairs={{0,1},{1,0},{2,3},{3,2},{4,5},{5,4},{6,7},{7,6},{8,9},{9,8},{10,11... | collective-permute-start | bytes 307208 | tf_op jit(solution)/shard_map/ppermute | solution.py:323
  37.8 15.4 %collective-permute-start.4 = (bf16[400,128]{1,0:T(8,128)(2,1)}, bf16[400,128]{1,0:T(8,128)(2,1)S(1)}, u32[]{:S(2)}, u32[]{:S(2)}) collective-permute-start(bf16[400,128]{1,0:T(8,128)(2,1)} %get-tuple-element.18), channel_id=1, source_target_pairs={{0,2},{1,3},{2,0},{3,1},{4,6},{5,7},{6,4},{7,5},{8,10},{9,11},{10,... | collective-permute-start | bytes 307208 | tf_op jit(solution)/shard_map/ppermute | solution.py:323
  40.4 12.7 %collective-permute-start.5 = (bf16[400,128]{1,0:T(8,128)(2,1)}, bf16[400,128]{1,0:T(8,128)(2,1)S(1)}, u32[]{:S(2)}, u32[]{:S(2)}) collective-permute-start(bf16[400,128]{1,0:T(8,128)(2,1)} %get-tuple-element.19), channel_id=1, source_target_pairs={{0,3},{1,2},{2,1},{3,0},{4,7},{5,6},{6,5},{7,4},{8,11},{9,10},{10,... | collective-permute-start | bytes 307208 | tf_op jit(solution)/shard_map/ppermute | solution.py:323
  53.1 0.9 %copy-start.13 = (f32[400,128]{1,0:T(8,128)S(1)}, f32[400,128]{1,0:T(8,128)}, u32[]{:S(2)}) copy-start(f32[400,128]{1,0:T(8,128)} %copy-done.12) | copy-start | bytes 614404

commit v5 on v3

--- a/solution.py
+++ b/solution.py
@@ -28,10 +28,6 @@
 
 def copied():
     return pl.BlockSpec()
-
-
-def anywhere():
-    return pl.BlockSpec(memory_space=pl.ANY)
 
 
 def smem():
@@ -105,10 +101,6 @@
     payload_ref[pl.ds(frames * group, 16), :] = gain_rows[...].astype(jnp.bfloat16)
 
 
-def after_kernel(strips_ref, arrived_ref, out_ref):
-    pass
-
-
 def window_kernel(frames, group, slot_ref, adjoint_ref, windows, place):
     width = adjoint_ref.shape[-1]
     for slot in range(frames):
@@ -267,17 +259,9 @@
         name="prepare_kernel",
     )(frame_adjoint[0], inputs[:, :, 0], gain.reshape(1, channels))
     partners = [[(z, z ^ s) for z in range(groups)] for s in range(groups)]
-    everything = [payload] + [
-        lax.ppermute(payload, "chan", partners[s]) for s in range(1, groups)
-    ]
-    strips = pl.pallas_call(
-        after_kernel,
-        out_shape=jax.ShapeDtypeStruct(strips.shape, strips.dtype),
-        in_specs=[anywhere(), anywhere()],
-        out_specs=anywhere(),
-        input_output_aliases={0: 0},
-        name="after_kernel",
-    )(strips, everything[1])
+    everything = [payload] * groups
+    for s in range(1, groups):
+        everything[s] = lax.ppermute(everything[s & (s - 1)], "chan", partners[s & -s])
     strips = lax.all_to_all(strips, "rows", split_axis=0, concat_axis=0, tiled=True)
     at = lax.axis_index("chan").astype(jnp.int32).reshape(1)
 

time: 53 us -> 48.7 us (0.919)
  starting transfers between devices: 21 us -> 18.7 us
  local copies, waits for them, and re-layouts: 2.39 us -> 1.74 us
  waiting for transfers between devices: 9.88 us -> 9.28 us
    all_to_all x1, waiting for transfers between devices: 3.35 us -> 0.01 us  [shards(): lax.all_to_all(strips, 'rows', split_axis=0, concat_axis=0, tiled=True)]
    ppermute x3, starting transfers between devices: 6.96 us -> 4.84 us  [shards(): lax.ppermute(everything[s & s - 1], 'chan', partners[s & -s])]
    ppermute x3, waiting for transfers between devices: 5.46 us -> 6.92 us  [shards(): lax.ppermute(everything[s & s - 1], 'chan', partners[s & -s])]
    ppermute x3, starting transfers between devices: 5.79 us -> 4.4 us  [shards(): lax.ppermute(parts[s], 'chan', partners[s])]
    all_to_all x1, starting transfers between devices: 3.99 us -> 5.3 us  [shards(): lax.all_to_all(strips, 'rows', split_axis=0, concat_axis=0, tiled=True)]
    all_to_all x1, waiting for transfers between devices: 1.06 us -> 2.35 us  [shards(): lax.all_to_all(packed.reshape(count, packed_rows // count, 128), 'rows',...]
    unnamed x10 -> x6, local copies, waits for them, and re-layouts: 2.39 us -> 1.74 us
  transfers between devices with their start and end apart: 8 -> 8, of which waited for: 4 -> 3; matrix products, arithmetic and copies ran while one was open for 2% -> 2% of each run, Pallas kernels for 5% -> 6%
where the time goes in v5:
time: 48.7 us; the launch traced here: 48.3 us
  starting transfers between devices  18.7 us (38%)
  waiting for transfers between devices  9.28 us (19%)
  blocking collectives  8.9 us (18%)
  Pallas kernels  7.86 us (16%)
  local copies, waits for them, and re-layouts  1.74 us (4%)
  other arithmetic  1.12 us (2%)
  between operations  0.68 us (1%)
    all_gather x1, blocking collectives, shards(): whole = lax.all_gather(summed, 'rows', axis=0, tiled=True)  8.9 us
    ppermute x3, waiting for transfers between devices, shards(): lax.ppermute(everything[s & s - 1], 'chan', partners[s & -s])  6.92 us
    all_to_all x1, starting transfers between devices, shards(): lax.all_to_all(strips, 'rows', split_axis=0, concat_axis=0, tiled=True)  5.3 us
    ppermute x3, starting transfers between devices, shards(): lax.ppermute(everything[s & s - 1], 'chan', partners[s & -s])  4.84 us
    ppermute x3, starting transfers between devices, shards(): lax.ppermute(parts[s], 'chan', partners[s])  4.4 us
    all_to_all x1, starting transfers between devices, shards(): lax.all_to_all(packed.reshape(count, packed_rows // count, 128), 'rows',...  4.15 us
    all_to_all x1, waiting for transfers between devices, shards(): lax.all_to_all(packed.reshape(count, packed_rows // count, 128), 'rows',...  2.35 us
    pallas_call x1, Pallas kernels, shards(): pl.pallas_call(functools.partial(grad_kernel, frames, group, factor), out...  2.07 us
  transfers between devices with their start and end apart: 8, of which 3 were waited for; matrix products, arithmetic and copies ran while one was open for 2% of the time, Pallas kernels for 6%

profile of v5, /device:TPU:0, one launch (start us, length us, event | category | flops | bytes accessed | tf_op | source)
XLA Modules:
  0.0 48.3 jit_solution(6853840239033893220)
XLA Ops:
  0.6 1.7 %prepare_kernel.1 = (bf16[8,3,48,128]{3,2,1,0:T(8,128)(2,1)}, bf16[400,128]{1,0:T(8,128)(2,1)}) custom-call(bf16[48,8,128]{2,1,0:T(8,128)(2,1)} %bitcast.11, bf16[8,48,128]{2,1,0:T(8,128)(2,1)} %bitcast.12, f32[1,48]{1,0:T(1,128)} %bitcast.13), custom_call_target="tpu_custom_call" | custom-call | tf_op jit(solution)/shard_map/prepare_kernel/pallas_call | solution.py:246
  2.4 5.3 %all-to-all-start = ((bf16[8,3,48,128]{3,2,1,0:T(8,128)(2,1)}), bf16[8,3,48,128]{3,2,1,0:T(8,128)(2,1)S(1)}, u32[]{:S(2)}, u32[]{:S(2)}) async-start(bf16[8,3,48,128]{3,2,1,0:T(8,128)(2,1)} %get-tuple-element.10), calls=%async_computation | async-start | bytes 589824 | tf_op jit(solution)/shard_map/all_to_all | solution.py:265
  7.7 2.6 %collective-permute-start.1 = (bf16[400,128]{1,0:T(8,128)(2,1)}, bf16[400,128]{1,0:T(8,128)(2,1)S(1)}, u32[]{:S(2)}, u32[]{:S(2)}) collective-permute-start(bf16[400,128]{1,0:T(8,128)(2,1)} %get-tuple-element.11.refs_0_.x_ref), channel_id=1, source_target_pairs={{0,2},{1,3},{2,0},{3,1},{4,6},{5,7},{6,4},{7,5},{8,10},{9,11},{10,... | collective-permute-start | bytes 307208 | tf_op jit(solution)/shard_map/ppermute | solution.py:264
  10.3 1.6 %collective-permute-start = (bf16[400,128]{1,0:T(8,128)(2,1)}, bf16[400,128]{1,0:T(8,128)(2,1)S(1)}, u32[]{:S(2)}, u32[]{:S(2)}) collective-permute-start(bf16[400,128]{1,0:T(8,128)(2,1)} %get-tuple-element.11.refs_0_.x_ref), channel_id=1, source_target_pairs={{0,1},{1,0},{2,3},{3,2},{4,5},{5,4},{6,7},{7,6},{8,9},{9,8},{10,11... | collective-permute-start | bytes 307208 | tf_op jit(solution)/shard_map/ppermute | solution.py:264
  11.8 4.5 %collective-permute-done.1.refs_2_ = bf16[400,128]{1,0:T(8,128)(2,1)S(1)} collective-permute-done((bf16[400,128]{1,0:T(8,128)(2,1)}, bf16[400,128]{1,0:T(8,128)(2,1)S(1)}, u32[]{:S(2)}, u32[]{:S(2)}) %collective-permute-start.1) | collective-permute-done | bytes 102432 | tf_op jit(solution)/shard_map/ppermute | solution.py:264
  16.4 0.7 %collective-permute-start.2 = (bf16[400,128]{1,0:T(8,128)(2,1)S(1)}, bf16[400,128]{1,0:T(8,128)(2,1)S(1)}, u32[]{:S(2)}, u32[]{:S(2)}) collective-permute-start(bf16[400,128]{1,0:T(8,128)(2,1)S(1)} %collective-permute-done.1.refs_2_), channel_id=1, source_target_pairs={{0,1},{1,0},{2,3},{3,2},{4,5},{5,4},{6,7},{7,6},{8,9},{9,8},{10,11... | collective-permute-start | bytes 307208 | tf_op jit(solution)/shard_map/ppermute | solution.py:264
  17.0 0.0 all-to-all-done.adjoint_ref
  17.0 0.7 %copy-done.2 = s32[8]{0:T(128)S(1)} copy-done((s32[8]{0:T(128)S(1)}, s32[8]{0:T(128)}, u32[]{:S(2)}) %copy-start.2) | copy-done | bytes 56
  17.7 0.9 %window_kernel.1.windows = bf16[1296,1024]{1,0:T(8,128)(2,1)S(1)} custom-call(s32[8]{0:T(128)S(1)} %copy-done.2, bf16[8,3,48,128]{3,2,1,0:T(8,128)(2,1)S(1)} %all-to-all-done.adjoint_ref), custom_call_target="tpu_custom_call" | custom-call | tf_op jit(solution)/shard_map/window_kernel/pallas_call | solution.py:274
  18.6 0.0 collective-permute-done.refs_1_
  18.6 2.4 %collective-permute-done.2.refs_3_ = bf16[400,128]{1,0:T(8,128)(2,1)S(1)} collective-permute-done((bf16[400,128]{1,0:T(8,128)(2,1)S(1)}, bf16[400,128]{1,0:T(8,128)(2,1)S(1)}, u32[]{:S(2)}, u32[]{:S(2)}) %collective-permute-start.2) | collective-permute-done | bytes 102432 | tf_op jit(solution)/shard_map/ppermute | solution.py:264
  21.0 2.1 %grad_kernel.1 = bf16[2048,128]{1,0:T(8,128)(2,1)} custom-call(s32[1]{0:T(128)} %bitcast.at_ref, bf16[1296,1024]{1,0:T(8,128)(2,1)S(1)} %window_kernel.1.windows, bf16[400,128]{1,0:T(8,128)(2,1)S(1)} %copy-done, bf16[400,128]{1,0:T(8,128)(2,1)S(1)} %collective-permute-done.refs_1_, bf16[400,128]{1,0:T(8,128)(2,1)S(1)} %collective-permute-done.1.refs_2_, ...), custom_call_target="tpu_custom_call" | custom-call | flops 509607936 | bytes 3047424 | tf_op jit(solution)/shard_map/grad_kernel/pallas_call | solution.py:283
  23.1 4.1 %all-to-all-start.1 = ((bf16[8,256,128]{2,1,0:T(8,128)(2,1)}), bf16[8,256,128]{2,1,0:T(8,128)(2,1)}, u32[]{:S(2)}, u32[]{:S(2)}) async-start(bf16[8,256,128]{2,1,0:T(8,128)(2,1)} %bitcast.4), calls=%async_computation.1 | async-start | bytes 1048576 | tf_op jit(solution)/shard_map/all_to_all | solution.py:294
  27.3 0.0 copy-start.1
  27.3 1.1 %copy-done.1 = bf16[27,48,192]{2,1,0:T(8,128)(2,1)S(1)} copy-done((bf16[27,48,192]{2,1,0:T(8,128)(2,1)S(1)}, bf16[27,48,192]{2,1,0:T(8,128)(2,1)}, u32[]{:S(2)}) %copy-start.1) | copy-done | bytes 497688
  28.3 1.9 %part_kernel.1 = (f32[400,128]{1,0:T(8,128)S(1)}, bf16[400,128]{1,0:T(8,128)(2,1)}, bf16[400,128]{1,0:T(8,128)(2,1)}, bf16[400,128]{1,0:T(8,128)(2,1)S(1)}) custom-call(s32[1]{0:T(128)} %bitcast.at_ref, bf16[1296,192]{1,0:T(8,128)(2,1)S(1)} %bitcast.10, bf16[1296,1024]{1,0:T(8,128)(2,1)S(1)} %window_kernel.1.windows, bf16[400,128]{1,0:T(8,128)(2,1)S(1)} %copy-done, ...), custom_call_target="tpu_custom_call" | custom-call | flops 509607936 | bytes 3047424 | tf_op jit(solution)/shard_map/part_kernel/pallas_call | solution.py:300
  30.3 0.9 %collective-permute-start.3 = (bf16[400,128]{1,0:T(8,128)(2,1)}, bf16[400,128]{1,0:T(8,128)(2,1)S(1)}, u32[]{:S(2)}, u32[]{:S(2)}) collective-permute-start(bf16[400,128]{1,0:T(8,128)(2,1)} %get-tuple-element.13), channel_id=1, source_target_pairs={{0,1},{1,0},{2,3},{3,2},{4,5},{5,4},{6,7},{7,6},{8,9},{9,8},{10,11... | collective-permute-start | bytes 307208 | tf_op jit(solution)/shard_map/ppermute | solution.py:314
  31.1 3.3 %collective-permute-start.4 = (bf16[400,128]{1,0:T(8,128)(2,1)}, bf16[400,128]{1,0:T(8,128)(2,1)S(1)}, u32[]{:S(2)}, u32[]{:S(2)}) collective-permute-start(bf16[400,128]{1,0:T(8,128)(2,1)} %get-tuple-element.14), channel_id=1, source_target_pairs={{0,2},{1,3},{2,0},{3,1},{4,6},{5,7},{6,4},{7,5},{8,10},{9,11},{10,... | collective-permute-start | bytes 307208 | tf_op jit(solution)/shard_map/ppermute | solution.py:314
  34.4 0.2 collective-permute-start.5
  34.7 2.4 %all-to-all-done.1 = bf16[8,256,128]{2,1,0:T(8,128)(2,1)} async-done(((bf16[8,256,128]{2,1,0:T(8,128)(2,1)}), bf16[8,256,128]{2,1,0:T(8,128)(2,1)}, u32[]{:S(2)}, u32[]{:S(2)}) %all-to-all-start.1) | async-done | bytes 524320 | tf_op jit(solution)/shard_map/all_to_all | solution.py:294
  37.0 1.1 %reduce_sum.12 = bf16[256,128]{1,0:T(8,128)(2,1)S(1)} reduce(bf16[8,256,128]{2,1,0:T(8,128)(2,1)} %all-to-all-done.1, bf16[]{:T(256)} %constant.3.clone.1), dimensions={0}, to_apply=%region_0.1 | reduce | flops 229376 | bytes 589826 | tf_op jit(solution)/shard_map/reduce_sum | solution.py:315
  38.1 8.9 %all_gather.3.packed_ref = bf16[2048,128]{1,0:T(8,128)(2,1)S(1)} all-gather(bf16[256,128]{1,0:T(8,128)(2,1)S(1)} %reduce_sum.12), channel_id=1, replica_groups=mesh['rows'=8,'chan'=4] {'rows'}, dimensions={0}, use_global_device_ids=true | all-gather | bytes 589824 | tf_op jit(solution)/shard_map/all_gather | solution.py:316
  47.0 0.0 collective-permute-done.3.refs_1_
  47.0 1.2 %finish_kernel.1 = (bf16[8,48,128]{2,1,0:T(8,128)(2,1)}, f32[1296,192]{1,0:T(8,128)}) custom-call(bf16[2048,128]{1,0:T(8,128)(2,1)S(1)} %all_gather.3.packed_ref, bf16[400,128]{1,0:T(8,128)(2,1)S(1)} %copy-done, f32[400,128]{1,0:T(8,128)S(1)} %get-tuple-element.12.refs_0_, bf16[400,128]{1,0:T(8,128)(2,1)S(1)} %collective-permute-done.3.refs_1_, ...), custom_call_target="tpu_custom_call" | custom-call | tf_op jit(solution)/shard_map/finish_kernel/pallas_call | solution.py:317
  (5 shorter events, 0.0 us)
Async XLA Ops:
  2.4 18.7 %copy-start = (bf16[400,128]{1,0:T(8,128)(2,1)S(1)}, bf16[400,128]{1,0:T(8,128)(2,1)}, u32[]{:S(2)}) copy-start(bf16[400,128]{1,0:T(8,128)(2,1)} %get-tuple-element.11.refs_0_.x_ref) | copy-start | bytes 307204
  2.4 14.7 %all-to-all-start = ((bf16[8,3,48,128]{3,2,1,0:T(8,128)(2,1)}), bf16[8,3,48,128]{3,2,1,0:T(8,128)(2,1)S(1)}, u32[]{:S(2)}, u32[]{:S(2)}) async-start(bf16[8,3,48,128]{3,2,1,0:T(8,128)(2,1)} %get-tuple-element.10), calls=%async_computation | async-start | bytes 589824 | tf_op jit(solution)/shard_map/all_to_all | solution.py:265
  7.7 8.7 %collective-permute-start.1 = (bf16[400,128]{1,0:T(8,128)(2,1)}, bf16[400,128]{1,0:T(8,128)(2,1)S(1)}, u32[]{:S(2)}, u32[]{:S(2)}) collective-permute-start(bf16[400,128]{1,0:T(8,128)(2,1)} %get-tuple-element.11.refs_0_.x_ref), channel_id=1, source_target_pairs={{0,2},{1,3},{2,0},{3,1},{4,6},{5,7},{6,4},{7,5},{8,10},{9,11},{10,... | collective-permute-start | bytes 307208 | tf_op jit(solution)/shard_map/ppermute | solution.py:264
  10.3 8.4 %collective-permute-start = (bf16[400,128]{1,0:T(8,128)(2,1)}, bf16[400,128]{1,0:T(8,128)(2,1)S(1)}, u32[]{:S(2)}, u32[]{:S(2)}) collective-permute-start(bf16[400,128]{1,0:T(8,128)(2,1)} %get-tuple-element.11.refs_0_.x_ref), channel_id=1, source_target_pairs={{0,1},{1,0},{2,3},{3,2},{4,5},{5,4},{6,7},{7,6},{8,9},{9,8},{10,11... | collective-permute-start | bytes 307208 | tf_op jit(solution)/shard_map/ppermute | solution.py:264
  16.4 4.7 %collective-permute-start.2 = (bf16[400,128]{1,0:T(8,128)(2,1)S(1)}, bf16[400,128]{1,0:T(8,128)(2,1)S(1)}, u32[]{:S(2)}, u32[]{:S(2)}) collective-permute-start(bf16[400,128]{1,0:T(8,128)(2,1)S(1)} %collective-permute-done.1.refs_2_), channel_id=1, source_target_pairs={{0,1},{1,0},{2,3},{3,2},{4,5},{5,4},{6,7},{7,6},{8,9},{9,8},{10,11... | collective-permute-start | bytes 307208 | tf_op jit(solution)/shard_map/ppermute | solution.py:264
  17.0 0.7 %copy-start.2 = (s32[8]{0:T(128)S(1)}, s32[8]{0:T(128)}, u32[]{:S(2)}) copy-start(s32[8]{0:T(128)} %slot_ref.1) | copy-start | bytes 100
  23.1 13.9 %all-to-all-start.1 = ((bf16[8,256,128]{2,1,0:T(8,128)(2,1)}), bf16[8,256,128]{2,1,0:T(8,128)(2,1)}, u32[]{:S(2)}, u32[]{:S(2)}) async-start(bf16[8,256,128]{2,1,0:T(8,128)(2,1)} %bitcast.4), calls=%async_computation.1 | async-start | bytes 1048576 | tf_op jit(solution)/shard_map/all_to_all | solution.py:294
  27.3 1.1 %copy-start.1 = (bf16[27,48,192]{2,1,0:T(8,128)(2,1)S(1)}, bf16[27,48,192]{2,1,0:T(8,128)(2,1)}, u32[]{:S(2)}) copy-start(bf16[27,48,192]{2,1,0:T(8,128)(2,1)} %param.9) | copy-start | bytes 1492996
  30.3 16.8 %collective-permute-start.3 = (bf16[400,128]{1,0:T(8,128)(2,1)}, bf16[400,128]{1,0:T(8,128)(2,1)S(1)}, u32[]{:S(2)}, u32[]{:S(2)}) collective-permute-start(bf16[400,128]{1,0:T(8,128)(2,1)} %get-tuple-element.13), channel_id=1, source_target_pairs={{0,1},{1,0},{2,3},{3,2},{4,5},{5,4},{6,7},{7,6},{8,9},{9,8},{10,11... | collective-permute-start | bytes 307208 | tf_op jit(solution)/shard_map/ppermute | solution.py:314
  31.1 15.9 %collective-permute-start.4 = (bf16[400,128]{1,0:T(8,128)(2,1)}, bf16[400,128]{1,0:T(8,128)(2,1)S(1)}, u32[]{:S(2)}, u32[]{:S(2)}) collective-permute-start(bf16[400,128]{1,0:T(8,128)(2,1)} %get-tuple-element.14), channel_id=1, source_target_pairs={{0,2},{1,3},{2,0},{3,1},{4,6},{5,7},{6,4},{7,5},{8,10},{9,11},{10,... | collective-permute-start | bytes 307208 | tf_op jit(solution)/shard_map/ppermute | solution.py:314
  34.4 12.6 %collective-permute-start.5 = (bf16[400,128]{1,0:T(8,128)(2,1)S(1)}, bf16[400,128]{1,0:T(8,128)(2,1)S(1)}, u32[]{:S(2)}, u32[]{:S(2)}) collective-permute-start(bf16[400,128]{1,0:T(8,128)(2,1)S(1)} %get-tuple-element.15), channel_id=1, source_target_pairs={{0,3},{1,2},{2,1},{3,0},{4,7},{5,6},{6,5},{7,4},{8,11},{9,10},{10,... | collective-permute-start | bytes 307208 | tf_op jit(solution)/shard_map/ppermute | solution.py:314

commit v6 on v5

--- a/solution.py
+++ b/solution.py
@@ -28,6 +28,10 @@
 
 def copied():
     return pl.BlockSpec()
+
+
+def anywhere():
+    return pl.BlockSpec(memory_space=pl.ANY)
 
 
 def smem():
@@ -101,6 +105,22 @@
     payload_ref[pl.ds(frames * group, 16), :] = gain_rows[...].astype(jnp.bfloat16)
 
 
+def hold_kernel(block_ref, out_ref):
+    pass
+
+
+def hold(block):
+    return pl.pallas_call(
+        hold_kernel,
+        out_shape=jax.ShapeDtypeStruct(block.shape, block.dtype),
+        in_specs=[anywhere()],
+        out_specs=anywhere(),
+        input_output_aliases={0: 0},
+        cost_estimate=pl.CostEstimate(flops=0, bytes_accessed=128 * MIB, transcendentals=0),
+        name="hold_kernel",
+    )(block)
+
+
 def window_kernel(frames, group, slot_ref, adjoint_ref, windows, place):
     width = adjoint_ref.shape[-1]
     for slot in range(frames):
@@ -262,6 +282,8 @@
     everything = [payload] * groups
     for s in range(1, groups):
         everything[s] = lax.ppermute(everything[s & (s - 1)], "chan", partners[s & -s])
+        if s & (s - 1) == 0 and s > 1:
+            everything[s] = hold(everything[s])
     strips = lax.all_to_all(strips, "rows", split_axis=0, concat_axis=0, tiled=True)
     at = lax.axis_index("chan").astype(jnp.int32).reshape(1)
 

time: 48.7 us -> 49.6 us (1.018)
  local copies, waits for them, and re-layouts: 1.74 us -> 2.39 us
    unnamed x6 -> x10, local copies, waits for them, and re-layouts: 1.74 us -> 2.39 us
where the time goes in v6:
time: 49.6 us; the launch traced here: 49.1 us
  starting transfers between devices  18.7 us (38%)
  waiting for transfers between devices  9.49 us (19%)
  blocking collectives  8.9 us (18%)
  Pallas kernels  7.86 us (16%)
  local copies, waits for them, and re-layouts  2.39 us (5%)
  other arithmetic  1.12 us (2%)
  between operations  0.68 us (1%)
    all_gather x1, blocking collectives, shards(): whole = lax.all_gather(summed, 'rows', axis=0, tiled=True)  8.9 us
    ppermute x3, waiting for transfers between devices, shards(): lax.ppermute(everything[s & s - 1], 'chan', partners[s & -s])  7.13 us
    all_to_all x1, starting transfers between devices, shards(): lax.all_to_all(strips, 'rows', split_axis=0, concat_axis=0, tiled=True)  5.3 us
    ppermute x3, starting transfers between devices, shards(): lax.ppermute(everything[s & s - 1], 'chan', partners[s & -s])  4.84 us
    ppermute x3, starting transfers between devices, shards(): lax.ppermute(parts[s], 'chan', partners[s])  4.41 us
    all_to_all x1, starting transfers between devices, shards(): lax.all_to_all(packed.reshape(count, packed_rows // count, 128), 'rows',...  4.14 us
    unnamed x10, local copies, waits for them, and re-layouts  2.39 us
    all_to_all x1, waiting for transfers between devices, shards(): lax.all_to_all(packed.reshape(count, packed_rows // count, 128), 'rows',...  2.35 us
  transfers between devices with their start and end apart: 8, of which 3 were waited for; matrix products, arithmetic and copies ran while one was open for 2% of the time, Pallas kernels for 6%

profile of v6, /device:TPU:0, one launch (start us, length us, event | category | flops | bytes accessed | tf_op | source)
XLA Modules:
  0.0 49.1 jit_solution(9640221269259711166)
XLA Ops:
  0.6 1.7 %prepare_kernel.1 = (bf16[8,3,48,128]{3,2,1,0:T(8,128)(2,1)}, bf16[400,128]{1,0:T(8,128)(2,1)}) custom-call(bf16[48,8,128]{2,1,0:T(8,128)(2,1)} %bitcast.11, bf16[8,48,128]{2,1,0:T(8,128)(2,1)} %bitcast.12, f32[1,48]{1,0:T(1,128)} %bitcast.13), custom_call_target="tpu_custom_call" | custom-call | tf_op jit(solution)/shard_map/prepare_kernel/pallas_call | solution.py:266
  2.4 5.3 %all-to-all-start = ((bf16[8,3,48,128]{3,2,1,0:T(8,128)(2,1)}), bf16[8,3,48,128]{3,2,1,0:T(8,128)(2,1)S(1)}, u32[]{:S(2)}, u32[]{:S(2)}) async-start(bf16[8,3,48,128]{3,2,1,0:T(8,128)(2,1)} %get-tuple-element.10), calls=%async_computation | async-start | bytes 589824 | tf_op jit(solution)/shard_map/all_to_all | solution.py:287
  7.7 2.6 %collective-permute-start.1 = (bf16[400,128]{1,0:T(8,128)(2,1)}, bf16[400,128]{1,0:T(8,128)(2,1)S(1)}, u32[]{:S(2)}, u32[]{:S(2)}) collective-permute-start(bf16[400,128]{1,0:T(8,128)(2,1)} %get-tuple-element.11.refs_0_.x_ref), channel_id=1, source_target_pairs={{0,2},{1,3},{2,0},{3,1},{4,6},{5,7},{6,4},{7,5},{8,10},{9,11},{10,... | collective-permute-start | bytes 307208 | tf_op jit(solution)/shard_map/ppermute | solution.py:284
  10.3 1.6 %collective-permute-start = (bf16[400,128]{1,0:T(8,128)(2,1)}, bf16[400,128]{1,0:T(8,128)(2,1)S(1)}, u32[]{:S(2)}, u32[]{:S(2)}) collective-permute-start(bf16[400,128]{1,0:T(8,128)(2,1)} %get-tuple-element.11.refs_0_.x_ref), channel_id=1, source_target_pairs={{0,1},{1,0},{2,3},{3,2},{4,5},{5,4},{6,7},{7,6},{8,9},{9,8},{10,11... | collective-permute-start | bytes 307208 | tf_op jit(solution)/shard_map/ppermute | solution.py:284
  11.8 4.5 %collective-permute-done.1.block_ref = bf16[400,128]{1,0:T(8,128)(2,1)S(1)} collective-permute-done((bf16[400,128]{1,0:T(8,128)(2,1)}, bf16[400,128]{1,0:T(8,128)(2,1)S(1)}, u32[]{:S(2)}, u32[]{:S(2)}) %collective-permute-start.1) | collective-permute-done | bytes 102432 | tf_op jit(solution)/shard_map/ppermute | solution.py:284
  16.4 0.6 %copy-done.1 = bf16[400,128]{1,0:T(8,128)(2,1)} copy-done((bf16[400,128]{1,0:T(8,128)(2,1)}, bf16[400,128]{1,0:T(8,128)(2,1)S(1)}, u32[]{:S(2)}) %copy-start.1) | copy-done | bytes 102424
  17.0 0.7 %collective-permute-start.2 = (bf16[400,128]{1,0:T(8,128)(2,1)}, bf16[400,128]{1,0:T(8,128)(2,1)S(1)}, u32[]{:S(2)}, u32[]{:S(2)}) collective-permute-start(bf16[400,128]{1,0:T(8,128)(2,1)} %hold_kernel.1.refs_2_), channel_id=1, source_target_pairs={{0,1},{1,0},{2,3},{3,2},{4,5},{5,4},{6,7},{7,6},{8,9},{9,8},{10,11... | collective-permute-start | bytes 307208 | tf_op jit(solution)/shard_map/ppermute | solution.py:284
  17.7 0.0 all-to-all-done.adjoint_ref
  17.7 0.7 %copy-done.4 = s32[8]{0:T(128)S(1)} copy-done((s32[8]{0:T(128)S(1)}, s32[8]{0:T(128)}, u32[]{:S(2)}) %copy-start.4) | copy-done | bytes 56
  18.4 0.9 %window_kernel.1.windows = bf16[1296,1024]{1,0:T(8,128)(2,1)S(1)} custom-call(s32[8]{0:T(128)S(1)} %copy-done.4, bf16[8,3,48,128]{3,2,1,0:T(8,128)(2,1)S(1)} %all-to-all-done.adjoint_ref), custom_call_target="tpu_custom_call" | custom-call | tf_op jit(solution)/shard_map/window_kernel/pallas_call | solution.py:296
  19.3 0.0 collective-permute-done.refs_1_
  19.3 2.6 %collective-permute-done.2.refs_3_ = bf16[400,128]{1,0:T(8,128)(2,1)S(1)} collective-permute-done((bf16[400,128]{1,0:T(8,128)(2,1)}, bf16[400,128]{1,0:T(8,128)(2,1)S(1)}, u32[]{:S(2)}, u32[]{:S(2)}) %collective-permute-start.2) | collective-permute-done | bytes 102432 | tf_op jit(solution)/shard_map/ppermute | solution.py:284
  21.9 2.1 %grad_kernel.1 = bf16[2048,128]{1,0:T(8,128)(2,1)} custom-call(s32[1]{0:T(128)} %bitcast.at_ref, bf16[1296,1024]{1,0:T(8,128)(2,1)S(1)} %window_kernel.1.windows, bf16[400,128]{1,0:T(8,128)(2,1)S(1)} %copy-done, bf16[400,128]{1,0:T(8,128)(2,1)S(1)} %collective-permute-done.refs_1_, bf16[400,128]{1,0:T(8,128)(2,1)S(1)} %copy-done.2, ...), custom_call_target="tpu_custom_call" | custom-call | flops 509607936 | bytes 3047424 | tf_op jit(solution)/shard_map/grad_kernel/pallas_call | solution.py:305
  24.0 4.1 %all-to-all-start.1 = ((bf16[8,256,128]{2,1,0:T(8,128)(2,1)}), bf16[8,256,128]{2,1,0:T(8,128)(2,1)}, u32[]{:S(2)}, u32[]{:S(2)}) async-start(bf16[8,256,128]{2,1,0:T(8,128)(2,1)} %bitcast.4), calls=%async_computation.1 | async-start | bytes 1048576 | tf_op jit(solution)/shard_map/all_to_all | solution.py:316
  28.1 0.0 copy-start.3
  28.1 1.1 %copy-done.3 = bf16[27,48,192]{2,1,0:T(8,128)(2,1)S(1)} copy-done((bf16[27,48,192]{2,1,0:T(8,128)(2,1)S(1)}, bf16[27,48,192]{2,1,0:T(8,128)(2,1)}, u32[]{:S(2)}) %copy-start.3) | copy-done | bytes 497688
  29.2 1.9 %part_kernel.1 = (f32[400,128]{1,0:T(8,128)S(1)}, bf16[400,128]{1,0:T(8,128)(2,1)}, bf16[400,128]{1,0:T(8,128)(2,1)}, bf16[400,128]{1,0:T(8,128)(2,1)S(1)}) custom-call(s32[1]{0:T(128)} %bitcast.at_ref, bf16[1296,192]{1,0:T(8,128)(2,1)S(1)} %bitcast.10, bf16[1296,1024]{1,0:T(8,128)(2,1)S(1)} %window_kernel.1.windows, bf16[400,128]{1,0:T(8,128)(2,1)S(1)} %copy-done, ...), custom_call_target="tpu_custom_call" | custom-call | flops 509607936 | bytes 3047424 | tf_op jit(solution)/shard_map/part_kernel/pallas_call | solution.py:322
  31.1 0.9 %collective-permute-start.3 = (bf16[400,128]{1,0:T(8,128)(2,1)}, bf16[400,128]{1,0:T(8,128)(2,1)S(1)}, u32[]{:S(2)}, u32[]{:S(2)}) collective-permute-start(bf16[400,128]{1,0:T(8,128)(2,1)} %get-tuple-element.13), channel_id=1, source_target_pairs={{0,1},{1,0},{2,3},{3,2},{4,5},{5,4},{6,7},{7,6},{8,9},{9,8},{10,11... | collective-permute-start | bytes 307208 | tf_op jit(solution)/shard_map/ppermute | solution.py:336
  32.0 3.3 %collective-permute-start.4 = (bf16[400,128]{1,0:T(8,128)(2,1)}, bf16[400,128]{1,0:T(8,128)(2,1)S(1)}, u32[]{:S(2)}, u32[]{:S(2)}) collective-permute-start(bf16[400,128]{1,0:T(8,128)(2,1)} %get-tuple-element.14), channel_id=1, source_target_pairs={{0,2},{1,3},{2,0},{3,1},{4,6},{5,7},{6,4},{7,5},{8,10},{9,11},{10,... | collective-permute-start | bytes 307208 | tf_op jit(solution)/shard_map/ppermute | solution.py:336
  35.3 0.2 collective-permute-start.5
  35.5 2.4 %all-to-all-done.1 = bf16[8,256,128]{2,1,0:T(8,128)(2,1)} async-done(((bf16[8,256,128]{2,1,0:T(8,128)(2,1)}), bf16[8,256,128]{2,1,0:T(8,128)(2,1)}, u32[]{:S(2)}, u32[]{:S(2)}) %all-to-all-start.1) | async-done | bytes 524320 | tf_op jit(solution)/shard_map/all_to_all | solution.py:316
  37.9 1.1 %reduce_sum.12 = bf16[256,128]{1,0:T(8,128)(2,1)S(1)} reduce(bf16[8,256,128]{2,1,0:T(8,128)(2,1)} %all-to-all-done.1, bf16[]{:T(256)} %constant.3.clone.1), dimensions={0}, to_apply=%region_0.1 | reduce | flops 229376 | bytes 589826 | tf_op jit(solution)/shard_map/reduce_sum | solution.py:337
  39.0 8.9 %all_gather.3.packed_ref = bf16[2048,128]{1,0:T(8,128)(2,1)S(1)} all-gather(bf16[256,128]{1,0:T(8,128)(2,1)S(1)} %reduce_sum.12), channel_id=1, replica_groups=mesh['rows'=8,'chan'=4] {'rows'}, dimensions={0}, use_global_device_ids=true | all-gather | bytes 589824 | tf_op jit(solution)/shard_map/all_gather | solution.py:338
  47.9 1.2 %finish_kernel.1 = (bf16[8,48,128]{2,1,0:T(8,128)(2,1)}, f32[1296,192]{1,0:T(8,128)}) custom-call(bf16[2048,128]{1,0:T(8,128)(2,1)S(1)} %all_gather.3.packed_ref, bf16[400,128]{1,0:T(8,128)(2,1)S(1)} %copy-done, f32[400,128]{1,0:T(8,128)S(1)} %get-tuple-element.12.refs_0_, bf16[400,128]{1,0:T(8,128)(2,1)S(1)} %collective-permute-done.3.refs_1_, ...), custom_call_target="tpu_custom_call" | custom-call | tf_op jit(solution)/shard_map/finish_kernel/pallas_call | solution.py:339
  (10 shorter events, 0.0 us)
Async XLA Ops:
  2.4 19.5 %copy-start = (bf16[400,128]{1,0:T(8,128)(2,1)S(1)}, bf16[400,128]{1,0:T(8,128)(2,1)}, u32[]{:S(2)}) copy-start(bf16[400,128]{1,0:T(8,128)(2,1)} %get-tuple-element.11.refs_0_.x_ref) | copy-start | bytes 307204
  2.4 15.3 %all-to-all-start = ((bf16[8,3,48,128]{3,2,1,0:T(8,128)(2,1)}), bf16[8,3,48,128]{3,2,1,0:T(8,128)(2,1)S(1)}, u32[]{:S(2)}, u32[]{:S(2)}) async-start(bf16[8,3,48,128]{3,2,1,0:T(8,128)(2,1)} %get-tuple-element.10), calls=%async_computation | async-start | bytes 589824 | tf_op jit(solution)/shard_map/all_to_all | solution.py:287
  7.7 8.7 %collective-permute-start.1 = (bf16[400,128]{1,0:T(8,128)(2,1)}, bf16[400,128]{1,0:T(8,128)(2,1)S(1)}, u32[]{:S(2)}, u32[]{:S(2)}) collective-permute-start(bf16[400,128]{1,0:T(8,128)(2,1)} %get-tuple-element.11.refs_0_.x_ref), channel_id=1, source_target_pairs={{0,2},{1,3},{2,0},{3,1},{4,6},{5,7},{6,4},{7,5},{8,10},{9,11},{10,... | collective-permute-start | bytes 307208 | tf_op jit(solution)/shard_map/ppermute | solution.py:284
  10.3 9.0 %collective-permute-start = (bf16[400,128]{1,0:T(8,128)(2,1)}, bf16[400,128]{1,0:T(8,128)(2,1)S(1)}, u32[]{:S(2)}, u32[]{:S(2)}) collective-permute-start(bf16[400,128]{1,0:T(8,128)(2,1)} %get-tuple-element.11.refs_0_.x_ref), channel_id=1, source_target_pairs={{0,1},{1,0},{2,3},{3,2},{4,5},{5,4},{6,7},{7,6},{8,9},{9,8},{10,11... | collective-permute-start | bytes 307208 | tf_op jit(solution)/shard_map/ppermute | solution.py:284
  16.4 0.6 %copy-start.1 = (bf16[400,128]{1,0:T(8,128)(2,1)}, bf16[400,128]{1,0:T(8,128)(2,1)S(1)}, u32[]{:S(2)}) copy-start(bf16[400,128]{1,0:T(8,128)(2,1)S(1)} %collective-permute-done.1.block_ref) | copy-start | bytes 307204
  17.0 4.9 %copy-start.2 = (bf16[400,128]{1,0:T(8,128)(2,1)S(1)}, bf16[400,128]{1,0:T(8,128)(2,1)}, u32[]{:S(2)}) copy-start(bf16[400,128]{1,0:T(8,128)(2,1)} %hold_kernel.1.refs_2_) | copy-start | bytes 307204
  17.0 4.9 %collective-permute-start.2 = (bf16[400,128]{1,0:T(8,128)(2,1)}, bf16[400,128]{1,0:T(8,128)(2,1)S(1)}, u32[]{:S(2)}, u32[]{:S(2)}) collective-permute-start(bf16[400,128]{1,0:T(8,128)(2,1)} %hold_kernel.1.refs_2_), channel_id=1, source_target_pairs={{0,1},{1,0},{2,3},{3,2},{4,5},{5,4},{6,7},{7,6},{8,9},{9,8},{10,11... | collective-permute-start | bytes 307208 | tf_op jit(solution)/shard_map/ppermute | solution.py:284
  17.7 0.7 %copy-start.4 = (s32[8]{0:T(128)S(1)}, s32[8]{0:T(128)}, u32[]{:S(2)}) copy-start(s32[8]{0:T(128)} %slot_ref.1) | copy-start | bytes 100
  24.0 13.9 %all-to-all-start.1 = ((bf16[8,256,128]{2,1,0:T(8,128)(2,1)}), bf16[8,256,128]{2,1,0:T(8,128)(2,1)}, u32[]{:S(2)}, u32[]{:S(2)}) async-start(bf16[8,256,128]{2,1,0:T(8,128)(2,1)} %bitcast.4), calls=%async_computation.1 | async-start | bytes 1048576 | tf_op jit(solution)/shard_map/all_to_all | solution.py:316
  28.1 1.1 %copy-start.3 = (bf16[27,48,192]{2,1,0:T(8,128)(2,1)S(1)}, bf16[27,48,192]{2,1,0:T(8,128)(2,1)}, u32[]{:S(2)}) copy-start(bf16[27,48,192]{2,1,0:T(8,128)(2,1)} %param.9) | copy-start | bytes 1492996
  31.1 16.8 %collective-permute-start.3 = (bf16[400,128]{1,0:T(8,128)(2,1)}, bf16[400,128]{1,0:T(8,128)(2,1)S(1)}, u32[]{:S(2)}, u32[]{:S(2)}) collective-permute-start(bf16[400,128]{1,0:T(8,128)(2,1)} %get-tuple-element.13), channel_id=1, source_target_pairs={{0,1},{1,0},{2,3},{3,2},{4,5},{5,4},{6,7},{7,6},{8,9},{9,8},{10,11... | collective-permute-start | bytes 307208 | tf_op jit(solution)/shard_map/ppermute | solution.py:336
  32.0 15.9 %collective-permute-start.4 = (bf16[400,128]{1,0:T(8,128)(2,1)}, bf16[400,128]{1,0:T(8,128)(2,1)S(1)}, u32[]{:S(2)}, u32[]{:S(2)}) collective-permute-start(bf16[400,128]{1,0:T(8,128)(2,1)} %get-tuple-element.14), channel_id=1, source_target_pairs={{0,2},{1,3},{2,0},{3,1},{4,6},{5,7},{6,4},{7,5},{8,10},{9,11},{10,... | collective-permute-start | bytes 307208 | tf_op jit(solution)/shard_map/ppermute | solution.py:336
  35.3 12.6 %collective-permute-start.5 = (bf16[400,128]{1,0:T(8,128)(2,1)S(1)}, bf16[400,128]{1,0:T(8,128)(2,1)S(1)}, u32[]{:S(2)}, u32[]{:S(2)}) collective-permute-start(bf16[400,128]{1,0:T(8,128)(2,1)S(1)} %get-tuple-element.15), channel_id=1, source_target_pairs={{0,3},{1,2},{2,1},{3,0},{4,7},{5,6},{6,5},{7,4},{8,11},{9,10},{10,... | collective-permute-start | bytes 307208 | tf_op jit(solution)/shard_map/ppermute | solution.py:336

commit v7 on v5

--- a/solution.py
+++ b/solution.py
@@ -30,12 +30,16 @@
     return pl.BlockSpec()
 
 
+def anywhere():
+    return pl.BlockSpec(memory_space=pl.ANY)
+
+
 def smem():
     return pl.BlockSpec(memory_space=pltpu.SMEM)
 
 
 def limit(taps_out, pixels):
-    return pltpu.CompilerParams(vmem_limit_bytes=10 * MIB + 6 * taps_out * pixels)
+    return pltpu.CompilerParams(vmem_limit_bytes=4 * MIB + 4 * taps_out * pixels)
 
 
 def cost(rows, columns, depth):
@@ -205,19 +209,10 @@
 
 
 def finish_kernel(frames, group, packed_ref, x_ref, *refs):
-    own_ref, others, (out_ref, grad_ref) = refs[0], refs[1:-2], refs[-2:]
+    own_ref, others = refs[0], refs[1:-5]
+    out_hbm, grad_hbm, out_ref, grad_ref, done = refs[-5:]
     taps_out, ins = grad_ref.shape
     blocks, rest, half, rows = packing(taps_out, ins, 1)
-    for block in range(blocks):
-        grad_ref[:, pl.ds(block * 128, 128)] = packed_ref[
-            pl.ds(block * taps_out, taps_out), :
-        ].astype(jnp.float32)
-    if rest:
-        both = packed_ref[pl.ds(blocks * taps_out, half), :].astype(jnp.float32)
-        grad_ref[pl.ds(0, half), pl.ds(blocks * 128, rest)] = both[:, :rest]
-        grad_ref[pl.ds(half, taps_out - half), pl.ds(blocks * 128, rest)] = both[
-            : taps_out - half, rest:
-        ]
 
     share = own_ref[pl.ds(frames * group + frames, frames), :]
     for ref in others:
@@ -231,6 +226,32 @@
         scale = own_ref[pl.ds(frames * group + t, 1), :]
         scaled = x_ref[pl.ds(t * group, group), :].astype(jnp.float32) * scale
         out_ref[t] = (term - scaled * share[t : t + 1]).astype(jnp.bfloat16)
+    copies = [pltpu.make_async_copy(out_ref, out_hbm, done.at[0])]
+    copies[0].start()
+
+    part = taps_out // 3
+    for p in range(3):
+        first = p * part
+        for block in range(blocks):
+            grad_ref[pl.ds(first, part), pl.ds(block * 128, 128)] = packed_ref[
+                pl.ds(block * taps_out + first, part), :
+            ].astype(jnp.float32)
+        if rest:
+            for begin, end, low in ((0, half, 0), (half, taps_out, rest)):
+                begin, end = max(begin, first), min(end, first + part)
+                if begin < end:
+                    shift = half if low else 0
+                    grad_ref[pl.ds(begin, end - begin), pl.ds(blocks * 128, rest)] = packed_ref[
+                        pl.ds(blocks * taps_out + begin - shift, end - begin), :
+                    ].astype(jnp.float32)[:, low : low + rest]
+        copies.append(
+            pltpu.make_async_copy(
+                grad_ref.at[pl.ds(first, part)], grad_hbm.at[pl.ds(first, part)], done.at[p + 1]
+            )
+        )
+        copies[-1].start()
+    for copy in copies:
+        copy.wait()
 
 
 def shards(frame_adjoint, frame_slot, inputs, gain, weight):
@@ -320,8 +341,13 @@
             jax.ShapeDtypeStruct((frames, group, width), jnp.bfloat16),
             jax.ShapeDtypeStruct((taps_out, ins), jnp.float32),
         ),
-        in_specs=[copied()] * (groups + 2),
-        out_specs=(vmem(), vmem()),
+        in_specs=[vmem()] * (groups + 2),
+        out_specs=(anywhere(), anywhere()),
+        scratch_shapes=[
+            pltpu.VMEM((frames, group, width), jnp.bfloat16),
+            pltpu.VMEM((taps_out, ins), jnp.float32),
+            pltpu.SemaphoreType.DMA((4,)),
+        ],
         compiler_params=limit(taps_out, pixels),
         name="finish_kernel",
     )(whole, payload, parts[0], *arrived)

time: 48.7 us -> 48.7 us (level)
  no operation moved by 1% of the time
where the time goes in v7:
time: 48.7 us; the launch traced here: 48.3 us
  starting transfers between devices  18.7 us (38%)
  waiting for transfers between devices  9.28 us (19%)
  blocking collectives  8.9 us (18%)
  Pallas kernels  7.85 us (16%)
  local copies, waits for them, and re-layouts  1.74 us (4%)
  other arithmetic  1.12 us (2%)
  between operations  0.68 us (1%)
    all_gather x1, blocking collectives, shards(): whole = lax.all_gather(summed, 'rows', axis=0, tiled=True)  8.9 us
    ppermute x3, waiting for transfers between devices, shards(): lax.ppermute(everything[s & s - 1], 'chan', partners[s & -s])  6.92 us
    all_to_all x1, starting transfers between devices, shards(): lax.all_to_all(strips, 'rows', split_axis=0, concat_axis=0, tiled=True)  5.3 us
    ppermute x3, starting transfers between devices, shards(): lax.ppermute(everything[s & s - 1], 'chan', partners[s & -s])  4.84 us
    ppermute x3, starting transfers between devices, shards(): lax.ppermute(parts[s], 'chan', partners[s])  4.4 us
    all_to_all x1, starting transfers between devices, shards(): lax.all_to_all(packed.reshape(count, packed_rows // count, 128), 'rows',...  4.15 us
    all_to_all x1, waiting for transfers between devices, shards(): lax.all_to_all(packed.reshape(count, packed_rows // count, 128), 'rows',...  2.35 us
    pallas_call x1, Pallas kernels, shards(): pl.pallas_call(functools.partial(grad_kernel, frames, group, factor), out...  2.07 us
  transfers between devices with their start and end apart: 8, of which 3 were waited for; matrix products, arithmetic and copies ran while one was open for 2% of the time, Pallas kernels for 6%

profile of v7, /device:TPU:0, one launch (start us, length us, event | category | flops | bytes accessed | tf_op | source)
XLA Modules:
  0.0 48.3 jit_solution(3995999859684778515)
XLA Ops:
  0.6 1.7 %prepare_kernel.1 = (bf16[8,3,48,128]{3,2,1,0:T(8,128)(2,1)}, bf16[400,128]{1,0:T(8,128)(2,1)}) custom-call(bf16[48,8,128]{2,1,0:T(8,128)(2,1)} %bitcast.11, bf16[8,48,128]{2,1,0:T(8,128)(2,1)} %bitcast.12, f32[1,48]{1,0:T(1,128)} %bitcast.13), custom_call_target="tpu_custom_call" | custom-call | tf_op jit(solution)/shard_map/prepare_kernel/pallas_call | solution.py:267
  2.4 5.3 %all-to-all-start = ((bf16[8,3,48,128]{3,2,1,0:T(8,128)(2,1)}), bf16[8,3,48,128]{3,2,1,0:T(8,128)(2,1)S(1)}, u32[]{:S(2)}, u32[]{:S(2)}) async-start(bf16[8,3,48,128]{3,2,1,0:T(8,128)(2,1)} %get-tuple-element.10), calls=%async_computation | async-start | bytes 589824 | tf_op jit(solution)/shard_map/all_to_all | solution.py:286
  7.7 2.6 %collective-permute-start.1 = (bf16[400,128]{1,0:T(8,128)(2,1)}, bf16[400,128]{1,0:T(8,128)(2,1)S(1)}, u32[]{:S(2)}, u32[]{:S(2)}) collective-permute-start(bf16[400,128]{1,0:T(8,128)(2,1)} %get-tuple-element.11.refs_0_.x_ref), channel_id=1, source_target_pairs={{0,2},{1,3},{2,0},{3,1},{4,6},{5,7},{6,4},{7,5},{8,10},{9,11},{10,... | collective-permute-start | bytes 307208 | tf_op jit(solution)/shard_map/ppermute | solution.py:285
  10.3 1.6 %collective-permute-start = (bf16[400,128]{1,0:T(8,128)(2,1)}, bf16[400,128]{1,0:T(8,128)(2,1)S(1)}, u32[]{:S(2)}, u32[]{:S(2)}) collective-permute-start(bf16[400,128]{1,0:T(8,128)(2,1)} %get-tuple-element.11.refs_0_.x_ref), channel_id=1, source_target_pairs={{0,1},{1,0},{2,3},{3,2},{4,5},{5,4},{6,7},{7,6},{8,9},{9,8},{10,11... | collective-permute-start | bytes 307208 | tf_op jit(solution)/shard_map/ppermute | solution.py:285
  11.8 4.5 %collective-permute-done.1.refs_2_ = bf16[400,128]{1,0:T(8,128)(2,1)S(1)} collective-permute-done((bf16[400,128]{1,0:T(8,128)(2,1)}, bf16[400,128]{1,0:T(8,128)(2,1)S(1)}, u32[]{:S(2)}, u32[]{:S(2)}) %collective-permute-start.1) | collective-permute-done | bytes 102432 | tf_op jit(solution)/shard_map/ppermute | solution.py:285
  16.4 0.7 %collective-permute-start.2 = (bf16[400,128]{1,0:T(8,128)(2,1)S(1)}, bf16[400,128]{1,0:T(8,128)(2,1)S(1)}, u32[]{:S(2)}, u32[]{:S(2)}) collective-permute-start(bf16[400,128]{1,0:T(8,128)(2,1)S(1)} %collective-permute-done.1.refs_2_), channel_id=1, source_target_pairs={{0,1},{1,0},{2,3},{3,2},{4,5},{5,4},{6,7},{7,6},{8,9},{9,8},{10,11... | collective-permute-start | bytes 307208 | tf_op jit(solution)/shard_map/ppermute | solution.py:285
  17.0 0.0 all-to-all-done.adjoint_ref
  17.0 0.7 %copy-done.2 = s32[8]{0:T(128)S(1)} copy-done((s32[8]{0:T(128)S(1)}, s32[8]{0:T(128)}, u32[]{:S(2)}) %copy-start.2) | copy-done | bytes 56
  17.7 0.9 %window_kernel.1.windows = bf16[1296,1024]{1,0:T(8,128)(2,1)S(1)} custom-call(s32[8]{0:T(128)S(1)} %copy-done.2, bf16[8,3,48,128]{3,2,1,0:T(8,128)(2,1)S(1)} %all-to-all-done.adjoint_ref), custom_call_target="tpu_custom_call" | custom-call | tf_op jit(solution)/shard_map/window_kernel/pallas_call | solution.py:295
  18.6 0.0 collective-permute-done.refs_1_
  18.6 2.4 %collective-permute-done.2.refs_3_ = bf16[400,128]{1,0:T(8,128)(2,1)S(1)} collective-permute-done((bf16[400,128]{1,0:T(8,128)(2,1)S(1)}, bf16[400,128]{1,0:T(8,128)(2,1)S(1)}, u32[]{:S(2)}, u32[]{:S(2)}) %collective-permute-start.2) | collective-permute-done | bytes 102432 | tf_op jit(solution)/shard_map/ppermute | solution.py:285
  21.0 2.1 %grad_kernel.1 = bf16[2048,128]{1,0:T(8,128)(2,1)} custom-call(s32[1]{0:T(128)} %bitcast.at_ref, bf16[1296,1024]{1,0:T(8,128)(2,1)S(1)} %window_kernel.1.windows, bf16[400,128]{1,0:T(8,128)(2,1)S(1)} %copy-done, bf16[400,128]{1,0:T(8,128)(2,1)S(1)} %collective-permute-done.refs_1_, bf16[400,128]{1,0:T(8,128)(2,1)S(1)} %collective-permute-done.1.refs_2_, ...), custom_call_target="tpu_custom_call" | custom-call | flops 509607936 | bytes 3047424 | tf_op jit(solution)/shard_map/grad_kernel/pallas_call | solution.py:304
  23.1 4.1 %all-to-all-start.1 = ((bf16[8,256,128]{2,1,0:T(8,128)(2,1)}), bf16[8,256,128]{2,1,0:T(8,128)(2,1)}, u32[]{:S(2)}, u32[]{:S(2)}) async-start(bf16[8,256,128]{2,1,0:T(8,128)(2,1)} %bitcast.4), calls=%async_computation.1 | async-start | bytes 1048576 | tf_op jit(solution)/shard_map/all_to_all | solution.py:315
  27.3 0.0 copy-start.1
  27.3 1.1 %copy-done.1 = bf16[27,48,192]{2,1,0:T(8,128)(2,1)S(1)} copy-done((bf16[27,48,192]{2,1,0:T(8,128)(2,1)S(1)}, bf16[27,48,192]{2,1,0:T(8,128)(2,1)}, u32[]{:S(2)}) %copy-start.1) | copy-done | bytes 497688
  28.3 1.9 %part_kernel.1 = (f32[400,128]{1,0:T(8,128)S(1)}, bf16[400,128]{1,0:T(8,128)(2,1)}, bf16[400,128]{1,0:T(8,128)(2,1)}, bf16[400,128]{1,0:T(8,128)(2,1)S(1)}) custom-call(s32[1]{0:T(128)} %bitcast.at_ref, bf16[1296,192]{1,0:T(8,128)(2,1)S(1)} %bitcast.10, bf16[1296,1024]{1,0:T(8,128)(2,1)S(1)} %window_kernel.1.windows, bf16[400,128]{1,0:T(8,128)(2,1)S(1)} %copy-done, ...), custom_call_target="tpu_custom_call" | custom-call | flops 509607936 | bytes 3047424 | tf_op jit(solution)/shard_map/part_kernel/pallas_call | solution.py:321
  30.3 0.9 %collective-permute-start.3 = (bf16[400,128]{1,0:T(8,128)(2,1)}, bf16[400,128]{1,0:T(8,128)(2,1)S(1)}, u32[]{:S(2)}, u32[]{:S(2)}) collective-permute-start(bf16[400,128]{1,0:T(8,128)(2,1)} %get-tuple-element.13), channel_id=1, source_target_pairs={{0,1},{1,0},{2,3},{3,2},{4,5},{5,4},{6,7},{7,6},{8,9},{9,8},{10,11... | collective-permute-start | bytes 307208 | tf_op jit(solution)/shard_map/ppermute | solution.py:335
  31.1 3.3 %collective-permute-start.4 = (bf16[400,128]{1,0:T(8,128)(2,1)}, bf16[400,128]{1,0:T(8,128)(2,1)S(1)}, u32[]{:S(2)}, u32[]{:S(2)}) collective-permute-start(bf16[400,128]{1,0:T(8,128)(2,1)} %get-tuple-element.14), channel_id=1, source_target_pairs={{0,2},{1,3},{2,0},{3,1},{4,6},{5,7},{6,4},{7,5},{8,10},{9,11},{10,... | collective-permute-start | bytes 307208 | tf_op jit(solution)/shard_map/ppermute | solution.py:335
  34.4 0.2 collective-permute-start.5
  34.7 2.4 %all-to-all-done.1 = bf16[8,256,128]{2,1,0:T(8,128)(2,1)} async-done(((bf16[8,256,128]{2,1,0:T(8,128)(2,1)}), bf16[8,256,128]{2,1,0:T(8,128)(2,1)}, u32[]{:S(2)}, u32[]{:S(2)}) %all-to-all-start.1) | async-done | bytes 524320 | tf_op jit(solution)/shard_map/all_to_all | solution.py:315
  37.0 1.1 %reduce_sum.12 = bf16[256,128]{1,0:T(8,128)(2,1)S(1)} reduce(bf16[8,256,128]{2,1,0:T(8,128)(2,1)} %all-to-all-done.1, bf16[]{:T(256)} %constant.3.clone.1), dimensions={0}, to_apply=%region_0.1 | reduce | flops 229376 | bytes 589826 | tf_op jit(solution)/shard_map/reduce_sum | solution.py:336
  38.1 8.9 %all_gather.3.packed_ref = bf16[2048,128]{1,0:T(8,128)(2,1)S(1)} all-gather(bf16[256,128]{1,0:T(8,128)(2,1)S(1)} %reduce_sum.12), channel_id=1, replica_groups=mesh['rows'=8,'chan'=4] {'rows'}, dimensions={0}, use_global_device_ids=true | all-gather | bytes 589824 | tf_op jit(solution)/shard_map/all_gather | solution.py:337
  47.0 0.0 collective-permute-done.5.refs_3_
  47.0 1.2 %finish_kernel.1 = (bf16[8,48,128]{2,1,0:T(8,128)(2,1)}, f32[1296,192]{1,0:T(8,128)}) custom-call(bf16[2048,128]{1,0:T(8,128)(2,1)S(1)} %all_gather.3.packed_ref, bf16[400,128]{1,0:T(8,128)(2,1)S(1)} %copy-done, f32[400,128]{1,0:T(8,128)S(1)} %get-tuple-element.12.refs_0_, bf16[400,128]{1,0:T(8,128)(2,1)S(1)} %collective-permute-done.3.refs_1_, ...), custom_call_target="tpu_custom_call" | custom-call | tf_op jit(solution)/shard_map/finish_kernel/pallas_call | solution.py:338
  (5 shorter events, 0.0 us)
Async XLA Ops:
  2.4 18.7 %copy-start = (bf16[400,128]{1,0:T(8,128)(2,1)S(1)}, bf16[400,128]{1,0:T(8,128)(2,1)}, u32[]{:S(2)}) copy-start(bf16[400,128]{1,0:T(8,128)(2,1)} %get-tuple-element.11.refs_0_.x_ref) | copy-start | bytes 307204
  2.4 14.7 %all-to-all-start = ((bf16[8,3,48,128]{3,2,1,0:T(8,128)(2,1)}), bf16[8,3,48,128]{3,2,1,0:T(8,128)(2,1)S(1)}, u32[]{:S(2)}, u32[]{:S(2)}) async-start(bf16[8,3,48,128]{3,2,1,0:T(8,128)(2,1)} %get-tuple-element.10), calls=%async_computation | async-start | bytes 589824 | tf_op jit(solution)/shard_map/all_to_all | solution.py:286
  7.7 8.7 %collective-permute-start.1 = (bf16[400,128]{1,0:T(8,128)(2,1)}, bf16[400,128]{1,0:T(8,128)(2,1)S(1)}, u32[]{:S(2)}, u32[]{:S(2)}) collective-permute-start(bf16[400,128]{1,0:T(8,128)(2,1)} %get-tuple-element.11.refs_0_.x_ref), channel_id=1, source_target_pairs={{0,2},{1,3},{2,0},{3,1},{4,6},{5,7},{6,4},{7,5},{8,10},{9,11},{10,... | collective-permute-start | bytes 307208 | tf_op jit(solution)/shard_map/ppermute | solution.py:285
  10.3 8.4 %collective-permute-start = (bf16[400,128]{1,0:T(8,128)(2,1)}, bf16[400,128]{1,0:T(8,128)(2,1)S(1)}, u32[]{:S(2)}, u32[]{:S(2)}) collective-permute-start(bf16[400,128]{1,0:T(8,128)(2,1)} %get-tuple-element.11.refs_0_.x_ref), channel_id=1, source_target_pairs={{0,1},{1,0},{2,3},{3,2},{4,5},{5,4},{6,7},{7,6},{8,9},{9,8},{10,11... | collective-permute-start | bytes 307208 | tf_op jit(solution)/shard_map/ppermute | solution.py:285
  16.4 4.7 %collective-permute-start.2 = (bf16[400,128]{1,0:T(8,128)(2,1)S(1)}, bf16[400,128]{1,0:T(8,128)(2,1)S(1)}, u32[]{:S(2)}, u32[]{:S(2)}) collective-permute-start(bf16[400,128]{1,0:T(8,128)(2,1)S(1)} %collective-permute-done.1.refs_2_), channel_id=1, source_target_pairs={{0,1},{1,0},{2,3},{3,2},{4,5},{5,4},{6,7},{7,6},{8,9},{9,8},{10,11... | collective-permute-start | bytes 307208 | tf_op jit(solution)/shard_map/ppermute | solution.py:285
  17.0 0.7 %copy-start.2 = (s32[8]{0:T(128)S(1)}, s32[8]{0:T(128)}, u32[]{:S(2)}) copy-start(s32[8]{0:T(128)} %slot_ref.1) | copy-start | bytes 100
  23.1 13.9 %all-to-all-start.1 = ((bf16[8,256,128]{2,1,0:T(8,128)(2,1)}), bf16[8,256,128]{2,1,0:T(8,128)(2,1)}, u32[]{:S(2)}, u32[]{:S(2)}) async-start(bf16[8,256,128]{2,1,0:T(8,128)(2,1)} %bitcast.4), calls=%async_computation.1 | async-start | bytes 1048576 | tf_op jit(solution)/shard_map/all_to_all | solution.py:315
  27.3 1.1 %copy-start.1 = (bf16[27,48,192]{2,1,0:T(8,128)(2,1)S(1)}, bf16[27,48,192]{2,1,0:T(8,128)(2,1)}, u32[]{:S(2)}) copy-start(bf16[27,48,192]{2,1,0:T(8,128)(2,1)} %param.9) | copy-start | bytes 1492996
  30.3 16.8 %collective-permute-start.3 = (bf16[400,128]{1,0:T(8,128)(2,1)}, bf16[400,128]{1,0:T(8,128)(2,1)S(1)}, u32[]{:S(2)}, u32[]{:S(2)}) collective-permute-start(bf16[400,128]{1,0:T(8,128)(2,1)} %get-tuple-element.13), channel_id=1, source_target_pairs={{0,1},{1,0},{2,3},{3,2},{4,5},{5,4},{6,7},{7,6},{8,9},{9,8},{10,11... | collective-permute-start | bytes 307208 | tf_op jit(solution)/shard_map/ppermute | solution.py:335
  31.1 15.9 %collective-permute-start.4 = (bf16[400,128]{1,0:T(8,128)(2,1)}, bf16[400,128]{1,0:T(8,128)(2,1)S(1)}, u32[]{:S(2)}, u32[]{:S(2)}) collective-permute-start(bf16[400,128]{1,0:T(8,128)(2,1)} %get-tuple-element.14), channel_id=1, source_target_pairs={{0,2},{1,3},{2,0},{3,1},{4,6},{5,7},{6,4},{7,5},{8,10},{9,11},{10,... | collective-permute-start | bytes 307208 | tf_op jit(solution)/shard_map/ppermute | solution.py:335
  34.4 12.6 %collective-permute-start.5 = (bf16[400,128]{1,0:T(8,128)(2,1)S(1)}, bf16[400,128]{1,0:T(8,128)(2,1)S(1)}, u32[]{:S(2)}, u32[]{:S(2)}) collective-permute-start(bf16[400,128]{1,0:T(8,128)(2,1)S(1)} %get-tuple-element.15), channel_id=1, source_target_pairs={{0,3},{1,2},{2,1},{3,0},{4,7},{5,6},{6,5},{7,4},{8,11},{9,10},{10,... | collective-permute-start | bytes 307208 | tf_op jit(solution)/shard_map/ppermute | solution.py:335

commit v8 on v5

--- a/solution.py
+++ b/solution.py
@@ -28,6 +28,10 @@
 
 def copied():
     return pl.BlockSpec()
+
+
+def anywhere():
+    return pl.BlockSpec(memory_space=pl.ANY)
 
 
 def smem():
@@ -62,43 +66,64 @@
     return scale, [value * scale for value in values]
 
 
-def prepare_kernel(adjoint_ref, x_ref, gain_ref, strips_ref, payload_ref, lines, gain_rows):
-    channels, height, width = adjoint_ref.shape
-    frames = x_ref.shape[0]
-    group = strips_ref.shape[2]
-    lines[...] = adjoint_ref[...].astype(jnp.float32).reshape(channels * height, width)
+def prepare_kernel(
+    frames, adjoint_hbm, x_hbm, gain_hbm, strips_hbm, payload_hbm,
+    held, lines, values, gain, gain_rows, strips, payload, moved,
+):
+    channels, height, width = held.shape
+    group = strips.shape[2]
+    last = frames * group
+    direct = group == channels
+    arriving = [
+        pltpu.make_async_copy(adjoint_hbm, held, moved.at[0]),
+        pltpu.make_async_copy(
+            x_hbm, payload.at[pl.ds(0, last)] if direct else values, moved.at[1]
+        ),
+        pltpu.make_async_copy(gain_hbm, gain, moved.at[2]),
+    ]
+    for copy in arriving:
+        copy.start()
+
+    arriving[0].wait()
+    lines[...] = held[...].astype(jnp.float32).reshape(channels * height, width)
     nothing = jnp.zeros((group, width), jnp.bfloat16)
-    strips_ref[0, 0] = nothing
-    strips_ref[height - 1, 2] = nothing
+    strips[0, 0] = nothing
+    strips[height - 1, 2] = nothing
     for r in range(height):
         row = lines[pl.ds(r, channels, stride=height), :]
-        if group > channels:
+        if not direct:
             row = jnp.concatenate(
                 [row, jnp.zeros((group - channels, width), jnp.float32)], axis=0
             )
         row = row.astype(jnp.bfloat16)
         for k in range(3):
             if 0 <= r + 1 - k < height:
-                strips_ref[r + 1 - k, k] = row
-    for t in range(frames):
-        values = x_ref[t]
-        if group > channels:
-            values = jnp.concatenate(
+                strips[r + 1 - k, k] = row
+    leaving = [pltpu.make_async_copy(strips, strips_hbm, moved.at[3])]
+    leaving[0].start()
+
+    arriving[1].wait()
+    arriving[2].wait()
+    if not direct:
+        for t in range(frames):
+            payload[pl.ds(t * group, group), :] = jnp.concatenate(
                 [
-                    values.astype(jnp.float32),
+                    values[t].astype(jnp.float32),
                     jnp.zeros((group - channels, width), jnp.float32),
                 ],
                 axis=0,
             ).astype(jnp.bfloat16)
-        payload_ref[pl.ds(t * group, group), :] = values
-    gain = gain_ref[...]
-    high = gain.astype(jnp.bfloat16).astype(jnp.float32)
-    middle = (gain - high).astype(jnp.bfloat16).astype(jnp.float32)
+    high = gain[...].astype(jnp.bfloat16).astype(jnp.float32)
+    middle = (gain[...] - high).astype(jnp.bfloat16).astype(jnp.float32)
     gain_rows[...] = jnp.zeros_like(gain_rows)
     gain_rows[pl.ds(0, 1), pl.ds(0, channels)] = high
     gain_rows[pl.ds(1, 1), pl.ds(0, channels)] = middle
-    gain_rows[pl.ds(2, 1), pl.ds(0, channels)] = gain - high - middle
-    payload_ref[pl.ds(frames * group, 16), :] = gain_rows[...].astype(jnp.bfloat16)
+    gain_rows[pl.ds(2, 1), pl.ds(0, channels)] = gain[...] - high - middle
+    payload[pl.ds(last, 16), :] = gain_rows[...].astype(jnp.bfloat16)
+    leaving.append(pltpu.make_async_copy(payload, payload_hbm, moved.at[4]))
+    leaving[1].start()
+    for copy in leaving:
+        copy.wait()
 
 
 def window_kernel(frames, group, slot_ref, adjoint_ref, windows, place):
@@ -243,25 +268,35 @@
 
     taps_out = 27 * group
     pixels = frames * width
+    sent = inputs[:, :, 0] if spare else inputs.reshape(frames * channels, width)
     strips, payload = pl.pallas_call(
-        prepare_kernel,
+        functools.partial(prepare_kernel, frames),
         out_shape=(
             jax.ShapeDtypeStruct((count, 3, group, width), jnp.bfloat16),
             jax.ShapeDtypeStruct((frames * group + 16, width), jnp.bfloat16),
         ),
-        in_specs=[copied(), copied(), copied()],
-        out_specs=(vmem(), vmem()),
+        in_specs=[anywhere(), anywhere(), anywhere()],
+        out_specs=(anywhere(), anywhere()),
         scratch_shapes=[
+            pltpu.VMEM((channels, count, width), jnp.bfloat16),
             pltpu.VMEM((channels * count, width), jnp.float32),
+            pltpu.VMEM(sent.shape if spare else (16, width), jnp.bfloat16),
+            pltpu.VMEM((1, channels), jnp.float32),
             pltpu.VMEM((16, width), jnp.float32),
+            pltpu.VMEM((count, 3, group, width), jnp.bfloat16),
+            pltpu.VMEM((frames * group + 16, width), jnp.bfloat16),
+            pltpu.SemaphoreType.DMA((5,)),
         ],
         compiler_params=pltpu.CompilerParams(vmem_limit_bytes=60 * MIB),
         name="prepare_kernel",
-    )(frame_adjoint[0], inputs[:, :, 0], gain.reshape(1, channels))
+    )(frame_adjoint[0], sent, gain.reshape(1, channels))
+
     partners = [[(z, z ^ s) for z in range(groups)] for s in range(groups)]
     everything = [payload] * groups
     for s in range(1, groups):
         everything[s] = lax.ppermute(everything[s & (s - 1)], "chan", partners[s & -s])
+    gate = min(2, groups - 1)
+    strips, everything[gate] = lax.optimization_barrier((strips, everything[gate]))
     strips = lax.all_to_all(strips, "rows", split_axis=0, concat_axis=0, tiled=True)
     at = lax.axis_index("chan").astype(jnp.int32).reshape(1)
 
@@ -296,12 +331,12 @@
         "rows", split_axis=0, concat_axis=0, tiled=True,
     )
 
-    sent = frames * group + round_up(2 * frames, 16)
+    part_rows = frames * group + round_up(2 * frames, 16)
     parts = pl.pallas_call(
         functools.partial(part_kernel, frames, group),
         out_shape=tuple(
             [jax.ShapeDtypeStruct((frames * (group + 2), width), jnp.float32)]
-            + [jax.ShapeDtypeStruct((sent, width), jnp.bfloat16)] * (groups - 1)
+            + [jax.ShapeDtypeStruct((part_rows, width), jnp.bfloat16)] * (groups - 1)
         ),
         in_specs=[smem(), vmem(), vmem()] + [copied()] * groups,
         out_specs=(vmem(),) * groups,

time: 48.7 us -> 52.1 us (1.070)
  waiting for transfers between devices: 9.28 us -> 12.9 us
    all_to_all x1, waiting for transfers between devices: 0.01 us -> 5.26 us  [shards(): lax.all_to_all(strips, 'rows', split_axis=0, concat_axis=0, tiled=True)]
    ppermute x3, waiting for transfers between devices: 6.92 us -> 5.29 us  [shards(): lax.ppermute(everything[s & s - 1], 'chan', partners[s & -s])]
    all_to_all x1, starting transfers between devices: 5.3 us -> 3.77 us  [shards(): lax.all_to_all(strips, 'rows', split_axis=0, concat_axis=0, tiled=True)]
    ppermute x3, starting transfers between devices: 4.84 us -> 6.13 us  [shards(): lax.ppermute(everything[s & s - 1], 'chan', partners[s & -s])]
  transfers between devices with their start and end apart: 8 -> 8, of which waited for: 3 -> 3; matrix products, arithmetic and copies ran while one was open for 2% -> 2% of each run, Pallas kernels for 6% -> 5%
where the time goes in v8:
time: 52.1 us; the launch traced here: 51.7 us
  starting transfers between devices  18.5 us (36%)
  waiting for transfers between devices  12.9 us (25%)
  blocking collectives  8.9 us (17%)
  Pallas kernels  7.83 us (15%)
  local copies, waits for them, and re-layouts  1.74 us (3%)
  other arithmetic  1.12 us (2%)
  between operations  0.71 us (1%)
    all_gather x1, blocking collectives, shards(): whole = lax.all_gather(summed, 'rows', axis=0, tiled=True)  8.9 us
    ppermute x3, starting transfers between devices, shards(): lax.ppermute(everything[s & s - 1], 'chan', partners[s & -s])  6.13 us
    ppermute x3, waiting for transfers between devices, shards(): lax.ppermute(everything[s & s - 1], 'chan', partners[s & -s])  5.29 us
    all_to_all x1, waiting for transfers between devices, shards(): lax.all_to_all(strips, 'rows', split_axis=0, concat_axis=0, tiled=True)  5.26 us
    ppermute x3, starting transfers between devices, shards(): lax.ppermute(parts[s], 'chan', partners[s])  4.4 us
    all_to_all x1, starting transfers between devices, shards(): lax.all_to_all(packed.reshape(count, packed_rows // count, 128), 'rows',...  4.15 us
    all_to_all x1, starting transfers between devices, shards(): lax.all_to_all(strips, 'rows', split_axis=0, concat_axis=0, tiled=True)  3.77 us
    all_to_all x1, waiting for transfers between devices, shards(): lax.all_to_all(packed.reshape(count, packed_rows // count, 128), 'rows',...  2.37 us
  transfers between devices with their start and end apart: 8, of which 3 were waited for; matrix products, arithmetic and copies ran while one was open for 2% of the time, Pallas kernels for 5%

profile of v8, /device:TPU:0, one launch (start us, length us, event | category | flops | bytes accessed | tf_op | source)
XLA Modules:
  0.0 51.7 jit_solution(13968518056115184637)
XLA Ops:
  0.6 1.7 %prepare_kernel.1 = (bf16[8,3,48,128]{3,2,1,0:T(8,128)(2,1)}, bf16[400,128]{1,0:T(8,128)(2,1)}) custom-call(bf16[48,8,128]{2,1,0:T(8,128)(2,1)} %bitcast.11, bf16[384,128]{1,0:T(8,128)(2,1)} %bitcast.12, f32[1,48]{1,0:T(1,128)} %bitcast.13), custom_call_target="tpu_custom_call" | custom-call | tf_op jit(solution)/shard_map/prepare_kernel/pallas_call | solution.py:272
  2.4 4.1 %collective-permute-start = (bf16[400,128]{1,0:T(8,128)(2,1)}, bf16[400,128]{1,0:T(8,128)(2,1)S(1)}, u32[]{:S(2)}, u32[]{:S(2)}) collective-permute-start(bf16[400,128]{1,0:T(8,128)(2,1)} %get-tuple-element.13.refs_0_.x_ref), channel_id=1, source_target_pairs={{0,2},{1,3},{2,0},{3,1},{4,6},{5,7},{6,4},{7,5},{8,10},{9,11},{10,... | collective-permute-start | bytes 307208 | tf_op jit(solution)/shard_map/ppermute | solution.py:297
  6.5 5.3 %collective-permute-done.refs_2_ = bf16[400,128]{1,0:T(8,128)(2,1)S(1)} collective-permute-done((bf16[400,128]{1,0:T(8,128)(2,1)}, bf16[400,128]{1,0:T(8,128)(2,1)S(1)}, u32[]{:S(2)}, u32[]{:S(2)}) %collective-permute-start) | collective-permute-done | bytes 102432 | tf_op jit(solution)/shard_map/ppermute | solution.py:297
  11.8 3.8 %all-to-all-start = ((bf16[8,3,48,128]{3,2,1,0:T(8,128)(2,1)}), bf16[8,3,48,128]{3,2,1,0:T(8,128)(2,1)S(1)}, u32[]{:S(2)}, u32[]{:S(2)}) async-start(bf16[8,3,48,128]{3,2,1,0:T(8,128)(2,1)} %get-tuple-element.14), calls=%async_computation | async-start | bytes 589824 | tf_op jit(solution)/shard_map/all_to_all | solution.py:300
  15.5 0.8 %collective-permute-start.1 = (bf16[400,128]{1,0:T(8,128)(2,1)}, bf16[400,128]{1,0:T(8,128)(2,1)S(1)}, u32[]{:S(2)}, u32[]{:S(2)}) collective-permute-start(bf16[400,128]{1,0:T(8,128)(2,1)} %get-tuple-element.13.refs_0_.x_ref), channel_id=1, source_target_pairs={{0,1},{1,0},{2,3},{3,2},{4,5},{5,4},{6,7},{7,6},{8,9},{9,8},{10,11... | collective-permute-start | bytes 307208 | tf_op jit(solution)/shard_map/ppermute | solution.py:297
  16.3 1.2 %collective-permute-start.2 = (bf16[400,128]{1,0:T(8,128)(2,1)S(1)}, bf16[400,128]{1,0:T(8,128)(2,1)S(1)}, u32[]{:S(2)}, u32[]{:S(2)}) collective-permute-start(bf16[400,128]{1,0:T(8,128)(2,1)S(1)} %collective-permute-done.refs_2_), channel_id=1, source_target_pairs={{0,1},{1,0},{2,3},{3,2},{4,5},{5,4},{6,7},{7,6},{8,9},{9,8},{10,11... | collective-permute-start | bytes 307208 | tf_op jit(solution)/shard_map/ppermute | solution.py:297
  17.6 5.3 %all-to-all-done.adjoint_ref = bf16[8,3,48,128]{3,2,1,0:T(8,128)(2,1)S(1)} async-done(((bf16[8,3,48,128]{3,2,1,0:T(8,128)(2,1)}), bf16[8,3,48,128]{3,2,1,0:T(8,128)(2,1)S(1)}, u32[]{:S(2)}, u32[]{:S(2)}) %all-to-all-start) | async-done | bytes 294944 | tf_op jit(solution)/shard_map/all_to_all | solution.py:300
  22.8 0.7 %copy-done.2 = s32[8]{0:T(128)S(1)} copy-done((s32[8]{0:T(128)S(1)}, s32[8]{0:T(128)}, u32[]{:S(2)}) %copy-start.2) | copy-done | bytes 56
  23.5 0.9 %window_kernel.1.windows = bf16[1296,1024]{1,0:T(8,128)(2,1)S(1)} custom-call(s32[8]{0:T(128)S(1)} %copy-done.2, bf16[8,3,48,128]{3,2,1,0:T(8,128)(2,1)S(1)} %all-to-all-done.adjoint_ref), custom_call_target="tpu_custom_call" | custom-call | tf_op jit(solution)/shard_map/window_kernel/pallas_call | solution.py:309
  24.4 0.0 collective-permute-done.1.refs_1_
  24.4 0.0 collective-permute-done.2.refs_3_
  24.4 2.1 %grad_kernel.1 = bf16[2048,128]{1,0:T(8,128)(2,1)} custom-call(s32[1]{0:T(128)} %bitcast.at_ref, bf16[1296,1024]{1,0:T(8,128)(2,1)S(1)} %window_kernel.1.windows, bf16[400,128]{1,0:T(8,128)(2,1)S(1)} %copy-done, bf16[400,128]{1,0:T(8,128)(2,1)S(1)} %collective-permute-done.1.refs_1_, bf16[400,128]{1,0:T(8,128)(2,1)S(1)} %collective-permute-done.refs_2_, ...), custom_call_target="tpu_custom_call" | custom-call | flops 509607936 | bytes 3047424 | tf_op jit(solution)/shard_map/grad_kernel/pallas_call | solution.py:318
  26.5 4.1 %all-to-all-start.1 = ((bf16[8,256,128]{2,1,0:T(8,128)(2,1)}), bf16[8,256,128]{2,1,0:T(8,128)(2,1)}, u32[]{:S(2)}, u32[]{:S(2)}) async-start(bf16[8,256,128]{2,1,0:T(8,128)(2,1)} %bitcast.4), calls=%async_computation.1 | async-start | bytes 1048576 | tf_op jit(solution)/shard_map/all_to_all | solution.py:329
  30.7 0.0 copy-start.1
  30.7 1.1 %copy-done.1 = bf16[27,48,192]{2,1,0:T(8,128)(2,1)S(1)} copy-done((bf16[27,48,192]{2,1,0:T(8,128)(2,1)S(1)}, bf16[27,48,192]{2,1,0:T(8,128)(2,1)}, u32[]{:S(2)}) %copy-start.1) | copy-done | bytes 497688
  31.8 1.9 %part_kernel.1 = (f32[400,128]{1,0:T(8,128)S(1)}, bf16[400,128]{1,0:T(8,128)(2,1)}, bf16[400,128]{1,0:T(8,128)(2,1)}, bf16[400,128]{1,0:T(8,128)(2,1)S(1)}) custom-call(s32[1]{0:T(128)} %bitcast.at_ref, bf16[1296,192]{1,0:T(8,128)(2,1)S(1)} %bitcast.10, bf16[1296,1024]{1,0:T(8,128)(2,1)S(1)} %window_kernel.1.windows, bf16[400,128]{1,0:T(8,128)(2,1)S(1)} %copy-done, ...), custom_call_target="tpu_custom_call" | custom-call | flops 509607936 | bytes 3047424 | tf_op jit(solution)/shard_map/part_kernel/pallas_call | solution.py:335
  33.6 0.8 %collective-permute-start.3 = (bf16[400,128]{1,0:T(8,128)(2,1)}, bf16[400,128]{1,0:T(8,128)(2,1)S(1)}, u32[]{:S(2)}, u32[]{:S(2)}) collective-permute-start(bf16[400,128]{1,0:T(8,128)(2,1)} %get-tuple-element.17), channel_id=1, source_target_pairs={{0,1},{1,0},{2,3},{3,2},{4,5},{5,4},{6,7},{7,6},{8,9},{9,8},{10,11... | collective-permute-start | bytes 307208 | tf_op jit(solution)/shard_map/ppermute | solution.py:349
  34.4 3.3 %collective-permute-start.4 = (bf16[400,128]{1,0:T(8,128)(2,1)}, bf16[400,128]{1,0:T(8,128)(2,1)S(1)}, u32[]{:S(2)}, u32[]{:S(2)}) collective-permute-start(bf16[400,128]{1,0:T(8,128)(2,1)} %get-tuple-element.18), channel_id=1, source_target_pairs={{0,2},{1,3},{2,0},{3,1},{4,6},{5,7},{6,4},{7,5},{8,10},{9,11},{10,... | collective-permute-start | bytes 307208 | tf_op jit(solution)/shard_map/ppermute | solution.py:349
  37.7 0.3 collective-permute-start.5
  38.0 2.4 %all-to-all-done.1 = bf16[8,256,128]{2,1,0:T(8,128)(2,1)} async-done(((bf16[8,256,128]{2,1,0:T(8,128)(2,1)}), bf16[8,256,128]{2,1,0:T(8,128)(2,1)}, u32[]{:S(2)}, u32[]{:S(2)}) %all-to-all-start.1) | async-done | bytes 524320 | tf_op jit(solution)/shard_map/all_to_all | solution.py:329
  40.4 1.1 %reduce_sum.12 = bf16[256,128]{1,0:T(8,128)(2,1)S(1)} reduce(bf16[8,256,128]{2,1,0:T(8,128)(2,1)} %all-to-all-done.1, bf16[]{:T(256)} %constant.3.clone.1), dimensions={0}, to_apply=%region_0.1 | reduce | flops 229376 | bytes 589826 | tf_op jit(solution)/shard_map/reduce_sum | solution.py:350
  41.5 8.9 %all_gather.3.packed_ref = bf16[2048,128]{1,0:T(8,128)(2,1)S(1)} all-gather(bf16[256,128]{1,0:T(8,128)(2,1)S(1)} %reduce_sum.12), channel_id=1, replica_groups=mesh['rows'=8,'chan'=4] {'rows'}, dimensions={0}, use_global_device_ids=true | all-gather | bytes 589824 | tf_op jit(solution)/shard_map/all_gather | solution.py:351
  50.4 0.0 collective-permute-done.3.refs_1_
  50.4 1.2 %finish_kernel.1 = (bf16[8,48,128]{2,1,0:T(8,128)(2,1)}, f32[1296,192]{1,0:T(8,128)}) custom-call(bf16[2048,128]{1,0:T(8,128)(2,1)S(1)} %all_gather.3.packed_ref, bf16[400,128]{1,0:T(8,128)(2,1)S(1)} %copy-done, f32[400,128]{1,0:T(8,128)S(1)} %get-tuple-element.16.refs_0_, bf16[400,128]{1,0:T(8,128)(2,1)S(1)} %collective-permute-done.3.refs_1_, ...), custom_call_target="tpu_custom_call" | custom-call | tf_op jit(solution)/shard_map/finish_kernel/pallas_call | solution.py:352
  (5 shorter events, 0.0 us)
Async XLA Ops:
  2.4 22.1 %copy-start = (bf16[400,128]{1,0:T(8,128)(2,1)S(1)}, bf16[400,128]{1,0:T(8,128)(2,1)}, u32[]{:S(2)}) copy-start(bf16[400,128]{1,0:T(8,128)(2,1)} %get-tuple-element.13.refs_0_.x_ref) | copy-start | bytes 307204
  2.4 9.4 %collective-permute-start = (bf16[400,128]{1,0:T(8,128)(2,1)}, bf16[400,128]{1,0:T(8,128)(2,1)S(1)}, u32[]{:S(2)}, u32[]{:S(2)}) collective-permute-start(bf16[400,128]{1,0:T(8,128)(2,1)} %get-tuple-element.13.refs_0_.x_ref), channel_id=1, source_target_pairs={{0,2},{1,3},{2,0},{3,1},{4,6},{5,7},{6,4},{7,5},{8,10},{9,11},{10,... | collective-permute-start | bytes 307208 | tf_op jit(solution)/shard_map/ppermute | solution.py:297
  11.8 11.1 %all-to-all-start = ((bf16[8,3,48,128]{3,2,1,0:T(8,128)(2,1)}), bf16[8,3,48,128]{3,2,1,0:T(8,128)(2,1)S(1)}, u32[]{:S(2)}, u32[]{:S(2)}) async-start(bf16[8,3,48,128]{3,2,1,0:T(8,128)(2,1)} %get-tuple-element.14), calls=%async_computation | async-start | bytes 589824 | tf_op jit(solution)/shard_map/all_to_all | solution.py:300
  15.5 8.9 %collective-permute-start.1 = (bf16[400,128]{1,0:T(8,128)(2,1)}, bf16[400,128]{1,0:T(8,128)(2,1)S(1)}, u32[]{:S(2)}, u32[]{:S(2)}) collective-permute-start(bf16[400,128]{1,0:T(8,128)(2,1)} %get-tuple-element.13.refs_0_.x_ref), channel_id=1, source_target_pairs={{0,1},{1,0},{2,3},{3,2},{4,5},{5,4},{6,7},{7,6},{8,9},{9,8},{10,11... | collective-permute-start | bytes 307208 | tf_op jit(solution)/shard_map/ppermute | solution.py:297
  16.3 8.1 %collective-permute-start.2 = (bf16[400,128]{1,0:T(8,128)(2,1)S(1)}, bf16[400,128]{1,0:T(8,128)(2,1)S(1)}, u32[]{:S(2)}, u32[]{:S(2)}) collective-permute-start(bf16[400,128]{1,0:T(8,128)(2,1)S(1)} %collective-permute-done.refs_2_), channel_id=1, source_target_pairs={{0,1},{1,0},{2,3},{3,2},{4,5},{5,4},{6,7},{7,6},{8,9},{9,8},{10,11... | collective-permute-start | bytes 307208 | tf_op jit(solution)/shard_map/ppermute | solution.py:297
  22.8 0.7 %copy-start.2 = (s32[8]{0:T(128)S(1)}, s32[8]{0:T(128)}, u32[]{:S(2)}) copy-start(s32[8]{0:T(128)} %slot_ref.1) | copy-start | bytes 100
  26.5 13.9 %all-to-all-start.1 = ((bf16[8,256,128]{2,1,0:T(8,128)(2,1)}), bf16[8,256,128]{2,1,0:T(8,128)(2,1)}, u32[]{:S(2)}, u32[]{:S(2)}) async-start(bf16[8,256,128]{2,1,0:T(8,128)(2,1)} %bitcast.4), calls=%async_computation.1 | async-start | bytes 1048576 | tf_op jit(solution)/shard_map/all_to_all | solution.py:329
  30.7 1.1 %copy-start.1 = (bf16[27,48,192]{2,1,0:T(8,128)(2,1)S(1)}, bf16[27,48,192]{2,1,0:T(8,128)(2,1)}, u32[]{:S(2)}) copy-start(bf16[27,48,192]{2,1,0:T(8,128)(2,1)} %param.9) | copy-start | bytes 1492996
  33.6 16.8 %collective-permute-start.3 = (bf16[400,128]{1,0:T(8,128)(2,1)}, bf16[400,128]{1,0:T(8,128)(2,1)S(1)}, u32[]{:S(2)}, u32[]{:S(2)}) collective-permute-start(bf16[400,128]{1,0:T(8,128)(2,1)} %get-tuple-element.17), channel_id=1, source_target_pairs={{0,1},{1,0},{2,3},{3,2},{4,5},{5,4},{6,7},{7,6},{8,9},{9,8},{10,11... | collective-permute-start | bytes 307208 | tf_op jit(solution)/shard_map/ppermute | solution.py:349
  34.4 16.0 %collective-permute-start.4 = (bf16[400,128]{1,0:T(8,128)(2,1)}, bf16[400,128]{1,0:T(8,128)(2,1)S(1)}, u32[]{:S(2)}, u32[]{:S(2)}) collective-permute-start(bf16[400,128]{1,0:T(8,128)(2,1)} %get-tuple-element.18), channel_id=1, source_target_pairs={{0,2},{1,3},{2,0},{3,1},{4,6},{5,7},{6,4},{7,5},{8,10},{9,11},{10,... | collective-permute-start | bytes 307208 | tf_op jit(solution)/shard_map/ppermute | solution.py:349
  37.7 12.7 %collective-permute-start.5 = (bf16[400,128]{1,0:T(8,128)(2,1)S(1)}, bf16[400,128]{1,0:T(8,128)(2,1)S(1)}, u32[]{:S(2)}, u32[]{:S(2)}) collective-permute-start(bf16[400,128]{1,0:T(8,128)(2,1)S(1)} %get-tuple-element.19), channel_id=1, source_target_pairs={{0,3},{1,2},{2,1},{3,0},{4,7},{5,6},{6,5},{7,4},{8,11},{9,10},{10,... | collective-permute-start | bytes 307208 | tf_op jit(solution)/shard_map/ppermute | solution.py:349

commit v9 on v5

--- a/solution.py
+++ b/solution.py
@@ -259,10 +259,15 @@
         name="prepare_kernel",
     )(frame_adjoint[0], inputs[:, :, 0], gain.reshape(1, channels))
     partners = [[(z, z ^ s) for z in range(groups)] for s in range(groups)]
-    everything = [payload] * groups
-    for s in range(1, groups):
-        everything[s] = lax.ppermute(everything[s & (s - 1)], "chan", partners[s & -s])
-    strips = lax.all_to_all(strips, "rows", split_axis=0, concat_axis=0, tiled=True)
+    everything = [payload] + [
+        lax.ppermute(payload, "chan", partners[s]) for s in range(1, groups)
+    ]
+    strips = lax.cond(
+        lax.axis_index("rows") < count,
+        lambda rows: lax.all_to_all(rows, "rows", split_axis=0, concat_axis=0, tiled=True),
+        lambda rows: rows,
+        strips,
+    )
     at = lax.axis_index("chan").astype(jnp.int32).reshape(1)
 
     kernel = weight.reshape(27, channels, groups, channels)

time: 48.7 us -> 50.2 us (1.031)
  blocking collectives: 8.9 us -> 19.9 us
  waiting for transfers between devices: 9.28 us -> 1.81 us
  starting transfers between devices: 18.7 us -> 14.2 us
  Pallas kernels: 7.86 us -> 9.73 us
  local copies, waits for them, and re-layouts: 1.74 us -> 2.29 us
    all_to_all x0 -> x1, blocking collectives: none -> 11 us  [shards(): lax.all_to_all(rows, 'rows', split_axis=0, concat_axis=0, tiled=True)]
    ppermute x3, waiting for transfers between devices: 6.92 us -> 0.01 us  [shards(): lax.ppermute(payload, 'chan', partners[s])]
    all_to_all x1 -> x0, starting transfers between devices: 5.3 us -> none  [shards(): lax.all_to_all(strips, 'rows', split_axis=0, concat_axis=0, tiled=True)]
    pallas_call x1, Pallas kernels: 2.07 us -> 3.06 us  [shards(): pl.pallas_call(functools.partial(grad_kernel, frames, group, factor), out...]
    pallas_call x1, Pallas kernels: 1.91 us -> 2.86 us  [shards(): pl.pallas_call(functools.partial(part_kernel, frames, group), out_shape=t...]
    ppermute x3, starting transfers between devices: 4.84 us -> 5.62 us  [shards(): lax.ppermute(payload, 'chan', partners[s])]
    all_to_all x1, waiting for transfers between devices: 2.35 us -> 1.8 us  [shards(): lax.all_to_all(packed.reshape(count, packed_rows // count, 128), 'rows',...]
    unnamed x6 -> x10, local copies, waits for them, and re-layouts: 1.74 us -> 2.27 us
  transfers between devices with their start and end apart: 8 -> 7, of which waited for: 3 -> 1; matrix products, arithmetic and copies ran while one was open for 2% -> 2% of each run, Pallas kernels for 6% -> 8%
where the time goes in v9:
time: 50.2 us; the launch traced here: 49.8 us
  blocking collectives  19.9 us (40%)
  starting transfers between devices  14.2 us (28%)
  Pallas kernels  9.73 us (19%)
  local copies, waits for them, and re-layouts  2.29 us (5%)
  waiting for transfers between devices  1.81 us (4%)
  other arithmetic  1.12 us (2%)
  between operations  0.72 us (1%)
    all_to_all x1, blocking collectives, shards(): lax.all_to_all(rows, 'rows', split_axis=0, concat_axis=0, tiled=True)  11 us
    all_gather x1, blocking collectives, shards(): whole = lax.all_gather(summed, 'rows', axis=0, tiled=True)  8.9 us
    ppermute x3, starting transfers between devices, shards(): lax.ppermute(payload, 'chan', partners[s])  5.62 us
    ppermute x3, starting transfers between devices, shards(): lax.ppermute(parts[s], 'chan', partners[s])  4.4 us
    all_to_all x1, starting transfers between devices, shards(): lax.all_to_all(packed.reshape(count, packed_rows // count, 128), 'rows',...  4.14 us
    pallas_call x1, Pallas kernels, shards(): pl.pallas_call(functools.partial(grad_kernel, frames, group, factor), out...  3.06 us
    pallas_call x1, Pallas kernels, shards(): pl.pallas_call(functools.partial(part_kernel, frames, group), out_shape=t...  2.86 us
    unnamed x10, local copies, waits for them, and re-layouts  2.27 us
  transfers between devices with their start and end apart: 7, of which 1 were waited for; matrix products, arithmetic and copies ran while one was open for 2% of the time, Pallas kernels for 8%

profile of v9, /device:TPU:0, one launch (start us, length us, event | category | flops | bytes accessed | tf_op | source)
XLA Modules:
  0.0 49.8 jit_solution(10033530005031037201)
XLA Ops:
  0.6 1.7 %prepare_kernel.1 = (bf16[8,3,48,128]{3,2,1,0:T(8,128)(2,1)S(1)}, bf16[400,128]{1,0:T(8,128)(2,1)}) custom-call(bf16[48,8,128]{2,1,0:T(8,128)(2,1)} %bitcast.11, bf16[8,48,128]{2,1,0:T(8,128)(2,1)} %bitcast.12, f32[1,48]{1,0:T(1,128)} %bitcast.13), custom_call_target="tpu_custom_call" | custom-call | tf_op jit(solution)/shard_map/prepare_kernel/pallas_call | solution.py:246
  2.3 3.0 %collective-permute-start = (bf16[400,128]{1,0:T(8,128)(2,1)}, bf16[400,128]{1,0:T(8,128)(2,1)S(1)}, u32[]{:S(2)}, u32[]{:S(2)}) collective-permute-start(bf16[400,128]{1,0:T(8,128)(2,1)} %get-tuple-element.16.refs_0_.x_ref), channel_id=1, source_target_pairs={{0,1},{1,0},{2,3},{3,2},{4,5},{5,4},{6,7},{7,6},{8,9},{9,8},{10,11... | collective-permute-start | bytes 307208 | tf_op jit(solution)/shard_map/ppermute | solution.py:263
  5.3 2.6 %collective-permute-start.1 = (bf16[400,128]{1,0:T(8,128)(2,1)}, bf16[400,128]{1,0:T(8,128)(2,1)}, u32[]{:S(2)}, u32[]{:S(2)}) collective-permute-start(bf16[400,128]{1,0:T(8,128)(2,1)} %get-tuple-element.16.refs_0_.x_ref), channel_id=1, source_target_pairs={{0,2},{1,3},{2,0},{3,1},{4,6},{5,7},{6,4},{7,5},{8,10},{9,11},{10,... | collective-permute-start | bytes 307208 | tf_op jit(solution)/shard_map/ppermute | solution.py:263
  7.9 0.0 collective-permute-start.2
  7.9 11.1 %conditional.1 = (bf16[8,3,48,128]{3,2,1,0:T(8,128)(2,1)S(1)}) conditional(s32[]{:T(128)} %convert_element_type.2, bf16[8,3,48,128]{3,2,1,0:T(8,128)(2,1)S(1)} %get-tuple-element.15, bf16[8,3,48,128]{3,2,1,0:T(8,128)(2,1)S(1)} %get-tuple-element.15), branch_computations={%region_0.0_spmd, %region_1.0_spmd} | conditional | bytes 1179656 | solution.py:265
  7.9 11.0 %all_to_all.9 = bf16[8,3,48,128]{3,2,1,0:T(8,128)(2,1)S(1)} all-to-all(bf16[8,3,48,128]{3,2,1,0:T(8,128)(2,1)S(1)} %copy.10), channel_id=1, replica_groups=mesh['rows'=8,'chan'=4] {'rows'}, dimensions={0} | all-to-all | bytes 589824 | tf_op jit(solution)/shard_map/cond/branch_1_fun/all_to_all | solution.py:267
  19.0 0.7 %copy-done.4 = s32[8]{0:T(128)S(1)} copy-done((s32[8]{0:T(128)S(1)}, s32[8]{0:T(128)}, u32[]{:S(2)}) %copy-start.4) | copy-done | bytes 56
  19.6 0.9 %window_kernel.1.windows = bf16[1296,1024]{1,0:T(8,128)(2,1)S(1)} custom-call(s32[8]{0:T(128)S(1)} %copy-done.4, bf16[8,3,48,128]{3,2,1,0:T(8,128)(2,1)S(1)} %get-tuple-element.25.adjoint_ref), custom_call_target="tpu_custom_call" | custom-call | tf_op jit(solution)/shard_map/window_kernel/pallas_call | solution.py:279
  20.5 0.0 copy-start.1
  20.6 0.0 collective-permute-done.refs_1_
  20.6 0.0 collective-permute-done.2.refs_3_
  20.6 3.1 %grad_kernel.1 = bf16[2048,128]{1,0:T(8,128)(2,1)} custom-call(s32[1]{0:T(128)} %bitcast.at_ref, bf16[1296,1024]{1,0:T(8,128)(2,1)S(1)} %window_kernel.1.windows, bf16[400,128]{1,0:T(8,128)(2,1)S(1)} %copy-done, bf16[400,128]{1,0:T(8,128)(2,1)S(1)} %collective-permute-done.refs_1_, bf16[400,128]{1,0:T(8,128)(2,1)} %collective-permute-done.1.refs_2_, ...), custom_call_target="tpu_custom_call" | custom-call | flops 509607936 | bytes 3047424 | tf_op jit(solution)/shard_map/grad_kernel/pallas_call | solution.py:288
  23.7 4.1 %all-to-all-start.1 = ((bf16[8,256,128]{2,1,0:T(8,128)(2,1)}), bf16[8,256,128]{2,1,0:T(8,128)(2,1)}, u32[]{:S(2)}, u32[]{:S(2)}) async-start(bf16[8,256,128]{2,1,0:T(8,128)(2,1)} %bitcast.4), calls=%async_computation.1 | async-start | bytes 1048576 | tf_op jit(solution)/shard_map/all_to_all | solution.py:299
  27.8 2.9 %part_kernel.1 = (f32[400,128]{1,0:T(8,128)S(1)}, bf16[400,128]{1,0:T(8,128)(2,1)}, bf16[400,128]{1,0:T(8,128)(2,1)}, bf16[400,128]{1,0:T(8,128)(2,1)}) custom-call(s32[1]{0:T(128)} %bitcast.at_ref, bf16[1296,192]{1,0:T(8,128)(2,1)S(1)} %bitcast.10, bf16[1296,1024]{1,0:T(8,128)(2,1)S(1)} %window_kernel.1.windows, bf16[400,128]{1,0:T(8,128)(2,1)S(1)} %copy-done, ...), custom_call_target="tpu_custom_call" | custom-call | flops 509607936 | bytes 3047424 | tf_op jit(solution)/shard_map/part_kernel/pallas_call | solution.py:305
  30.7 0.7 %copy-done.2 = f32[400,128]{1,0:T(8,128)} copy-done((f32[400,128]{1,0:T(8,128)}, f32[400,128]{1,0:T(8,128)S(1)}, u32[]{:S(2)}) %copy-start.2) | copy-done | bytes 204824
  31.4 0.7 %collective-permute-start.3 = (bf16[400,128]{1,0:T(8,128)(2,1)}, bf16[400,128]{1,0:T(8,128)(2,1)S(1)}, u32[]{:S(2)}, u32[]{:S(2)}) collective-permute-start(bf16[400,128]{1,0:T(8,128)(2,1)} %get-tuple-element.18), channel_id=1, source_target_pairs={{0,1},{1,0},{2,3},{3,2},{4,5},{5,4},{6,7},{7,6},{8,9},{9,8},{10,11... | collective-permute-start | bytes 307208 | tf_op jit(solution)/shard_map/ppermute | solution.py:319
  32.1 3.5 %collective-permute-start.4 = (bf16[400,128]{1,0:T(8,128)(2,1)}, bf16[400,128]{1,0:T(8,128)(2,1)S(1)}, u32[]{:S(2)}, u32[]{:S(2)}) collective-permute-start(bf16[400,128]{1,0:T(8,128)(2,1)} %get-tuple-element.19), channel_id=1, source_target_pairs={{0,2},{1,3},{2,0},{3,1},{4,6},{5,7},{6,4},{7,5},{8,10},{9,11},{10,... | collective-permute-start | bytes 307208 | tf_op jit(solution)/shard_map/ppermute | solution.py:319
  35.5 0.2 collective-permute-start.5
  35.8 1.8 %all-to-all-done.1 = bf16[8,256,128]{2,1,0:T(8,128)(2,1)} async-done(((bf16[8,256,128]{2,1,0:T(8,128)(2,1)}), bf16[8,256,128]{2,1,0:T(8,128)(2,1)}, u32[]{:S(2)}, u32[]{:S(2)}) %all-to-all-start.1) | async-done | bytes 524320 | tf_op jit(solution)/shard_map/all_to_all | solution.py:299
  37.6 1.1 %reduce_sum.12 = bf16[256,128]{1,0:T(8,128)(2,1)S(1)} reduce(bf16[8,256,128]{2,1,0:T(8,128)(2,1)} %all-to-all-done.1, bf16[]{:T(256)} %constant.14.clone.1), dimensions={0}, to_apply=%region_2.3 | reduce | flops 229376 | bytes 589826 | tf_op jit(solution)/shard_map/reduce_sum | solution.py:320
  38.7 8.9 %all_gather.3.packed_ref = bf16[2048,128]{1,0:T(8,128)(2,1)S(1)} all-gather(bf16[256,128]{1,0:T(8,128)(2,1)S(1)} %reduce_sum.12), channel_id=1, replica_groups=mesh['rows'=8,'chan'=4] {'rows'}, dimensions={0}, use_global_device_ids=true | all-gather | bytes 589824 | tf_op jit(solution)/shard_map/all_gather | solution.py:321
  47.6 0.0 collective-permute-done.5.refs_3_
  47.6 0.9 %copy-done.3 = f32[400,128]{1,0:T(8,128)S(1)} copy-done((f32[400,128]{1,0:T(8,128)S(1)}, f32[400,128]{1,0:T(8,128)}, u32[]{:S(2)}) %copy-start.3) | copy-done | bytes 204824
  48.5 1.2 %finish_kernel.1 = (bf16[8,48,128]{2,1,0:T(8,128)(2,1)}, f32[1296,192]{1,0:T(8,128)}) custom-call(bf16[2048,128]{1,0:T(8,128)(2,1)S(1)} %all_gather.3.packed_ref, bf16[400,128]{1,0:T(8,128)(2,1)S(1)} %copy-done, f32[400,128]{1,0:T(8,128)S(1)} %copy-done.3, bf16[400,128]{1,0:T(8,128)(2,1)S(1)} %collective-permute-done.3.refs_1_, ...), custom_call_target="tpu_custom_call" | custom-call | tf_op jit(solution)/shard_map/finish_kernel/pallas_call | solution.py:322
  (10 shorter events, 0.0 us)
Async XLA Ops:
  2.3 18.3 %copy-start = (bf16[400,128]{1,0:T(8,128)(2,1)S(1)}, bf16[400,128]{1,0:T(8,128)(2,1)}, u32[]{:S(2)}) copy-start(bf16[400,128]{1,0:T(8,128)(2,1)} %get-tuple-element.16.refs_0_.x_ref) | copy-start | bytes 307204
  2.3 18.3 %collective-permute-start = (bf16[400,128]{1,0:T(8,128)(2,1)}, bf16[400,128]{1,0:T(8,128)(2,1)S(1)}, u32[]{:S(2)}, u32[]{:S(2)}) collective-permute-start(bf16[400,128]{1,0:T(8,128)(2,1)} %get-tuple-element.16.refs_0_.x_ref), channel_id=1, source_target_pairs={{0,1},{1,0},{2,3},{3,2},{4,5},{5,4},{6,7},{7,6},{8,9},{9,8},{10,11... | collective-permute-start | bytes 307208 | tf_op jit(solution)/shard_map/ppermute | solution.py:263
  5.3 15.3 %collective-permute-start.1 = (bf16[400,128]{1,0:T(8,128)(2,1)}, bf16[400,128]{1,0:T(8,128)(2,1)}, u32[]{:S(2)}, u32[]{:S(2)}) collective-permute-start(bf16[400,128]{1,0:T(8,128)(2,1)} %get-tuple-element.16.refs_0_.x_ref), channel_id=1, source_target_pairs={{0,2},{1,3},{2,0},{3,1},{4,6},{5,7},{6,4},{7,5},{8,10},{9,11},{10,... | collective-permute-start | bytes 307208 | tf_op jit(solution)/shard_map/ppermute | solution.py:263
  7.9 12.7 %collective-permute-start.2 = (bf16[400,128]{1,0:T(8,128)(2,1)}, bf16[400,128]{1,0:T(8,128)(2,1)}, u32[]{:S(2)}, u32[]{:S(2)}) collective-permute-start(bf16[400,128]{1,0:T(8,128)(2,1)} %get-tuple-element.16.refs_0_.x_ref), channel_id=1, source_target_pairs={{0,3},{1,2},{2,1},{3,0},{4,7},{5,6},{6,5},{7,4},{8,11},{9,10},{10,... | collective-permute-start | bytes 307208 | tf_op jit(solution)/shard_map/ppermute | solution.py:263
  19.0 0.7 %copy-start.4 = (s32[8]{0:T(128)S(1)}, s32[8]{0:T(128)}, u32[]{:S(2)}) copy-start(s32[8]{0:T(128)} %slot_ref.1) | copy-start | bytes 100
  20.5 7.3 %copy-start.1 = (bf16[27,48,192]{2,1,0:T(8,128)(2,1)S(1)}, bf16[27,48,192]{2,1,0:T(8,128)(2,1)}, u32[]{:S(2)}) copy-start(bf16[27,48,192]{2,1,0:T(8,128)(2,1)} %param.11) | copy-start | bytes 1492996
  23.7 13.9 %all-to-all-start.1 = ((bf16[8,256,128]{2,1,0:T(8,128)(2,1)}), bf16[8,256,128]{2,1,0:T(8,128)(2,1)}, u32[]{:S(2)}, u32[]{:S(2)}) async-start(bf16[8,256,128]{2,1,0:T(8,128)(2,1)} %bitcast.4), calls=%async_computation.1 | async-start | bytes 1048576 | tf_op jit(solution)/shard_map/all_to_all | solution.py:299
  30.7 0.7 %copy-start.2 = (f32[400,128]{1,0:T(8,128)}, f32[400,128]{1,0:T(8,128)S(1)}, u32[]{:S(2)}) copy-start(f32[400,128]{1,0:T(8,128)S(1)} %get-tuple-element.17.refs_0_) | copy-start | bytes 614404
  31.4 16.2 %collective-permute-start.3 = (bf16[400,128]{1,0:T(8,128)(2,1)}, bf16[400,128]{1,0:T(8,128)(2,1)S(1)}, u32[]{:S(2)}, u32[]{:S(2)}) collective-permute-start(bf16[400,128]{1,0:T(8,128)(2,1)} %get-tuple-element.18), channel_id=1, source_target_pairs={{0,1},{1,0},{2,3},{3,2},{4,5},{5,4},{6,7},{7,6},{8,9},{9,8},{10,11... | collective-permute-start | bytes 307208 | tf_op jit(solution)/shard_map/ppermute | solution.py:319
  32.1 15.5 %collective-permute-start.4 = (bf16[400,128]{1,0:T(8,128)(2,1)}, bf16[400,128]{1,0:T(8,128)(2,1)S(1)}, u32[]{:S(2)}, u32[]{:S(2)}) collective-permute-start(bf16[400,128]{1,0:T(8,128)(2,1)} %get-tuple-element.19), channel_id=1, source_target_pairs={{0,2},{1,3},{2,0},{3,1},{4,6},{5,7},{6,4},{7,5},{8,10},{9,11},{10,... | collective-permute-start | bytes 307208 | tf_op jit(solution)/shard_map/ppermute | solution.py:319
  35.5 12.1 %collective-permute-start.5 = (bf16[400,128]{1,0:T(8,128)(2,1)}, bf16[400,128]{1,0:T(8,128)(2,1)S(1)}, u32[]{:S(2)}, u32[]{:S(2)}) collective-permute-start(bf16[400,128]{1,0:T(8,128)(2,1)} %get-tuple-element.20), channel_id=1, source_target_pairs={{0,3},{1,2},{2,1},{3,0},{4,7},{5,6},{6,5},{7,4},{8,11},{9,10},{10,... | collective-permute-start | bytes 307208 | tf_op jit(solution)/shard_map/ppermute | solution.py:319
  47.6 0.9 %copy-start.3 = (f32[400,128]{1,0:T(8,128)S(1)}, f32[400,128]{1,0:T(8,128)}, u32[]{:S(2)}) copy-start(f32[400,128]{1,0:T(8,128)} %copy-done.2) | copy-start | bytes 614404

commit v10 on v5

--- a/solution.py
+++ b/solution.py
@@ -46,23 +46,38 @@
     )
 
 
-def gains(x_refs, start, group):
+def grouped(x_refs, pieces):
+    found, start = [], 0
+    for count in pieces:
+        found.append(x_refs[start : start + count])
+        start += count
+    return found
+
+
+def frame_of(refs, t, frames, group):
+    share = frames // len(refs)
+    return refs[t // share][pl.ds(t % share * group, group), :].astype(jnp.float32)
+
+
+def gains(x_groups, frames, group):
     found = []
-    for ref in x_refs:
-        rows = ref[pl.ds(start, 16), :].astype(jnp.float32)
+    for refs in x_groups:
+        rows = refs[0][pl.ds(frames // len(refs) * group, 16), :].astype(jnp.float32)
         gain = rows[0:1] + rows[1:2] + rows[2:3]
         found.append(jnp.transpose(jnp.broadcast_to(gain, (128, 128)))[:group])
     return found
 
 
-def norm(x_refs, t, group):
-    values = [ref[pl.ds(t * group, group), :].astype(jnp.float32) for ref in x_refs]
+def norm(x_groups, t, frames, group):
+    values = [frame_of(refs, t, frames, group) for refs in x_groups]
     squares = sum(jnp.sum(value * value, axis=0, keepdims=True) for value in values)
     scale = lax.rsqrt(squares / CHANNELS + EPSILON)
     return scale, [value * scale for value in values]
 
 
-def prepare_kernel(adjoint_ref, x_ref, gain_ref, strips_ref, payload_ref, lines, gain_rows):
+def prepare_kernel(
+    adjoint_ref, x_ref, gain_ref, strips_ref, payload_ref, first_ref, second_ref, lines, gain_rows
+):
     channels, height, width = adjoint_ref.shape
     frames = x_ref.shape[0]
     group = strips_ref.shape[2]
@@ -91,6 +106,8 @@
                 axis=0,
             ).astype(jnp.bfloat16)
         payload_ref[pl.ds(t * group, group), :] = values
+        half_ref = first_ref if t < frames // 2 else second_ref
+        half_ref[pl.ds(t % (frames // 2) * group, group), :] = values
     gain = gain_ref[...]
     high = gain.astype(jnp.bfloat16).astype(jnp.float32)
     middle = (gain - high).astype(jnp.bfloat16).astype(jnp.float32)
@@ -98,7 +115,8 @@
     gain_rows[pl.ds(0, 1), pl.ds(0, channels)] = high
     gain_rows[pl.ds(1, 1), pl.ds(0, channels)] = middle
     gain_rows[pl.ds(2, 1), pl.ds(0, channels)] = gain - high - middle
-    payload_ref[pl.ds(frames * group, 16), :] = gain_rows[...].astype(jnp.bfloat16)
+    for ref, start in ((payload_ref, frames * group), (first_ref, frames // 2 * group)):
+        ref[pl.ds(start, 16), :] = gain_rows[...].astype(jnp.bfloat16)
 
 
 def window_kernel(frames, group, slot_ref, adjoint_ref, windows, place):
@@ -127,15 +145,15 @@
                             pl.ds((a * 9 + b * 3 + c) * group, group), pl.ds(t * width, width)
                         ] = shifted
 
-def grad_kernel(frames, group, factor, at_ref, windows, *refs):
-    groups = len(refs) - 2
-    x_refs = refs[:groups]
-    grad_ref, hidden = refs[groups:]
+def grad_kernel(frames, group, pieces, factor, at_ref, windows, *refs):
+    groups = len(pieces)
+    x_groups = grouped(refs, pieces)
+    grad_ref, hidden = refs[sum(pieces) :]
     ins = groups * group
     width = windows.shape[1] // frames
-    gain = gains(x_refs, frames * group, group)
+    gain = gains(x_groups, frames, group)
     for t in range(frames):
-        scale, scaled = norm(x_refs, t, group)
+        scale, scaled = norm(x_groups, t, frames, group)
         for s in range(groups):
             normed = scaled[s] * gain[s]
             value = (normed * jax.nn.sigmoid(normed)).astype(jnp.bfloat16)
@@ -168,19 +186,19 @@
         grad_ref[pl.ds(base, tail), :] = jnp.zeros((tail, 128), jnp.bfloat16)
 
 
-def part_kernel(frames, group, at_ref, weight_ref, windows, *refs):
-    groups = (len(refs) - 1) // 2
-    x_refs = refs[:groups]
-    part_refs = refs[groups : 2 * groups]
-    product = refs[2 * groups]
+def part_kernel(frames, group, pieces, at_ref, weight_ref, windows, *refs):
+    groups, given = len(pieces), sum(pieces)
+    x_groups = grouped(refs, pieces)
+    part_refs = refs[given : given + groups]
+    product = refs[given + groups]
     width = part_refs[0].shape[-1]
     product[...] = lax.dot_general(
         weight_ref[...], windows[...], (((0,), (0,)), ((), ())), preferred_element_type=jnp.float32
     )
-    gain = gains(x_refs, frames * group, group)
+    gain = gains(x_groups, frames, group)
     shares = []
     for t in range(frames):
-        scale, scaled = norm(x_refs, t, group)
+        scale, scaled = norm(x_groups, t, frames, group)
         part_refs[0][pl.ds(frames * group + t, 1), :] = scale
         share = jnp.zeros((1, width), jnp.float32)
         for s in range(groups):
@@ -243,14 +261,17 @@
 
     taps_out = 27 * group
     pixels = frames * width
-    strips, payload = pl.pallas_call(
+    half = frames // 2 * group
+    strips, payload, *halves = pl.pallas_call(
         prepare_kernel,
         out_shape=(
             jax.ShapeDtypeStruct((count, 3, group, width), jnp.bfloat16),
             jax.ShapeDtypeStruct((frames * group + 16, width), jnp.bfloat16),
+            jax.ShapeDtypeStruct((half + 16, width), jnp.bfloat16),
+            jax.ShapeDtypeStruct((half, width), jnp.bfloat16),
         ),
         in_specs=[copied(), copied(), copied()],
-        out_specs=(vmem(), vmem()),
+        out_specs=(vmem(),) * 4,
         scratch_shapes=[
             pltpu.VMEM((channels * count, width), jnp.float32),
             pltpu.VMEM((16, width), jnp.float32),
@@ -259,9 +280,12 @@
         name="prepare_kernel",
     )(frame_adjoint[0], inputs[:, :, 0], gain.reshape(1, channels))
     partners = [[(z, z ^ s) for z in range(groups)] for s in range(groups)]
-    everything = [payload] * groups
-    for s in range(1, groups):
-        everything[s] = lax.ppermute(everything[s & (s - 1)], "chan", partners[s & -s])
+    everything = [[payload], [lax.ppermute(payload, "chan", partners[1])]]
+    for s in range(2, groups):
+        source = everything[s & (s - 1)] if s & (s - 1) else halves
+        everything.append([lax.ppermute(part, "chan", partners[s & -s]) for part in source])
+    pieces_of = tuple(len(parts) for parts in everything)
+    blocks = [part for parts in everything for part in parts]
     strips = lax.all_to_all(strips, "rows", split_axis=0, concat_axis=0, tiled=True)
     at = lax.axis_index("chan").astype(jnp.int32).reshape(1)
 
@@ -281,15 +305,15 @@
         name="window_kernel",
     )(frame_slot, strips)
     packed = pl.pallas_call(
-        functools.partial(grad_kernel, frames, group, factor),
+        functools.partial(grad_kernel, frames, group, pieces_of, factor),
         out_shape=jax.ShapeDtypeStruct((packed_rows, 128), jnp.bfloat16),
-        in_specs=[smem(), vmem()] + [copied()] * groups,
+        in_specs=[smem(), vmem()] + [copied()] * len(blocks),
         out_specs=vmem(),
         scratch_shapes=[pltpu.VMEM((ins, pixels), jnp.bfloat16)],
         compiler_params=limit(taps_out, pixels),
         cost_estimate=cost(taps_out, ins, pixels),
         name="grad_kernel",
-    )(at, windows, *everything)
+    )(at, windows, *blocks)
 
     pieces = lax.all_to_all(
         packed.reshape(count, packed_rows // count, 128),
@@ -298,18 +322,18 @@
 
     sent = frames * group + round_up(2 * frames, 16)
     parts = pl.pallas_call(
-        functools.partial(part_kernel, frames, group),
+        functools.partial(part_kernel, frames, group, pieces_of),
         out_shape=tuple(
             [jax.ShapeDtypeStruct((frames * (group + 2), width), jnp.float32)]
             + [jax.ShapeDtypeStruct((sent, width), jnp.bfloat16)] * (groups - 1)
         ),
-        in_specs=[smem(), vmem(), vmem()] + [copied()] * groups,
+        in_specs=[smem(), vmem(), vmem()] + [copied()] * len(blocks),
         out_specs=(vmem(),) * groups,
         scratch_shapes=[pltpu.VMEM((ins, pixels), jnp.float32)],
         compiler_params=limit(taps_out, pixels),
         cost_estimate=cost(taps_out, ins, pixels),
         name="part_kernel",
-    )(at, kernel, windows, *everything)
+    )(at, kernel, windows, *blocks)
 
     arrived = [lax.ppermute(parts[s], "chan", partners[s]) for s in range(1, groups)]
     summed = jnp.sum(pieces.astype(jnp.float32), axis=0).astype(jnp.bfloat16)

time: 48.7 us -> 49.6 us (1.018)
  starting transfers between devices: 18.7 us -> 19.6 us
    ppermute x3 -> x5, starting transfers between devices: 4.84 us -> 5.79 us  [the longest x4 4.21 us: shards(): lax.ppermute(part, 'chan', partners[s & -s])]
    ppermute x3 -> x5, waiting for transfers between devices: 6.92 us -> 6.82 us  [the longest x4 6.82 us: shards(): lax.ppermute(part, 'chan', partners[s & -s])]
  transfers between devices with their start and end apart: 8 -> 10, of which waited for: 3 -> 4; matrix products, arithmetic and copies ran while one was open for 2% -> 2% of each run, Pallas kernels for 6% -> 6%
where the time goes in v10:
time: 49.6 us; the launch traced here: 49.2 us
  starting transfers between devices  19.6 us (40%)
  waiting for transfers between devices  9.19 us (19%)
  blocking collectives  8.9 us (18%)
  Pallas kernels  7.88 us (16%)
  local copies, waits for them, and re-layouts  1.74 us (4%)
  other arithmetic  1.12 us (2%)
  between operations  0.68 us (1%)
    all_gather x1, blocking collectives, shards(): whole = lax.all_gather(summed, 'rows', axis=0, tiled=True)  8.9 us
    ppermute x4, waiting for transfers between devices, shards(): lax.ppermute(part, 'chan', partners[s & -s])  6.82 us
    all_to_all x1, starting transfers between devices, shards(): lax.all_to_all(strips, 'rows', split_axis=0, concat_axis=0, tiled=True)  5.3 us
    ppermute x3, starting transfers between devices, shards(): lax.ppermute(parts[s], 'chan', partners[s])  4.41 us
    ppermute x4, starting transfers between devices, shards(): lax.ppermute(part, 'chan', partners[s & -s])  4.21 us
    all_to_all x1, starting transfers between devices, shards(): lax.all_to_all(packed.reshape(count, packed_rows // count, 128), 'rows',...  4.14 us
    all_to_all x1, waiting for transfers between devices, shards(): lax.all_to_all(packed.reshape(count, packed_rows // count, 128), 'rows',...  2.35 us
    pallas_call x1, Pallas kernels, shards(): pl.pallas_call(functools.partial(grad_kernel, frames, group, pieces_of, f...  2.07 us
  transfers between devices with their start and end apart: 10, of which 4 were waited for; matrix products, arithmetic and copies ran while one was open for 2% of the time, Pallas kernels for 6%

profile of v10, /device:TPU:0, one launch (start us, length us, event | category | flops | bytes accessed | tf_op | source)
XLA Modules:
  0.0 49.2 jit_solution(14775908043634629886)
XLA Ops:
  0.6 1.8 %prepare_kernel.1 = (bf16[8,3,48,128]{3,2,1,0:T(8,128)(2,1)}, bf16[400,128]{1,0:T(8,128)(2,1)}, bf16[208,128]{1,0:T(8,128)(2,1)}, bf16[192,128]{1,0:T(8,128)(2,1)}) custom-call(bf16[48,8,128]{2,1,0:T(8,128)(2,1)} %bitcast.11, bf16[8,48,128]{2,1,0:T(8,128)(2,1)} %bitcast.12, f32[1,48]{1,0:T(1,128)} %bitcast.13), custom_call_target="tpu_custom_call" | custom-call | tf_op jit(solution)/shard_map/prepare_kernel/pallas_call | solution.py:265
  2.4 5.3 %all-to-all-start = ((bf16[8,3,48,128]{3,2,1,0:T(8,128)(2,1)}), bf16[8,3,48,128]{3,2,1,0:T(8,128)(2,1)S(1)}, u32[]{:S(2)}, u32[]{:S(2)}) async-start(bf16[8,3,48,128]{3,2,1,0:T(8,128)(2,1)} %get-tuple-element.12), calls=%async_computation | async-start | bytes 589824 | tf_op jit(solution)/shard_map/all_to_all | solution.py:289
  7.7 2.6 %collective-permute-start.1 = (bf16[208,128]{1,0:T(8,128)(2,1)}, bf16[208,128]{1,0:T(8,128)(2,1)S(1)}, u32[]{:S(2)}, u32[]{:S(2)}) collective-permute-start(bf16[208,128]{1,0:T(8,128)(2,1)} %get-tuple-element.14), channel_id=1, source_target_pairs={{0,2},{1,3},{2,0},{3,1},{4,6},{5,7},{6,4},{7,5},{8,10},{9,11},{10,... | collective-permute-start | bytes 159752 | tf_op jit(solution)/shard_map/ppermute | solution.py:286
  10.3 1.6 %collective-permute-start = (bf16[400,128]{1,0:T(8,128)(2,1)}, bf16[400,128]{1,0:T(8,128)(2,1)S(1)}, u32[]{:S(2)}, u32[]{:S(2)}) collective-permute-start(bf16[400,128]{1,0:T(8,128)(2,1)} %get-tuple-element.13.refs_0_.x_ref), channel_id=1, source_target_pairs={{0,1},{1,0},{2,3},{3,2},{4,5},{5,4},{6,7},{7,6},{8,9},{9,8},{10,11... | collective-permute-start | bytes 307208 | tf_op jit(solution)/shard_map/ppermute | solution.py:283
  11.9 0.3 collective-permute-start.2
  12.2 1.7 %collective-permute-done.1.refs_2_ = bf16[208,128]{1,0:T(8,128)(2,1)S(1)} collective-permute-done((bf16[208,128]{1,0:T(8,128)(2,1)}, bf16[208,128]{1,0:T(8,128)(2,1)S(1)}, u32[]{:S(2)}, u32[]{:S(2)}) %collective-permute-start.1) | collective-permute-done | bytes 53280 | tf_op jit(solution)/shard_map/ppermute | solution.py:286
  13.9 1.1 %collective-permute-start.3 = (bf16[208,128]{1,0:T(8,128)(2,1)S(1)}, bf16[208,128]{1,0:T(8,128)(2,1)S(1)}, u32[]{:S(2)}, u32[]{:S(2)}) collective-permute-start(bf16[208,128]{1,0:T(8,128)(2,1)S(1)} %collective-permute-done.1.refs_2_), channel_id=1, source_target_pairs={{0,1},{1,0},{2,3},{3,2},{4,5},{5,4},{6,7},{7,6},{8,9},{9,8},{10,11... | collective-permute-start | bytes 159752 | tf_op jit(solution)/shard_map/ppermute | solution.py:286
  15.1 2.8 %collective-permute-done.2.refs_3_ = bf16[192,128]{1,0:T(8,128)(2,1)S(1)} collective-permute-done((bf16[192,128]{1,0:T(8,128)(2,1)}, bf16[192,128]{1,0:T(8,128)(2,1)S(1)}, u32[]{:S(2)}, u32[]{:S(2)}) %collective-permute-start.2) | collective-permute-done | bytes 49184 | tf_op jit(solution)/shard_map/ppermute | solution.py:286
  17.8 0.2 collective-permute-start.4
  18.0 0.7 %copy-done.2 = s32[8]{0:T(128)S(1)} copy-done((s32[8]{0:T(128)S(1)}, s32[8]{0:T(128)}, u32[]{:S(2)}) %copy-start.2) | copy-done | bytes 56
  18.6 0.9 %window_kernel.1.windows = bf16[1296,1024]{1,0:T(8,128)(2,1)S(1)} custom-call(s32[8]{0:T(128)S(1)} %copy-done.2, bf16[8,3,48,128]{3,2,1,0:T(8,128)(2,1)S(1)} %all-to-all-done.adjoint_ref), custom_call_target="tpu_custom_call" | custom-call | tf_op jit(solution)/shard_map/window_kernel/pallas_call | solution.py:298
  19.6 2.3 %collective-permute-done.4.refs_5_ = bf16[192,128]{1,0:T(8,128)(2,1)S(1)} collective-permute-done((bf16[192,128]{1,0:T(8,128)(2,1)S(1)}, bf16[192,128]{1,0:T(8,128)(2,1)S(1)}, u32[]{:S(2)}, u32[]{:S(2)}) %collective-permute-start.4) | collective-permute-done | bytes 49184 | tf_op jit(solution)/shard_map/ppermute | solution.py:286
  21.9 2.1 %grad_kernel.1 = bf16[2048,128]{1,0:T(8,128)(2,1)} custom-call(s32[1]{0:T(128)} %bitcast.at_ref, bf16[1296,1024]{1,0:T(8,128)(2,1)S(1)} %window_kernel.1.windows, bf16[400,128]{1,0:T(8,128)(2,1)S(1)} %copy-done, bf16[400,128]{1,0:T(8,128)(2,1)S(1)} %collective-permute-done.refs_1_, bf16[208,128]{1,0:T(8,128)(2,1)S(1)} %collective-permute-done.1.refs_2_, ...), custom_call_target="tpu_custom_call" | custom-call | flops 509607936 | bytes 3047424 | tf_op jit(solution)/shard_map/grad_kernel/pallas_call | solution.py:307
  24.0 4.1 %all-to-all-start.1 = ((bf16[8,256,128]{2,1,0:T(8,128)(2,1)}), bf16[8,256,128]{2,1,0:T(8,128)(2,1)}, u32[]{:S(2)}, u32[]{:S(2)}) async-start(bf16[8,256,128]{2,1,0:T(8,128)(2,1)} %bitcast.4), calls=%async_computation.1 | async-start | bytes 1048576 | tf_op jit(solution)/shard_map/all_to_all | solution.py:318
  28.1 0.0 copy-start.1
  28.1 1.1 %copy-done.1 = bf16[27,48,192]{2,1,0:T(8,128)(2,1)S(1)} copy-done((bf16[27,48,192]{2,1,0:T(8,128)(2,1)S(1)}, bf16[27,48,192]{2,1,0:T(8,128)(2,1)}, u32[]{:S(2)}) %copy-start.1) | copy-done | bytes 497688
  29.2 1.9 %part_kernel.1 = (f32[400,128]{1,0:T(8,128)S(1)}, bf16[400,128]{1,0:T(8,128)(2,1)}, bf16[400,128]{1,0:T(8,128)(2,1)}, bf16[400,128]{1,0:T(8,128)(2,1)S(1)}) custom-call(s32[1]{0:T(128)} %bitcast.at_ref, bf16[1296,192]{1,0:T(8,128)(2,1)S(1)} %bitcast.10, bf16[1296,1024]{1,0:T(8,128)(2,1)S(1)} %window_kernel.1.windows, bf16[400,128]{1,0:T(8,128)(2,1)S(1)} %copy-done, ...), custom_call_target="tpu_custom_call" | custom-call | flops 509607936 | bytes 3047424 | tf_op jit(solution)/shard_map/part_kernel/pallas_call | solution.py:324
  31.1 0.2 collective-permute-start.5
  31.3 1.9 %collective-permute-start.6 = (bf16[400,128]{1,0:T(8,128)(2,1)}, bf16[400,128]{1,0:T(8,128)(2,1)S(1)}, u32[]{:S(2)}, u32[]{:S(2)}) collective-permute-start(bf16[400,128]{1,0:T(8,128)(2,1)} %get-tuple-element.18), channel_id=1, source_target_pairs={{0,2},{1,3},{2,0},{3,1},{4,6},{5,7},{6,4},{7,5},{8,10},{9,11},{10,... | collective-permute-start | bytes 307208 | tf_op jit(solution)/shard_map/ppermute | solution.py:338
  33.2 2.3 %collective-permute-start.7 = (bf16[400,128]{1,0:T(8,128)(2,1)S(1)}, bf16[400,128]{1,0:T(8,128)(2,1)S(1)}, u32[]{:S(2)}, u32[]{:S(2)}) collective-permute-start(bf16[400,128]{1,0:T(8,128)(2,1)S(1)} %get-tuple-element.19), channel_id=1, source_target_pairs={{0,3},{1,2},{2,1},{3,0},{4,7},{5,6},{6,5},{7,4},{8,11},{9,10},{10,... | collective-permute-start | bytes 307208 | tf_op jit(solution)/shard_map/ppermute | solution.py:338
  35.5 2.4 %all-to-all-done.1 = bf16[8,256,128]{2,1,0:T(8,128)(2,1)} async-done(((bf16[8,256,128]{2,1,0:T(8,128)(2,1)}), bf16[8,256,128]{2,1,0:T(8,128)(2,1)}, u32[]{:S(2)}, u32[]{:S(2)}) %all-to-all-start.1) | async-done | bytes 524320 | tf_op jit(solution)/shard_map/all_to_all | solution.py:318
  37.9 1.1 %reduce_sum.12 = bf16[256,128]{1,0:T(8,128)(2,1)S(1)} reduce(bf16[8,256,128]{2,1,0:T(8,128)(2,1)} %all-to-all-done.1, bf16[]{:T(256)} %constant.3.clone.1), dimensions={0}, to_apply=%region_0.1 | reduce | flops 229376 | bytes 589826 | tf_op jit(solution)/shard_map/reduce_sum | solution.py:339
  39.0 8.9 %all_gather.3.packed_ref = bf16[2048,128]{1,0:T(8,128)(2,1)S(1)} all-gather(bf16[256,128]{1,0:T(8,128)(2,1)S(1)} %reduce_sum.12), channel_id=1, replica_groups=mesh['rows'=8,'chan'=4] {'rows'}, dimensions={0}, use_global_device_ids=true | all-gather | bytes 589824 | tf_op jit(solution)/shard_map/all_gather | solution.py:340
  47.9 1.2 %finish_kernel.1 = (bf16[8,48,128]{2,1,0:T(8,128)(2,1)}, f32[1296,192]{1,0:T(8,128)}) custom-call(bf16[2048,128]{1,0:T(8,128)(2,1)S(1)} %all_gather.3.packed_ref, bf16[400,128]{1,0:T(8,128)(2,1)S(1)} %copy-done, f32[400,128]{1,0:T(8,128)S(1)} %get-tuple-element.16.refs_0_, bf16[400,128]{1,0:T(8,128)(2,1)S(1)} %collective-permute-done.5.refs_1_, ...), custom_call_target="tpu_custom_call" | custom-call | tf_op jit(solution)/shard_map/finish_kernel/pallas_call | solution.py:341
  (9 shorter events, 0.0 us)
Async XLA Ops:
  2.4 19.5 %copy-start = (bf16[400,128]{1,0:T(8,128)(2,1)S(1)}, bf16[400,128]{1,0:T(8,128)(2,1)}, u32[]{:S(2)}) copy-start(bf16[400,128]{1,0:T(8,128)(2,1)} %get-tuple-element.13.refs_0_.x_ref) | copy-start | bytes 307204
  2.4 15.6 %all-to-all-start = ((bf16[8,3,48,128]{3,2,1,0:T(8,128)(2,1)}), bf16[8,3,48,128]{3,2,1,0:T(8,128)(2,1)S(1)}, u32[]{:S(2)}, u32[]{:S(2)}) async-start(bf16[8,3,48,128]{3,2,1,0:T(8,128)(2,1)} %get-tuple-element.12), calls=%async_computation | async-start | bytes 589824 | tf_op jit(solution)/shard_map/all_to_all | solution.py:289
  7.7 6.2 %collective-permute-start.1 = (bf16[208,128]{1,0:T(8,128)(2,1)}, bf16[208,128]{1,0:T(8,128)(2,1)S(1)}, u32[]{:S(2)}, u32[]{:S(2)}) collective-permute-start(bf16[208,128]{1,0:T(8,128)(2,1)} %get-tuple-element.14), channel_id=1, source_target_pairs={{0,2},{1,3},{2,0},{3,1},{4,6},{5,7},{6,4},{7,5},{8,10},{9,11},{10,... | collective-permute-start | bytes 159752 | tf_op jit(solution)/shard_map/ppermute | solution.py:286
  10.3 11.6 %collective-permute-start = (bf16[400,128]{1,0:T(8,128)(2,1)}, bf16[400,128]{1,0:T(8,128)(2,1)S(1)}, u32[]{:S(2)}, u32[]{:S(2)}) collective-permute-start(bf16[400,128]{1,0:T(8,128)(2,1)} %get-tuple-element.13.refs_0_.x_ref), channel_id=1, source_target_pairs={{0,1},{1,0},{2,3},{3,2},{4,5},{5,4},{6,7},{7,6},{8,9},{9,8},{10,11... | collective-permute-start | bytes 307208 | tf_op jit(solution)/shard_map/ppermute | solution.py:283
  11.9 5.9 %collective-permute-start.2 = (bf16[192,128]{1,0:T(8,128)(2,1)}, bf16[192,128]{1,0:T(8,128)(2,1)S(1)}, u32[]{:S(2)}, u32[]{:S(2)}) collective-permute-start(bf16[192,128]{1,0:T(8,128)(2,1)} %get-tuple-element.15), channel_id=1, source_target_pairs={{0,2},{1,3},{2,0},{3,1},{4,6},{5,7},{6,4},{7,5},{8,10},{9,11},{10,... | collective-permute-start | bytes 147464 | tf_op jit(solution)/shard_map/ppermute | solution.py:286
  13.9 8.0 %collective-permute-start.3 = (bf16[208,128]{1,0:T(8,128)(2,1)S(1)}, bf16[208,128]{1,0:T(8,128)(2,1)S(1)}, u32[]{:S(2)}, u32[]{:S(2)}) collective-permute-start(bf16[208,128]{1,0:T(8,128)(2,1)S(1)} %collective-permute-done.1.refs_2_), channel_id=1, source_target_pairs={{0,1},{1,0},{2,3},{3,2},{4,5},{5,4},{6,7},{7,6},{8,9},{9,8},{10,11... | collective-permute-start | bytes 159752 | tf_op jit(solution)/shard_map/ppermute | solution.py:286
  17.8 4.1 %collective-permute-start.4 = (bf16[192,128]{1,0:T(8,128)(2,1)S(1)}, bf16[192,128]{1,0:T(8,128)(2,1)S(1)}, u32[]{:S(2)}, u32[]{:S(2)}) collective-permute-start(bf16[192,128]{1,0:T(8,128)(2,1)S(1)} %collective-permute-done.2.refs_3_), channel_id=1, source_target_pairs={{0,1},{1,0},{2,3},{3,2},{4,5},{5,4},{6,7},{7,6},{8,9},{9,8},{10,11... | collective-permute-start | bytes 147464 | tf_op jit(solution)/shard_map/ppermute | solution.py:286
  18.0 0.7 %copy-start.2 = (s32[8]{0:T(128)S(1)}, s32[8]{0:T(128)}, u32[]{:S(2)}) copy-start(s32[8]{0:T(128)} %slot_ref.1) | copy-start | bytes 100
  24.0 13.9 %all-to-all-start.1 = ((bf16[8,256,128]{2,1,0:T(8,128)(2,1)}), bf16[8,256,128]{2,1,0:T(8,128)(2,1)}, u32[]{:S(2)}, u32[]{:S(2)}) async-start(bf16[8,256,128]{2,1,0:T(8,128)(2,1)} %bitcast.4), calls=%async_computation.1 | async-start | bytes 1048576 | tf_op jit(solution)/shard_map/all_to_all | solution.py:318
  28.1 1.1 %copy-start.1 = (bf16[27,48,192]{2,1,0:T(8,128)(2,1)S(1)}, bf16[27,48,192]{2,1,0:T(8,128)(2,1)}, u32[]{:S(2)}) copy-start(bf16[27,48,192]{2,1,0:T(8,128)(2,1)} %param.9) | copy-start | bytes 1492996
  31.1 16.8 %collective-permute-start.5 = (bf16[400,128]{1,0:T(8,128)(2,1)}, bf16[400,128]{1,0:T(8,128)(2,1)S(1)}, u32[]{:S(2)}, u32[]{:S(2)}) collective-permute-start(bf16[400,128]{1,0:T(8,128)(2,1)} %get-tuple-element.17), channel_id=1, source_target_pairs={{0,1},{1,0},{2,3},{3,2},{4,5},{5,4},{6,7},{7,6},{8,9},{9,8},{10,11... | collective-permute-start | bytes 307208 | tf_op jit(solution)/shard_map/ppermute | solution.py:338
  31.3 16.6 %collective-permute-start.6 = (bf16[400,128]{1,0:T(8,128)(2,1)}, bf16[400,128]{1,0:T(8,128)(2,1)S(1)}, u32[]{:S(2)}, u32[]{:S(2)}) collective-permute-start(bf16[400,128]{1,0:T(8,128)(2,1)} %get-tuple-element.18), channel_id=1, source_target_pairs={{0,2},{1,3},{2,0},{3,1},{4,6},{5,7},{6,4},{7,5},{8,10},{9,11},{10,... | collective-permute-start | bytes 307208 | tf_op jit(solution)/shard_map/ppermute | solution.py:338
  33.2 14.7 %collective-permute-start.7 = (bf16[400,128]{1,0:T(8,128)(2,1)S(1)}, bf16[400,128]{1,0:T(8,128)(2,1)S(1)}, u32[]{:S(2)}, u32[]{:S(2)}) collective-permute-start(bf16[400,128]{1,0:T(8,128)(2,1)S(1)} %get-tuple-element.19), channel_id=1, source_target_pairs={{0,3},{1,2},{2,1},{3,0},{4,7},{5,6},{6,5},{7,4},{8,11},{9,10},{10,... | collective-permute-start | bytes 307208 | tf_op jit(solution)/shard_map/ppermute | solution.py:338

commit v11 on v4

--- a/solution.py
+++ b/solution.py
@@ -105,10 +105,22 @@
     payload_ref[pl.ds(frames * group, 16), :] = gain_rows[...].astype(jnp.bfloat16)
 
 
-def hidden_kernel(frames, group, at_ref, *refs):
-    x_refs, hidden = refs[:-1], refs[-1]
-    groups = len(x_refs)
-    width = hidden.shape[1] // frames
+def grad_kernel(frames, group, factor, at_ref, adjoint_ref, slot_hbm, *refs):
+    groups = (len(refs) - 6) // 2
+    x_hbm = refs[:groups]
+    grad_ref, windows, place, hidden, slots, moved = refs[groups : groups + 6]
+    x_refs = refs[groups + 6 :]
+    ins = groups * group
+    width = adjoint_ref.shape[-1]
+    arriving = [
+        pltpu.make_async_copy(source, target, moved.at[k])
+        for k, (source, target) in enumerate(zip((slot_hbm, *x_hbm), (slots, *x_refs)))
+    ]
+    for copy in arriving:
+        copy.start()
+    for copy in arriving:
+        copy.wait()
+
     gain = gains(x_refs, frames * group, group)
     for t in range(frames):
         scale, scaled = norm(x_refs, t, group)
@@ -118,12 +130,8 @@
             start = pl.multiple_of((at_ref[0] ^ s) * group, 16)
             hidden[pl.ds(start, group), pl.ds(t * width, width)] = value
 
-
-def grad_kernel(frames, factor, slot_ref, adjoint_ref, hidden, grad_ref, windows, place):
-    group, ins = adjoint_ref.shape[2], hidden.shape[0]
-    width = adjoint_ref.shape[-1]
     for slot in range(frames):
-        place[slot_ref[slot]] = slot
+        place[slots[slot]] = slot
 
     lane = lax.broadcasted_iota(jnp.int32, (group, width), 1)
     nothing = jnp.zeros((group, width), jnp.bfloat16)
@@ -209,7 +217,9 @@
 
 
 def finish_kernel(frames, group, packed_ref, x_ref, *refs):
-    own_ref, others, (out_ref, grad_ref) = refs[0], refs[1:-2], refs[-2:]
+    own_hbm, others, (out_ref, grad_ref, own_ref, moved) = refs[0], refs[1:-4], refs[-4:]
+    own_copy = pltpu.make_async_copy(own_hbm, own_ref, moved)
+    own_copy.start()
     taps_out, ins = grad_ref.shape
     blocks, rest, half, rows = packing(taps_out, ins, 1)
     for block in range(blocks):
@@ -223,6 +233,7 @@
             : taps_out - half, rest:
         ]
 
+    own_copy.wait()
     share = own_ref[pl.ds(frames * group + frames, frames), :]
     for ref in others:
         both = ref[pl.ds(frames * group, round_up(2 * frames, 16)), :].astype(jnp.float32)
@@ -266,7 +277,12 @@
     everything = [payload] + [
         lax.ppermute(payload, "chan", partners[s]) for s in range(1, groups)
     ]
-    strips = lax.all_to_all(strips, "rows", split_axis=0, concat_axis=0, tiled=True)
+    strips = lax.cond(
+        lax.axis_index("rows") < count,
+        lambda rows: lax.all_to_all(rows, "rows", split_axis=0, concat_axis=0, tiled=True),
+        lambda rows: rows,
+        strips,
+    )
     at = lax.axis_index("chan").astype(jnp.int32).reshape(1)
 
     kernel = weight.reshape(27, channels, groups, channels)
@@ -275,30 +291,25 @@
 
     packed_rows = packing(taps_out, ins, count)[3]
     factor = float(frames * count * width) ** (-0.5)
-    hidden = pl.pallas_call(
-        functools.partial(hidden_kernel, frames, group),
-        out_shape=jax.ShapeDtypeStruct((ins, pixels), jnp.bfloat16),
-        in_specs=[smem()] + [copied()] * groups,
-        out_specs=vmem(),
-        compiler_params=limit(taps_out, pixels),
-        cost_estimate=pl.CostEstimate(
-            flops=16 * ins * pixels, bytes_accessed=32 * ins * pixels, transcendentals=ins * pixels
-        ),
-        name="hidden_kernel",
-    )(at, *everything)
     packed, windows = pl.pallas_call(
-        functools.partial(grad_kernel, frames, factor),
+        functools.partial(grad_kernel, frames, group, factor),
         out_shape=(
             jax.ShapeDtypeStruct((packed_rows, 128), jnp.bfloat16),
             jax.ShapeDtypeStruct((taps_out, pixels), jnp.bfloat16),
         ),
-        in_specs=[smem(), copied(), vmem()],
+        in_specs=[smem(), vmem()] + [anywhere()] * (groups + 1),
         out_specs=(vmem(), vmem()),
-        scratch_shapes=[pltpu.SMEM((frames,), jnp.int32)],
+        scratch_shapes=[
+            pltpu.SMEM((frames,), jnp.int32),
+            pltpu.VMEM((ins, pixels), jnp.bfloat16),
+            pltpu.SMEM((frames,), jnp.int32),
+            pltpu.SemaphoreType.DMA((groups + 1,)),
+        ]
+        + [pltpu.VMEM(payload.shape, jnp.bfloat16)] * groups,
         compiler_params=limit(taps_out, pixels),
         cost_estimate=cost(taps_out, ins, pixels),
         name="grad_kernel",
-    )(frame_slot, strips, hidden)
+    )(at, strips, frame_slot, *everything)
 
     pieces = lax.all_to_all(
         packed.reshape(count, packed_rows // count, 128),
@@ -329,8 +340,12 @@
             jax.ShapeDtypeStruct((frames, group, width), jnp.bfloat16),
             jax.ShapeDtypeStruct((taps_out, ins), jnp.float32),
         ),
-        in_specs=[copied()] * (groups + 2),
+        in_specs=[copied(), copied(), anywhere()] + [copied()] * (groups - 1),
         out_specs=(vmem(), vmem()),
+        scratch_shapes=[
+            pltpu.VMEM((frames * (group + 2), width), jnp.float32),
+            pltpu.SemaphoreType.DMA,
+        ],
         compiler_params=limit(taps_out, pixels),
         name="finish_kernel",
     )(whole, payload, parts[0], *arrived)

time: 55.9 us -> 54.9 us (0.982)
  blocking collectives: 9.33 us -> 20.3 us
  waiting for transfers between devices: 9.64 us -> 0.95 us
  starting transfers between devices: 18.2 us -> 14.2 us
  Pallas kernels: 6.99 us -> 8.1 us
    all_to_all x0 -> x1, blocking collectives: none -> 11 us  [shards(): lax.all_to_all(rows, 'rows', split_axis=0, concat_axis=0, tiled=True)]
    ppermute x3, waiting for transfers between devices: 8.71 us -> 0.01 us  [shards(): lax.ppermute(payload, 'chan', partners[s])]
    all_to_all x1 -> x0, starting transfers between devices: 5.3 us -> none  [shards(): lax.all_to_all(strips, 'rows', split_axis=0, concat_axis=0, tiled=True)]
    ppermute x3, starting transfers between devices: 4.39 us -> 5.62 us  [shards(): lax.ppermute(payload, 'chan', partners[s])]
    pallas_call x2 -> x1, Pallas kernels: 1.99 us -> 2.99 us  [shards(): pl.pallas_call(functools.partial(grad_kernel, frames, group, factor), out...]
    unnamed x30 -> x28, local copies, waits for them, and re-layouts: 9.22 us -> 8.89 us
  transfers between devices with their start and end apart: 8 -> 7, of which waited for: 3 -> 1; matrix products, arithmetic and copies ran while one was open for 2% -> 2% of each run, Pallas kernels for 4% -> 4%
where the time goes in v11:
time: 54.9 us; the launch traced here: 54.3 us
  blocking collectives  20.3 us (37%)
  starting transfers between devices  14.2 us (26%)
  local copies, waits for them, and re-layouts  8.91 us (16%)
  Pallas kernels  8.1 us (15%)
  other arithmetic  1.12 us (2%)
  waiting for transfers between devices  0.95 us (2%)
  between operations  0.73 us (1%)
    all_to_all x1, blocking collectives, shards(): lax.all_to_all(rows, 'rows', split_axis=0, concat_axis=0, tiled=True)  11 us
    all_gather x1, blocking collectives, shards(): whole = lax.all_gather(summed, 'rows', axis=0, tiled=True)  9.32 us
    unnamed x28, local copies, waits for them, and re-layouts  8.89 us
    ppermute x3, starting transfers between devices, shards(): lax.ppermute(payload, 'chan', partners[s])  5.62 us
    ppermute x3, starting transfers between devices, shards(): lax.ppermute(parts[s], 'chan', partners[s])  4.4 us
    all_to_all x1, starting transfers between devices, shards(): lax.all_to_all(packed.reshape(count, packed_rows // count, 128), 'rows',...  4.15 us
    pallas_call x1, Pallas kernels, shards(): pl.pallas_call(functools.partial(grad_kernel, frames, group, factor), out...  2.99 us
    pallas_call x1, Pallas kernels, shards(): pl.pallas_call(functools.partial(part_kernel, frames, group), out_shape=t...  1.91 us
  transfers between devices with their start and end apart: 7, of which 1 were waited for; matrix products, arithmetic and copies ran while one was open for 2% of the time, Pallas kernels for 4%

profile of v11, /device:TPU:0, one launch (start us, length us, event | category | flops | bytes accessed | tf_op | source)
XLA Modules:
  0.0 54.3 jit_solution(12810272482509205531)
XLA Ops:
  0.6 1.7 %prepare_kernel.1 = (bf16[8,3,48,128]{3,2,1,0:T(8,128)(2,1)S(1)}, bf16[400,128]{1,0:T(8,128)(2,1)}) custom-call(bf16[48,8,128]{2,1,0:T(8,128)(2,1)} %bitcast.12, bf16[8,48,128]{2,1,0:T(8,128)(2,1)} %bitcast.13, f32[1,48]{1,0:T(1,128)} %bitcast.14), custom_call_target="tpu_custom_call" | custom-call | tf_op jit(solution)/shard_map/prepare_kernel/pallas_call | solution.py:261
  2.4 3.0 %collective-permute-start = (bf16[400,128]{1,0:T(8,128)(2,1)}, bf16[400,128]{1,0:T(8,128)(2,1)S(1)}, u32[]{:S(2)}, u32[]{:S(2)}) collective-permute-start(bf16[400,128]{1,0:T(8,128)(2,1)} %get-tuple-element.18.refs_0_.x_ref), channel_id=1, source_target_pairs={{0,1},{1,0},{2,3},{3,2},{4,5},{5,4},{6,7},{7,6},{8,9},{9,8},{10,11... | collective-permute-start | bytes 307208 | tf_op jit(solution)/shard_map/ppermute | solution.py:278
  5.4 2.6 %collective-permute-start.1 = (bf16[400,128]{1,0:T(8,128)(2,1)}, bf16[400,128]{1,0:T(8,128)(2,1)S(1)}, u32[]{:S(2)}, u32[]{:S(2)}) collective-permute-start(bf16[400,128]{1,0:T(8,128)(2,1)} %get-tuple-element.18.refs_0_.x_ref), channel_id=1, source_target_pairs={{0,2},{1,3},{2,0},{3,1},{4,6},{5,7},{6,4},{7,5},{8,10},{9,11},{10,... | collective-permute-start | bytes 307208 | tf_op jit(solution)/shard_map/ppermute | solution.py:278
  8.0 11.1 %conditional.1 = (bf16[8,3,48,128]{3,2,1,0:T(8,128)(2,1)S(1)}) conditional(s32[]{:T(128)} %convert_element_type.2, bf16[8,3,48,128]{3,2,1,0:T(8,128)(2,1)S(1)} %get-tuple-element.17, bf16[8,3,48,128]{3,2,1,0:T(8,128)(2,1)S(1)} %get-tuple-element.17), branch_computations={%region_0.0_spmd, %region_1.0_spmd} | conditional | bytes 1179656 | solution.py:280
  8.0 11.0 %all_to_all.9 = bf16[8,3,48,128]{3,2,1,0:T(8,128)(2,1)S(1)} all-to-all(bf16[8,3,48,128]{3,2,1,0:T(8,128)(2,1)S(1)} %copy.10), channel_id=1, replica_groups=mesh['rows'=8,'chan'=4] {'rows'}, dimensions={0} | all-to-all | bytes 589824 | tf_op jit(solution)/shard_map/cond/branch_1_fun/all_to_all | solution.py:282
  19.1 0.7 %copy-done.6 = bf16[400,128]{1,0:T(8,128)(2,1)} copy-done((bf16[400,128]{1,0:T(8,128)(2,1)}, bf16[400,128]{1,0:T(8,128)(2,1)S(1)}, u32[]{:S(2)}) %copy-start.6) | copy-done | bytes 102424
  20.4 0.9 %copy-done.2 = bf16[400,128]{1,0:T(8,128)(2,1)S(1)} copy-done((bf16[400,128]{1,0:T(8,128)(2,1)S(1)}, bf16[400,128]{1,0:T(8,128)(2,1)}, u32[]{:S(2)}) %copy-start.2) | copy-done | bytes 102424
  21.3 0.9 %copy-done.7 = bf16[400,128]{1,0:T(8,128)(2,1)S(1)} copy-done((bf16[400,128]{1,0:T(8,128)(2,1)S(1)}, bf16[400,128]{1,0:T(8,128)(2,1)}, u32[]{:S(2)}) %copy-start.7) | copy-done | bytes 102424
  22.2 0.9 %copy-done.10 = bf16[400,128]{1,0:T(8,128)(2,1)S(1)} copy-done((bf16[400,128]{1,0:T(8,128)(2,1)S(1)}, bf16[400,128]{1,0:T(8,128)(2,1)}, u32[]{:S(2)}) %copy-start.10) | copy-done | bytes 102424
  23.1 0.7 %copy-done.12 = s32[8]{0:T(128)S(1)} copy-done((s32[8]{0:T(128)S(1)}, s32[8]{0:T(128)}, u32[]{:S(2)}) %copy-start.12) | copy-done | bytes 56
  23.8 3.0 %grad_kernel.1 = (bf16[2048,128]{1,0:T(8,128)(2,1)S(1)}, bf16[1296,1024]{1,0:T(8,128)(2,1)S(1)}) custom-call(s32[1]{0:T(128)} %bitcast.at_ref, bf16[8,3,48,128]{3,2,1,0:T(8,128)(2,1)} %copy-done.13, s32[8]{0:T(128)S(1)} %copy-done.12, bf16[400,128]{1,0:T(8,128)(2,1)S(1)} %copy-done.2, bf16[400,128]{1,0:T(8,128)(2,1)S(1)} %collective-permute-done.refs_1_, ...), custom_call_target="tpu_custom_call" | custom-call | flops 509607936 | bytes 3047424 | tf_op jit(solution)/shard_map/grad_kernel/pallas_call | solution.py:294
  26.8 0.8 %copy-done.1 = bf16[2048,128]{1,0:T(8,128)(2,1)} copy-done((bf16[2048,128]{1,0:T(8,128)(2,1)}, bf16[2048,128]{1,0:T(8,128)(2,1)S(1)}, u32[]{:S(2)}) %copy-start.1) | copy-done | bytes 524312
  27.6 4.1 %all-to-all-start.1 = ((bf16[8,256,128]{2,1,0:T(8,128)(2,1)}), bf16[8,256,128]{2,1,0:T(8,128)(2,1)}, u32[]{:S(2)}, u32[]{:S(2)}) async-start(bf16[8,256,128]{2,1,0:T(8,128)(2,1)} %bitcast.11), calls=%async_computation.1 | async-start | bytes 1048576 | tf_op jit(solution)/shard_map/all_to_all | solution.py:314
  31.7 0.9 %copy-done.8 = bf16[400,128]{1,0:T(8,128)(2,1)S(1)} copy-done((bf16[400,128]{1,0:T(8,128)(2,1)S(1)}, bf16[400,128]{1,0:T(8,128)(2,1)}, u32[]{:S(2)}) %copy-start.8) | copy-done | bytes 102424
  32.6 0.9 %copy-done.11 = bf16[400,128]{1,0:T(8,128)(2,1)S(1)} copy-done((bf16[400,128]{1,0:T(8,128)(2,1)S(1)}, bf16[400,128]{1,0:T(8,128)(2,1)}, u32[]{:S(2)}) %copy-start.11) | copy-done | bytes 102424
  33.5 1.9 %part_kernel.1 = (f32[400,128]{1,0:T(8,128)S(1)}, bf16[400,128]{1,0:T(8,128)(2,1)}, bf16[400,128]{1,0:T(8,128)(2,1)}, bf16[400,128]{1,0:T(8,128)(2,1)}) custom-call(s32[1]{0:T(128)} %bitcast.at_ref, bf16[1296,192]{1,0:T(8,128)(2,1)S(1)} %bitcast.10, bf16[1296,1024]{1,0:T(8,128)(2,1)S(1)} %get-tuple-element.20.windows, bf16[400,128]{1,0:T(8,128)(2,1)S(1)} %copy-done.3, ...), custom_call_target="tpu_custom_call" | custom-call | flops 509607936 | bytes 3047424 | tf_op jit(solution)/shard_map/part_kernel/pallas_call | solution.py:320
  35.4 0.7 %copy-done.4 = f32[400,128]{1,0:T(8,128)} copy-done((f32[400,128]{1,0:T(8,128)}, f32[400,128]{1,0:T(8,128)S(1)}, u32[]{:S(2)}) %copy-start.4) | copy-done | bytes 204824
  36.1 0.7 %collective-permute-start.3 = (bf16[400,128]{1,0:T(8,128)(2,1)}, bf16[400,128]{1,0:T(8,128)(2,1)S(1)}, u32[]{:S(2)}, u32[]{:S(2)}) collective-permute-start(bf16[400,128]{1,0:T(8,128)(2,1)} %get-tuple-element.22), channel_id=1, source_target_pairs={{0,1},{1,0},{2,3},{3,2},{4,5},{5,4},{6,7},{7,6},{8,9},{9,8},{10,11... | collective-permute-start | bytes 307208 | tf_op jit(solution)/shard_map/ppermute | solution.py:334
  36.8 3.5 %collective-permute-start.4 = (bf16[400,128]{1,0:T(8,128)(2,1)}, bf16[400,128]{1,0:T(8,128)(2,1)S(1)}, u32[]{:S(2)}, u32[]{:S(2)}) collective-permute-start(bf16[400,128]{1,0:T(8,128)(2,1)} %get-tuple-element.23), channel_id=1, source_target_pairs={{0,2},{1,3},{2,0},{3,1},{4,6},{5,7},{6,4},{7,5},{8,10},{9,11},{10,... | collective-permute-start | bytes 307208 | tf_op jit(solution)/shard_map/ppermute | solution.py:334
  40.5 0.9 %all-to-all-done.1 = bf16[8,256,128]{2,1,0:T(8,128)(2,1)} async-done(((bf16[8,256,128]{2,1,0:T(8,128)(2,1)}), bf16[8,256,128]{2,1,0:T(8,128)(2,1)}, u32[]{:S(2)}, u32[]{:S(2)}) %all-to-all-start.1) | async-done | bytes 524320 | tf_op jit(solution)/shard_map/all_to_all | solution.py:314
  41.5 1.1 %reduce_sum.12 = bf16[256,128]{1,0:T(8,128)(2,1)S(1)} reduce(bf16[8,256,128]{2,1,0:T(8,128)(2,1)} %all-to-all-done.1, bf16[]{:T(256)} %constant.14.clone.1), dimensions={0}, to_apply=%region_2.3 | reduce | flops 229376 | bytes 589826 | tf_op jit(solution)/shard_map/reduce_sum | solution.py:335
  42.6 9.3 %all_gather.3.packed_ref = bf16[2048,128]{1,0:T(8,128)(2,1)S(1)} all-gather(bf16[256,128]{1,0:T(8,128)(2,1)S(1)} %reduce_sum.12), channel_id=1, replica_groups=mesh['rows'=8,'chan'=4] {'rows'}, dimensions={0}, use_global_device_ids=true | all-gather | bytes 589824 | tf_op jit(solution)/shard_map/all_gather | solution.py:336
  51.9 0.9 %copy-done.5 = f32[400,128]{1,0:T(8,128)S(1)} copy-done((f32[400,128]{1,0:T(8,128)S(1)}, f32[400,128]{1,0:T(8,128)}, u32[]{:S(2)}) %copy-start.5) | copy-done | bytes 204824
  52.8 1.5 %finish_kernel.1 = (bf16[8,48,128]{2,1,0:T(8,128)(2,1)}, f32[1296,192]{1,0:T(8,128)}) custom-call(bf16[2048,128]{1,0:T(8,128)(2,1)S(1)} %all_gather.3.packed_ref, bf16[400,128]{1,0:T(8,128)(2,1)S(1)} %copy-done.3, f32[400,128]{1,0:T(8,128)S(1)} %copy-done.5, bf16[400,128]{1,0:T(8,128)(2,1)S(1)} %collective-permute-done.3.refs_1_, ...), custom_call_target="tpu_custom_call" | custom-call | tf_op jit(solution)/shard_map/finish_kernel/pallas_call | solution.py:337
  (27 shorter events, 1.0 us)
Async XLA Ops:
  0.6 31.1 %copy-start = (bf16[27,48,192]{2,1,0:T(8,128)(2,1)S(1)}, bf16[27,48,192]{2,1,0:T(8,128)(2,1)}, u32[]{:S(2)}) copy-start(bf16[27,48,192]{2,1,0:T(8,128)(2,1)} %param.11) | copy-start | bytes 1492996
  2.4 29.4 %copy-start.3 = (bf16[400,128]{1,0:T(8,128)(2,1)S(1)}, bf16[400,128]{1,0:T(8,128)(2,1)}, u32[]{:S(2)}) copy-start(bf16[400,128]{1,0:T(8,128)(2,1)} %get-tuple-element.18.refs_0_.x_ref) | copy-start | bytes 307204
  2.4 16.7 %collective-permute-start = (bf16[400,128]{1,0:T(8,128)(2,1)}, bf16[400,128]{1,0:T(8,128)(2,1)S(1)}, u32[]{:S(2)}, u32[]{:S(2)}) collective-permute-start(bf16[400,128]{1,0:T(8,128)(2,1)} %get-tuple-element.18.refs_0_.x_ref), channel_id=1, source_target_pairs={{0,1},{1,0},{2,3},{3,2},{4,5},{5,4},{6,7},{7,6},{8,9},{9,8},{10,11... | collective-permute-start | bytes 307208 | tf_op jit(solution)/shard_map/ppermute | solution.py:278
  5.4 13.7 %collective-permute-start.1 = (bf16[400,128]{1,0:T(8,128)(2,1)}, bf16[400,128]{1,0:T(8,128)(2,1)S(1)}, u32[]{:S(2)}, u32[]{:S(2)}) collective-permute-start(bf16[400,128]{1,0:T(8,128)(2,1)} %get-tuple-element.18.refs_0_.x_ref), channel_id=1, source_target_pairs={{0,2},{1,3},{2,0},{3,1},{4,6},{5,7},{6,4},{7,5},{8,10},{9,11},{10,... | collective-permute-start | bytes 307208 | tf_op jit(solution)/shard_map/ppermute | solution.py:278
  8.0 11.8 %collective-permute-start.2 = (bf16[400,128]{1,0:T(8,128)(2,1)}, bf16[400,128]{1,0:T(8,128)(2,1)S(1)}, u32[]{:S(2)}, u32[]{:S(2)}) collective-permute-start(bf16[400,128]{1,0:T(8,128)(2,1)} %get-tuple-element.18.refs_0_.x_ref), channel_id=1, source_target_pairs={{0,3},{1,2},{2,1},{3,0},{4,7},{5,6},{6,5},{7,4},{8,11},{9,10},{10,... | collective-permute-start | bytes 307208 | tf_op jit(solution)/shard_map/ppermute | solution.py:278
  19.0 0.7 %copy-start.13 = (bf16[8,3,48,128]{3,2,1,0:T(8,128)(2,1)}, bf16[8,3,48,128]{3,2,1,0:T(8,128)(2,1)S(1)}, u32[]{:S(2)}) copy-start(bf16[8,3,48,128]{3,2,1,0:T(8,128)(2,1)S(1)} %get-tuple-element.29.adjoint_ref) | copy-start | bytes 884740
  19.0 0.7 %copy-start.6 = (bf16[400,128]{1,0:T(8,128)(2,1)}, bf16[400,128]{1,0:T(8,128)(2,1)S(1)}, u32[]{:S(2)}) copy-start(bf16[400,128]{1,0:T(8,128)(2,1)S(1)} %collective-permute-done.1.refs_2_) | copy-start | bytes 307204
  19.8 0.6 %copy-start.9 = (bf16[400,128]{1,0:T(8,128)(2,1)}, bf16[400,128]{1,0:T(8,128)(2,1)S(1)}, u32[]{:S(2)}) copy-start(bf16[400,128]{1,0:T(8,128)(2,1)S(1)} %collective-permute-done.2.refs_3_) | copy-start | bytes 307204
  20.4 0.9 %copy-start.2 = (bf16[400,128]{1,0:T(8,128)(2,1)S(1)}, bf16[400,128]{1,0:T(8,128)(2,1)}, u32[]{:S(2)}) copy-start(bf16[400,128]{1,0:T(8,128)(2,1)} %get-tuple-element.18.refs_0_.x_ref) | copy-start | bytes 307204
  21.3 0.9 %copy-start.7 = (bf16[400,128]{1,0:T(8,128)(2,1)S(1)}, bf16[400,128]{1,0:T(8,128)(2,1)}, u32[]{:S(2)}) copy-start(bf16[400,128]{1,0:T(8,128)(2,1)} %copy-done.6) | copy-start | bytes 307204
  22.2 0.9 %copy-start.10 = (bf16[400,128]{1,0:T(8,128)(2,1)S(1)}, bf16[400,128]{1,0:T(8,128)(2,1)}, u32[]{:S(2)}) copy-start(bf16[400,128]{1,0:T(8,128)(2,1)} %copy-done.9) | copy-start | bytes 307204
  23.1 0.7 %copy-start.12 = (s32[8]{0:T(128)S(1)}, s32[8]{0:T(128)}, u32[]{:S(2)}) copy-start(s32[8]{0:T(128)} %slot_hbm.1) | copy-start | bytes 100
  26.8 0.8 %copy-start.1 = (bf16[2048,128]{1,0:T(8,128)(2,1)}, bf16[2048,128]{1,0:T(8,128)(2,1)S(1)}, u32[]{:S(2)}) copy-start(bf16[2048,128]{1,0:T(8,128)(2,1)S(1)} %get-tuple-element.19) | copy-start | bytes 1572868
  27.6 13.9 %all-to-all-start.1 = ((bf16[8,256,128]{2,1,0:T(8,128)(2,1)}), bf16[8,256,128]{2,1,0:T(8,128)(2,1)}, u32[]{:S(2)}, u32[]{:S(2)}) async-start(bf16[8,256,128]{2,1,0:T(8,128)(2,1)} %bitcast.11), calls=%async_computation.1 | async-start | bytes 1048576 | tf_op jit(solution)/shard_map/all_to_all | solution.py:314
  31.7 0.9 %copy-start.8 = (bf16[400,128]{1,0:T(8,128)(2,1)S(1)}, bf16[400,128]{1,0:T(8,128)(2,1)}, u32[]{:S(2)}) copy-start(bf16[400,128]{1,0:T(8,128)(2,1)} %copy-done.6) | copy-start | bytes 307204
  32.6 0.9 %copy-start.11 = (bf16[400,128]{1,0:T(8,128)(2,1)S(1)}, bf16[400,128]{1,0:T(8,128)(2,1)}, u32[]{:S(2)}) copy-start(bf16[400,128]{1,0:T(8,128)(2,1)} %copy-done.9) | copy-start | bytes 307204
  35.4 0.7 %copy-start.4 = (f32[400,128]{1,0:T(8,128)}, f32[400,128]{1,0:T(8,128)S(1)}, u32[]{:S(2)}) copy-start(f32[400,128]{1,0:T(8,128)S(1)} %get-tuple-element.21.refs_0_) | copy-start | bytes 614404
  36.1 15.8 %collective-permute-start.3 = (bf16[400,128]{1,0:T(8,128)(2,1)}, bf16[400,128]{1,0:T(8,128)(2,1)S(1)}, u32[]{:S(2)}, u32[]{:S(2)}) collective-permute-start(bf16[400,128]{1,0:T(8,128)(2,1)} %get-tuple-element.22), channel_id=1, source_target_pairs={{0,1},{1,0},{2,3},{3,2},{4,5},{5,4},{6,7},{7,6},{8,9},{9,8},{10,11... | collective-permute-start | bytes 307208 | tf_op jit(solution)/shard_map/ppermute | solution.py:334
  36.8 15.1 %collective-permute-start.4 = (bf16[400,128]{1,0:T(8,128)(2,1)}, bf16[400,128]{1,0:T(8,128)(2,1)S(1)}, u32[]{:S(2)}, u32[]{:S(2)}) collective-permute-start(bf16[400,128]{1,0:T(8,128)(2,1)} %get-tuple-element.23), channel_id=1, source_target_pairs={{0,2},{1,3},{2,0},{3,1},{4,6},{5,7},{6,4},{7,5},{8,10},{9,11},{10,... | collective-permute-start | bytes 307208 | tf_op jit(solution)/shard_map/ppermute | solution.py:334
  40.3 11.6 %collective-permute-start.5 = (bf16[400,128]{1,0:T(8,128)(2,1)}, bf16[400,128]{1,0:T(8,128)(2,1)S(1)}, u32[]{:S(2)}, u32[]{:S(2)}) collective-permute-start(bf16[400,128]{1,0:T(8,128)(2,1)} %get-tuple-element.24), channel_id=1, source_target_pairs={{0,3},{1,2},{2,1},{3,0},{4,7},{5,6},{6,5},{7,4},{8,11},{9,10},{10,... | collective-permute-start | bytes 307208 | tf_op jit(solution)/shard_map/ppermute | solution.py:334
  51.9 0.9 %copy-start.5 = (f32[400,128]{1,0:T(8,128)S(1)}, f32[400,128]{1,0:T(8,128)}, u32[]{:S(2)}) copy-start(f32[400,128]{1,0:T(8,128)} %copy-done.4) | copy-start | bytes 614404

commit v12 on v9

--- a/solution.py
+++ b/solution.py
@@ -101,7 +101,7 @@
     payload_ref[pl.ds(frames * group, 16), :] = gain_rows[...].astype(jnp.bfloat16)
 
 
-def window_kernel(frames, group, slot_ref, adjoint_ref, windows, place):
+def build_windows(frames, group, slot_ref, adjoint_ref, windows, place):
     width = adjoint_ref.shape[-1]
     for slot in range(frames):
         place[slot_ref[slot]] = slot
@@ -127,12 +127,14 @@
                             pl.ds((a * 9 + b * 3 + c) * group, group), pl.ds(t * width, width)
                         ] = shifted
 
-def grad_kernel(frames, group, factor, at_ref, windows, *refs):
-    groups = len(refs) - 2
+
+def grad_kernel(frames, group, factor, at_ref, slot_ref, adjoint_ref, *refs):
+    groups = len(refs) - 4
     x_refs = refs[:groups]
-    grad_ref, hidden = refs[groups:]
+    grad_ref, place, windows, hidden = refs[groups:]
     ins = groups * group
-    width = windows.shape[1] // frames
+    width = adjoint_ref.shape[-1]
+    build_windows(frames, group, slot_ref, adjoint_ref, windows, place)
     gain = gains(x_refs, frames * group, group)
     for t in range(frames):
         scale, scaled = norm(x_refs, t, group)
@@ -168,11 +170,12 @@
         grad_ref[pl.ds(base, tail), :] = jnp.zeros((tail, 128), jnp.bfloat16)
 
 
-def part_kernel(frames, group, at_ref, weight_ref, windows, *refs):
-    groups = (len(refs) - 1) // 2
+def part_kernel(frames, group, at_ref, slot_ref, adjoint_ref, weight_ref, *refs):
+    groups = (len(refs) - 3) // 2
     x_refs = refs[:groups]
     part_refs = refs[groups : 2 * groups]
-    product = refs[2 * groups]
+    place, windows, product = refs[2 * groups :]
+    build_windows(frames, group, slot_ref, adjoint_ref, windows, place)
     width = part_refs[0].shape[-1]
     product[...] = lax.dot_general(
         weight_ref[...], windows[...], (((0,), (0,)), ((), ())), preferred_element_type=jnp.float32
@@ -276,25 +279,20 @@
 
     packed_rows = packing(taps_out, ins, count)[3]
     factor = float(frames * count * width) ** (-0.5)
-    windows = pl.pallas_call(
-        functools.partial(window_kernel, frames, group),
-        out_shape=jax.ShapeDtypeStruct((taps_out, pixels), jnp.bfloat16),
-        in_specs=[smem(), copied()],
-        out_specs=vmem(),
-        scratch_shapes=[pltpu.SMEM((frames,), jnp.int32)],
-        compiler_params=limit(taps_out, pixels),
-        name="window_kernel",
-    )(frame_slot, strips)
     packed = pl.pallas_call(
         functools.partial(grad_kernel, frames, group, factor),
         out_shape=jax.ShapeDtypeStruct((packed_rows, 128), jnp.bfloat16),
-        in_specs=[smem(), vmem()] + [copied()] * groups,
+        in_specs=[smem(), smem(), copied()] + [copied()] * groups,
         out_specs=vmem(),
-        scratch_shapes=[pltpu.VMEM((ins, pixels), jnp.bfloat16)],
+        scratch_shapes=[
+            pltpu.SMEM((frames,), jnp.int32),
+            pltpu.VMEM((taps_out, pixels), jnp.bfloat16),
+            pltpu.VMEM((ins, pixels), jnp.bfloat16),
+        ],
         compiler_params=limit(taps_out, pixels),
         cost_estimate=cost(taps_out, ins, pixels),
         name="grad_kernel",
-    )(at, windows, *everything)
+    )(at, frame_slot, strips, *everything)
 
     pieces = lax.all_to_all(
         packed.reshape(count, packed_rows // count, 128),
@@ -308,13 +306,17 @@
             [jax.ShapeDtypeStruct((frames * (group + 2), width), jnp.float32)]
             + [jax.ShapeDtypeStruct((sent, width), jnp.bfloat16)] * (groups - 1)
         ),
-        in_specs=[smem(), vmem(), vmem()] + [copied()] * groups,
+        in_specs=[smem(), smem(), copied(), copied()] + [copied()] * groups,
         out_specs=(vmem(),) * groups,
-        scratch_shapes=[pltpu.VMEM((ins, pixels), jnp.float32)],
+        scratch_shapes=[
+            pltpu.SMEM((frames,), jnp.int32),
+            pltpu.VMEM((taps_out, pixels), jnp.bfloat16),
+            pltpu.VMEM((ins, pixels), jnp.float32),
+        ],
         compiler_params=limit(taps_out, pixels),
         cost_estimate=cost(taps_out, ins, pixels),
         name="part_kernel",
-    )(at, kernel, windows, *everything)
+    )(at, frame_slot, strips, kernel, *everything)
 
     arrived = [lax.ppermute(parts[s], "chan", partners[s]) for s in range(1, groups)]
     summed = jnp.sum(pieces.astype(jnp.float32), axis=0).astype(jnp.bfloat16)

time: 50.2 us -> 46.4 us (0.924)
  Pallas kernels: 9.73 us -> 7.79 us
  local copies, waits for them, and re-layouts: 2.29 us -> 0.92 us
  waiting for transfers between devices: 1.81 us -> 3.09 us
  other arithmetic: 1.12 us -> 0.07 us
  starting transfers between devices: 14.2 us -> 13.6 us
    unnamed x10 -> x8, local copies, waits for them, and re-layouts: 2.27 us -> 0.9 us
    all_to_all x1, waiting for transfers between devices: 1.8 us -> 3.08 us  [shards(): lax.all_to_all(packed.reshape(count, packed_rows // count, 128), 'rows',...]
    reduce_sum x1, other arithmetic: 1.12 us -> 0.07 us  [shards(): summed = jnp.sum(pieces.astype(jnp.float32), axis=0).astype(jnp.bfloat16)]
    pallas_call x1 -> x0, Pallas kernels: 0.93 us -> none  [shards(): pl.pallas_call(functools.partial(window_kernel, frames, group), out_shape...]
    pallas_call x1, Pallas kernels: 2.86 us -> 2.09 us  [shards(): pl.pallas_call(functools.partial(part_kernel, frames, group), out_shape=t...]
    all_to_all x1, starting transfers between devices: 4.14 us -> 3.49 us  [shards(): lax.all_to_all(packed.reshape(count, packed_rows // count, 128), 'rows',...]
  transfers between devices with their start and end apart: 7 -> 7, of which waited for: 1 -> 1; matrix products, arithmetic and copies ran while one was open for 2% -> 0% of each run, Pallas kernels for 8% -> 5%
where the time goes in v12:
time: 46.4 us; the launch traced here: 46.1 us
  blocking collectives  19.9 us (43%)
  starting transfers between devices  13.6 us (29%)
  Pallas kernels  7.79 us (17%)
  waiting for transfers between devices  3.09 us (7%)
  local copies, waits for them, and re-layouts  0.92 us (2%)
  between operations  0.7 us (2%)
    all_to_all x1, blocking collectives, shards(): lax.all_to_all(rows, 'rows', split_axis=0, concat_axis=0, tiled=True)  11 us
    all_gather x1, blocking collectives, shards(): whole = lax.all_gather(summed, 'rows', axis=0, tiled=True)  8.9 us
    ppermute x3, starting transfers between devices, shards(): lax.ppermute(payload, 'chan', partners[s])  5.62 us
    ppermute x3, starting transfers between devices, shards(): lax.ppermute(parts[s], 'chan', partners[s])  4.48 us
    all_to_all x1, starting transfers between devices, shards(): lax.all_to_all(packed.reshape(count, packed_rows // count, 128), 'rows',...  3.49 us
    all_to_all x1, waiting for transfers between devices, shards(): lax.all_to_all(packed.reshape(count, packed_rows // count, 128), 'rows',...  3.08 us
    pallas_call x1, Pallas kernels, shards(): pl.pallas_call(functools.partial(grad_kernel, frames, group, factor), out...  2.81 us
    pallas_call x1, Pallas kernels, shards(): pl.pallas_call(functools.partial(part_kernel, frames, group), out_shape=t...  2.09 us
  transfers between devices with their start and end apart: 7, of which 1 were waited for; matrix products, arithmetic and copies ran while one was open for 0% of the time, Pallas kernels for 5%

profile of v12, /device:TPU:0, one launch (start us, length us, event | category | flops | bytes accessed | tf_op | source)
XLA Modules:
  0.0 46.1 jit_solution(15063227685703834833)
XLA Ops:
  0.6 1.6 %prepare_kernel.1 = (bf16[8,3,48,128]{3,2,1,0:T(8,128)(2,1)S(1)}, bf16[400,128]{1,0:T(8,128)(2,1)}) custom-call(bf16[48,8,128]{2,1,0:T(8,128)(2,1)} %bitcast.11, bf16[8,48,128]{2,1,0:T(8,128)(2,1)} %bitcast.12, f32[1,48]{1,0:T(1,128)} %bitcast.13), custom_call_target="tpu_custom_call" | custom-call | tf_op jit(solution)/shard_map/prepare_kernel/pallas_call | solution.py:249
  2.3 5.0 %collective-permute-start.2 = (bf16[400,128]{1,0:T(8,128)(2,1)}, bf16[400,128]{1,0:T(8,128)(2,1)S(1)}, u32[]{:S(2)}, u32[]{:S(2)}) collective-permute-start(bf16[400,128]{1,0:T(8,128)(2,1)} %get-tuple-element.16.refs_0_.x_ref), channel_id=1, source_target_pairs={{0,3},{1,2},{2,1},{3,0},{4,7},{5,6},{6,5},{7,4},{8,11},{9,10},{10,... | collective-permute-start | bytes 307208 | tf_op jit(solution)/shard_map/ppermute | solution.py:266
  7.3 0.0 collective-permute-start.1
  7.3 0.6 %collective-permute-start = (bf16[400,128]{1,0:T(8,128)(2,1)}, bf16[400,128]{1,0:T(8,128)(2,1)S(1)}, u32[]{:S(2)}, u32[]{:S(2)}) collective-permute-start(bf16[400,128]{1,0:T(8,128)(2,1)} %get-tuple-element.16.refs_0_.x_ref), channel_id=1, source_target_pairs={{0,1},{1,0},{2,3},{3,2},{4,5},{5,4},{6,7},{7,6},{8,9},{9,8},{10,11... | collective-permute-start | bytes 307208 | tf_op jit(solution)/shard_map/ppermute | solution.py:266
  7.9 11.1 %conditional.1 = (bf16[8,3,48,128]{3,2,1,0:T(8,128)(2,1)S(1)}) conditional(s32[]{:T(128)} %convert_element_type.2, bf16[8,3,48,128]{3,2,1,0:T(8,128)(2,1)S(1)} %get-tuple-element.15, bf16[8,3,48,128]{3,2,1,0:T(8,128)(2,1)S(1)} %get-tuple-element.15), branch_computations={%region_0.0_spmd, %region_1.0_spmd} | conditional | bytes 1179656 | solution.py:268
  7.9 11.0 %all_to_all.9 = bf16[8,3,48,128]{3,2,1,0:T(8,128)(2,1)S(1)} all-to-all(bf16[8,3,48,128]{3,2,1,0:T(8,128)(2,1)S(1)} %copy.10), channel_id=1, replica_groups=mesh['rows'=8,'chan'=4] {'rows'}, dimensions={0} | all-to-all | bytes 589824 | tf_op jit(solution)/shard_map/cond/branch_1_fun/all_to_all | solution.py:270
  19.0 0.0 collective-permute-done.2.refs_3_
  19.0 0.0 collective-permute-done.1.refs_2_
  19.0 0.0 collective-permute-done.refs_1_
  19.0 0.9 %copy-done = bf16[400,128]{1,0:T(8,128)(2,1)S(1)} copy-done((bf16[400,128]{1,0:T(8,128)(2,1)S(1)}, bf16[400,128]{1,0:T(8,128)(2,1)}, u32[]{:S(2)}) %copy-start) | copy-done | bytes 102424
  19.9 2.8 %grad_kernel.1 = bf16[2048,128]{1,0:T(8,128)(2,1)} custom-call(s32[1]{0:T(128)} %bitcast.at_ref, s32[8]{0:T(128)S(1)} %copy-done.3, bf16[8,3,48,128]{3,2,1,0:T(8,128)(2,1)S(1)} %get-tuple-element.25.adjoint_ref, bf16[400,128]{1,0:T(8,128)(2,1)S(1)} %copy-done, bf16[400,128]{1,0:T(8,128)(2,1)S(1)} %collective-permute-done.refs_1_, ...), custom_call_target="tpu_custom_call" | custom-call | flops 509607936 | bytes 3047424 | tf_op jit(solution)/shard_map/grad_kernel/pallas_call | solution.py:282
  22.7 3.5 %all-to-all-start.1 = ((bf16[8,256,128]{2,1,0:T(8,128)(2,1)}), bf16[8,256,128]{2,1,0:T(8,128)(2,1)S(1)}, u32[]{:S(2)}, u32[]{:S(2)}) async-start(bf16[8,256,128]{2,1,0:T(8,128)(2,1)} %bitcast.4), calls=%async_computation.1 | async-start | bytes 1048576 | tf_op jit(solution)/shard_map/all_to_all | solution.py:297
  26.2 0.0 copy-done.1
  26.2 2.1 %part_kernel.1 = (f32[400,128]{1,0:T(8,128)S(1)}, bf16[400,128]{1,0:T(8,128)(2,1)S(1)}, bf16[400,128]{1,0:T(8,128)(2,1)S(1)}, bf16[400,128]{1,0:T(8,128)(2,1)S(1)}) custom-call(s32[1]{0:T(128)} %bitcast.at_ref, s32[8]{0:T(128)S(1)} %copy-done.3, bf16[8,3,48,128]{3,2,1,0:T(8,128)(2,1)S(1)} %get-tuple-element.25.adjoint_ref, bf16[1296,192]{1,0:T(8,128)(2,1)S(1)} %bitcast.10, ...), custom_call_target="tpu_custom_call" | custom-call | flops 509607936 | bytes 3047424 | tf_op jit(solution)/shard_map/part_kernel/pallas_call | solution.py:303
  28.3 1.3 %collective-permute-start.3 = (bf16[400,128]{1,0:T(8,128)(2,1)S(1)}, bf16[400,128]{1,0:T(8,128)(2,1)S(1)}, u32[]{:S(2)}, u32[]{:S(2)}) collective-permute-start(bf16[400,128]{1,0:T(8,128)(2,1)S(1)} %get-tuple-element.18), channel_id=1, source_target_pairs={{0,1},{1,0},{2,3},{3,2},{4,5},{5,4},{6,7},{7,6},{8,9},{9,8},{10,11... | collective-permute-start | bytes 307208 | tf_op jit(solution)/shard_map/ppermute | solution.py:321
  29.6 2.9 %collective-permute-start.4 = (bf16[400,128]{1,0:T(8,128)(2,1)S(1)}, bf16[400,128]{1,0:T(8,128)(2,1)S(1)}, u32[]{:S(2)}, u32[]{:S(2)}) collective-permute-start(bf16[400,128]{1,0:T(8,128)(2,1)S(1)} %get-tuple-element.19), channel_id=1, source_target_pairs={{0,2},{1,3},{2,0},{3,1},{4,6},{5,7},{6,4},{7,5},{8,10},{9,11},{10,... | collective-permute-start | bytes 307208 | tf_op jit(solution)/shard_map/ppermute | solution.py:321
  32.6 0.2 collective-permute-start.5
  32.8 3.1 %all-to-all-done.1 = bf16[8,256,128]{2,1,0:T(8,128)(2,1)S(1)} async-done(((bf16[8,256,128]{2,1,0:T(8,128)(2,1)}), bf16[8,256,128]{2,1,0:T(8,128)(2,1)S(1)}, u32[]{:S(2)}, u32[]{:S(2)}) %all-to-all-start.1) | async-done | bytes 524320 | tf_op jit(solution)/shard_map/all_to_all | solution.py:297
  35.9 0.1 reduce_sum.12
  36.0 8.9 %all_gather.3.packed_ref = bf16[2048,128]{1,0:T(8,128)(2,1)S(1)} all-gather(bf16[256,128]{1,0:T(8,128)(2,1)S(1)} %reduce_sum.12), channel_id=1, replica_groups=mesh['rows'=8,'chan'=4] {'rows'}, dimensions={0}, use_global_device_ids=true | all-gather | bytes 589824 | tf_op jit(solution)/shard_map/all_gather | solution.py:323
  44.9 0.0 collective-permute-done.3.refs_1_
  44.9 0.0 collective-permute-done.4.refs_2_
  44.9 0.0 collective-permute-done.5.refs_3_
  44.9 1.2 %finish_kernel.1 = (bf16[8,48,128]{2,1,0:T(8,128)(2,1)}, f32[1296,192]{1,0:T(8,128)}) custom-call(bf16[2048,128]{1,0:T(8,128)(2,1)S(1)} %all_gather.3.packed_ref, bf16[400,128]{1,0:T(8,128)(2,1)S(1)} %copy-done.1, f32[400,128]{1,0:T(8,128)S(1)} %get-tuple-element.17.refs_0_, bf16[400,128]{1,0:T(8,128)(2,1)S(1)} %collective-permute-done.3.refs_1_, ...), custom_call_target="tpu_custom_call" | custom-call | tf_op jit(solution)/shard_map/finish_kernel/pallas_call | solution.py:324
  (7 shorter events, 0.0 us)
Async XLA Ops:
  0.6 18.3 %copy-start.3 = (s32[8]{0:T(128)S(1)}, s32[8]{0:T(128)}, u32[]{:S(2)}) copy-start(s32[8]{0:T(128)} %slot_ref.3) | copy-start | bytes 100
  2.3 16.7 %collective-permute-start.2 = (bf16[400,128]{1,0:T(8,128)(2,1)}, bf16[400,128]{1,0:T(8,128)(2,1)S(1)}, u32[]{:S(2)}, u32[]{:S(2)}) collective-permute-start(bf16[400,128]{1,0:T(8,128)(2,1)} %get-tuple-element.16.refs_0_.x_ref), channel_id=1, source_target_pairs={{0,3},{1,2},{2,1},{3,0},{4,7},{5,6},{6,5},{7,4},{8,11},{9,10},{10,... | collective-permute-start | bytes 307208 | tf_op jit(solution)/shard_map/ppermute | solution.py:266
  7.3 11.6 %collective-permute-start.1 = (bf16[400,128]{1,0:T(8,128)(2,1)}, bf16[400,128]{1,0:T(8,128)(2,1)S(1)}, u32[]{:S(2)}, u32[]{:S(2)}) collective-permute-start(bf16[400,128]{1,0:T(8,128)(2,1)} %get-tuple-element.16.refs_0_.x_ref), channel_id=1, source_target_pairs={{0,2},{1,3},{2,0},{3,1},{4,6},{5,7},{6,4},{7,5},{8,10},{9,11},{10,... | collective-permute-start | bytes 307208 | tf_op jit(solution)/shard_map/ppermute | solution.py:266
  7.3 11.6 %collective-permute-start = (bf16[400,128]{1,0:T(8,128)(2,1)}, bf16[400,128]{1,0:T(8,128)(2,1)S(1)}, u32[]{:S(2)}, u32[]{:S(2)}) collective-permute-start(bf16[400,128]{1,0:T(8,128)(2,1)} %get-tuple-element.16.refs_0_.x_ref), channel_id=1, source_target_pairs={{0,1},{1,0},{2,3},{3,2},{4,5},{5,4},{6,7},{7,6},{8,9},{9,8},{10,11... | collective-permute-start | bytes 307208 | tf_op jit(solution)/shard_map/ppermute | solution.py:266
  19.0 0.9 %copy-start = (bf16[400,128]{1,0:T(8,128)(2,1)S(1)}, bf16[400,128]{1,0:T(8,128)(2,1)}, u32[]{:S(2)}) copy-start(bf16[400,128]{1,0:T(8,128)(2,1)} %get-tuple-element.16.refs_0_.x_ref) | copy-start | bytes 307204
  19.9 6.3 %copy-start.1 = (bf16[400,128]{1,0:T(8,128)(2,1)S(1)}, bf16[400,128]{1,0:T(8,128)(2,1)}, u32[]{:S(2)}) copy-start(bf16[400,128]{1,0:T(8,128)(2,1)} %get-tuple-element.16.refs_0_.x_ref) | copy-start | bytes 307204
  19.9 6.3 %copy-start.2 = (bf16[27,48,192]{2,1,0:T(8,128)(2,1)S(1)}, bf16[27,48,192]{2,1,0:T(8,128)(2,1)}, u32[]{:S(2)}) copy-start(bf16[27,48,192]{2,1,0:T(8,128)(2,1)} %param.11) | copy-start | bytes 1492996
  22.7 13.2 %all-to-all-start.1 = ((bf16[8,256,128]{2,1,0:T(8,128)(2,1)}), bf16[8,256,128]{2,1,0:T(8,128)(2,1)S(1)}, u32[]{:S(2)}, u32[]{:S(2)}) async-start(bf16[8,256,128]{2,1,0:T(8,128)(2,1)} %bitcast.4), calls=%async_computation.1 | async-start | bytes 1048576 | tf_op jit(solution)/shard_map/all_to_all | solution.py:297
  28.3 16.5 %collective-permute-start.3 = (bf16[400,128]{1,0:T(8,128)(2,1)S(1)}, bf16[400,128]{1,0:T(8,128)(2,1)S(1)}, u32[]{:S(2)}, u32[]{:S(2)}) collective-permute-start(bf16[400,128]{1,0:T(8,128)(2,1)S(1)} %get-tuple-element.18), channel_id=1, source_target_pairs={{0,1},{1,0},{2,3},{3,2},{4,5},{5,4},{6,7},{7,6},{8,9},{9,8},{10,11... | collective-permute-start | bytes 307208 | tf_op jit(solution)/shard_map/ppermute | solution.py:321
  29.6 15.2 %collective-permute-start.4 = (bf16[400,128]{1,0:T(8,128)(2,1)S(1)}, bf16[400,128]{1,0:T(8,128)(2,1)S(1)}, u32[]{:S(2)}, u32[]{:S(2)}) collective-permute-start(bf16[400,128]{1,0:T(8,128)(2,1)S(1)} %get-tuple-element.19), channel_id=1, source_target_pairs={{0,2},{1,3},{2,0},{3,1},{4,6},{5,7},{6,4},{7,5},{8,10},{9,11},{10,... | collective-permute-start | bytes 307208 | tf_op jit(solution)/shard_map/ppermute | solution.py:321
  32.6 12.3 %collective-permute-start.5 = (bf16[400,128]{1,0:T(8,128)(2,1)S(1)}, bf16[400,128]{1,0:T(8,128)(2,1)S(1)}, u32[]{:S(2)}, u32[]{:S(2)}) collective-permute-start(bf16[400,128]{1,0:T(8,128)(2,1)S(1)} %get-tuple-element.20), channel_id=1, source_target_pairs={{0,3},{1,2},{2,1},{3,0},{4,7},{5,6},{6,5},{7,4},{8,11},{9,10},{10,... | collective-permute-start | bytes 307208 | tf_op jit(solution)/shard_map/ppermute | solution.py:321

commit v13 on v12

--- a/solution.py
+++ b/solution.py
@@ -46,9 +46,11 @@
     )
 
 
-def gains(x_refs, start, group):
-    found = []
-    for ref in x_refs:
+def gains(gain_ref, line, x_refs, start, group):
+    line[...] = jnp.zeros_like(line)
+    line[pl.ds(0, 1), pl.ds(0, gain_ref.shape[1])] = gain_ref[...]
+    found = [jnp.transpose(jnp.broadcast_to(line[pl.ds(0, 1), :], (128, 128)))[:group]]
+    for ref in x_refs[1:]:
         rows = ref[pl.ds(start, 16), :].astype(jnp.float32)
         gain = rows[0:1] + rows[1:2] + rows[2:3]
         found.append(jnp.transpose(jnp.broadcast_to(gain, (128, 128)))[:group])
@@ -128,14 +130,14 @@
                         ] = shifted
 
 
-def grad_kernel(frames, group, factor, at_ref, slot_ref, adjoint_ref, *refs):
-    groups = len(refs) - 4
+def grad_kernel(frames, group, factor, at_ref, slot_ref, gain_ref, adjoint_ref, *refs):
+    groups = len(refs) - 5
     x_refs = refs[:groups]
-    grad_ref, place, windows, hidden = refs[groups:]
+    grad_ref, place, line, windows, hidden = refs[groups:]
     ins = groups * group
     width = adjoint_ref.shape[-1]
     build_windows(frames, group, slot_ref, adjoint_ref, windows, place)
-    gain = gains(x_refs, frames * group, group)
+    gain = gains(gain_ref, line, x_refs, frames * group, group)
     for t in range(frames):
         scale, scaled = norm(x_refs, t, group)
         for s in range(groups):
@@ -170,17 +172,17 @@
         grad_ref[pl.ds(base, tail), :] = jnp.zeros((tail, 128), jnp.bfloat16)
 
 
-def part_kernel(frames, group, at_ref, slot_ref, adjoint_ref, weight_ref, *refs):
-    groups = (len(refs) - 3) // 2
+def part_kernel(frames, group, at_ref, slot_ref, gain_ref, adjoint_ref, weight_ref, *refs):
+    groups = (len(refs) - 4) // 2
     x_refs = refs[:groups]
     part_refs = refs[groups : 2 * groups]
-    place, windows, product = refs[2 * groups :]
+    place, line, windows, product = refs[2 * groups :]
     build_windows(frames, group, slot_ref, adjoint_ref, windows, place)
     width = part_refs[0].shape[-1]
     product[...] = lax.dot_general(
         weight_ref[...], windows[...], (((0,), (0,)), ((), ())), preferred_element_type=jnp.float32
     )
-    gain = gains(x_refs, frames * group, group)
+    gain = gains(gain_ref, line, x_refs, frames * group, group)
     shares = []
     for t in range(frames):
         scale, scaled = norm(x_refs, t, group)
@@ -262,7 +264,9 @@
         name="prepare_kernel",
     )(frame_adjoint[0], inputs[:, :, 0], gain.reshape(1, channels))
     partners = [[(z, z ^ s) for z in range(groups)] for s in range(groups)]
-    everything = [payload] + [
+    own = jnp.pad(inputs[:, :, 0], ((0, 0), (0, spare), (0, 0))).reshape(frames * group, width)
+    gain_line = gain.reshape(1, channels)
+    everything = [own] + [
         lax.ppermute(payload, "chan", partners[s]) for s in range(1, groups)
     ]
     strips = lax.cond(
@@ -282,17 +286,18 @@
     packed = pl.pallas_call(
         functools.partial(grad_kernel, frames, group, factor),
         out_shape=jax.ShapeDtypeStruct((packed_rows, 128), jnp.bfloat16),
-        in_specs=[smem(), smem(), copied()] + [copied()] * groups,
+        in_specs=[smem(), smem()] + [copied()] * (groups + 2),
         out_specs=vmem(),
         scratch_shapes=[
             pltpu.SMEM((frames,), jnp.int32),
+            pltpu.VMEM((8, 128), jnp.float32),
             pltpu.VMEM((taps_out, pixels), jnp.bfloat16),
             pltpu.VMEM((ins, pixels), jnp.bfloat16),
         ],
         compiler_params=limit(taps_out, pixels),
         cost_estimate=cost(taps_out, ins, pixels),
         name="grad_kernel",
-    )(at, frame_slot, strips, *everything)
+    )(at, frame_slot, gain_line, strips, *everything)
 
     pieces = lax.all_to_all(
         packed.reshape(count, packed_rows // count, 128),
@@ -306,17 +311,18 @@
             [jax.ShapeDtypeStruct((frames * (group + 2), width), jnp.float32)]
             + [jax.ShapeDtypeStruct((sent, width), jnp.bfloat16)] * (groups - 1)
         ),
-        in_specs=[smem(), smem(), copied(), copied()] + [copied()] * groups,
+        in_specs=[smem(), smem()] + [copied()] * (groups + 3),
         out_specs=(vmem(),) * groups,
         scratch_shapes=[
             pltpu.SMEM((frames,), jnp.int32),
+            pltpu.VMEM((8, 128), jnp.float32),
             pltpu.VMEM((taps_out, pixels), jnp.bfloat16),
             pltpu.VMEM((ins, pixels), jnp.float32),
         ],
         compiler_params=limit(taps_out, pixels),
         cost_estimate=cost(taps_out, ins, pixels),
         name="part_kernel",
-    )(at, frame_slot, strips, kernel, *everything)
+    )(at, frame_slot, gain_line, strips, kernel, *everything)
 
     arrived = [lax.ppermute(parts[s], "chan", partners[s]) for s in range(1, groups)]
     summed = jnp.sum(pieces.astype(jnp.float32), axis=0).astype(jnp.bfloat16)
@@ -331,7 +337,7 @@
         out_specs=(vmem(), vmem()),
         compiler_params=limit(taps_out, pixels),
         name="finish_kernel",
-    )(whole, payload, parts[0], *arrived)
+    )(whole, own, parts[0], *arrived)
     grad = grad.reshape(27, group, groups, group)[:, :channels, :, :channels]
     return (
         input_adjoint[:, :channels, None, :],

time: 46.4 us -> 45.6 us (0.983)
  local copies, waits for them, and re-layouts: 0.92 us -> 0.04 us
    unnamed x8, local copies, waits for them, and re-layouts: 0.9 us -> 0.02 us
where the time goes in v13:
time: 45.6 us; the launch traced here: 45.3 us
  blocking collectives  19.9 us (44%)
  starting transfers between devices  13.6 us (30%)
  Pallas kernels  7.87 us (17%)
  waiting for transfers between devices  3.09 us (7%)
  between operations  0.72 us (2%)
    all_to_all x1, blocking collectives, shards(): lax.all_to_all(rows, 'rows', split_axis=0, concat_axis=0, tiled=True)  11 us
    all_gather x1, blocking collectives, shards(): whole = lax.all_gather(summed, 'rows', axis=0, tiled=True)  8.9 us
    ppermute x3, starting transfers between devices, shards(): lax.ppermute(payload, 'chan', partners[s])  5.62 us
    ppermute x3, starting transfers between devices, shards(): lax.ppermute(parts[s], 'chan', partners[s])  4.48 us
    all_to_all x1, starting transfers between devices, shards(): lax.all_to_all(packed.reshape(count, packed_rows // count, 128), 'rows',...  3.49 us
    all_to_all x1, waiting for transfers between devices, shards(): lax.all_to_all(packed.reshape(count, packed_rows // count, 128), 'rows',...  3.08 us
    pallas_call x1, Pallas kernels, shards(): pl.pallas_call(functools.partial(grad_kernel, frames, group, factor), out...  2.84 us
    pallas_call x1, Pallas kernels, shards(): pl.pallas_call(functools.partial(part_kernel, frames, group), out_shape=t...  2.1 us
  transfers between devices with their start and end apart: 7, of which 1 were waited for; matrix products, arithmetic and copies ran while one was open for 0% of the time, Pallas kernels for 5%

profile of v13, /device:TPU:0, one launch (start us, length us, event | category | flops | bytes accessed | tf_op | source)
XLA Modules:
  0.0 45.3 jit_solution(13917091097661803033)
XLA Ops:
  0.6 0.0 copy-start
  0.7 1.7 %prepare_kernel.1 = (bf16[8,3,48,128]{3,2,1,0:T(8,128)(2,1)S(1)}, bf16[400,128]{1,0:T(8,128)(2,1)}) custom-call(bf16[48,8,128]{2,1,0:T(8,128)(2,1)} %bitcast.19, bf16[8,48,128]{2,1,0:T(8,128)(2,1)} %bitcast.11, f32[1,48]{1,0:T(1,128)} %bitcast.15), custom_call_target="tpu_custom_call" | custom-call | tf_op jit(solution)/shard_map/prepare_kernel/pallas_call | solution.py:251
  2.4 5.0 %collective-permute-start.2 = (bf16[400,128]{1,0:T(8,128)(2,1)}, bf16[400,128]{1,0:T(8,128)(2,1)S(1)}, u32[]{:S(2)}, u32[]{:S(2)}) collective-permute-start(bf16[400,128]{1,0:T(8,128)(2,1)} %get-tuple-element.16), channel_id=1, source_target_pairs={{0,3},{1,2},{2,1},{3,0},{4,7},{5,6},{6,5},{7,4},{8,11},{9,10},{10,... | collective-permute-start | bytes 307208 | tf_op jit(solution)/shard_map/ppermute | solution.py:270
  7.4 0.0 collective-permute-start.1
  7.4 0.6 %collective-permute-start = (bf16[400,128]{1,0:T(8,128)(2,1)}, bf16[400,128]{1,0:T(8,128)(2,1)S(1)}, u32[]{:S(2)}, u32[]{:S(2)}) collective-permute-start(bf16[400,128]{1,0:T(8,128)(2,1)} %get-tuple-element.16), channel_id=1, source_target_pairs={{0,1},{1,0},{2,3},{3,2},{4,5},{5,4},{6,7},{7,6},{8,9},{9,8},{10,11... | collective-permute-start | bytes 307208 | tf_op jit(solution)/shard_map/ppermute | solution.py:270
  8.0 11.1 %conditional.1 = (bf16[8,3,48,128]{3,2,1,0:T(8,128)(2,1)S(1)}) conditional(s32[]{:T(128)} %convert_element_type.2, bf16[8,3,48,128]{3,2,1,0:T(8,128)(2,1)S(1)} %get-tuple-element.15, bf16[8,3,48,128]{3,2,1,0:T(8,128)(2,1)S(1)} %get-tuple-element.15), branch_computations={%region_0.1_spmd, %region_1.2_spmd} | conditional | bytes 1179656 | solution.py:272
  8.0 11.0 %all_to_all.9 = bf16[8,3,48,128]{3,2,1,0:T(8,128)(2,1)S(1)} all-to-all(bf16[8,3,48,128]{3,2,1,0:T(8,128)(2,1)S(1)} %copy.10), channel_id=1, replica_groups=mesh['rows'=8,'chan'=4] {'rows'}, dimensions={0} | all-to-all | bytes 589824 | tf_op jit(solution)/shard_map/cond/branch_1_fun/all_to_all | solution.py:274
  19.0 0.0 collective-permute-done.2.refs_3_
  19.0 0.0 collective-permute-done.1.refs_2_
  19.0 0.0 collective-permute-done.refs_1_
  19.1 0.0 copy-start.2
  19.1 2.8 %grad_kernel.1 = bf16[2048,128]{1,0:T(8,128)(2,1)} custom-call(s32[1]{0:T(128)} %bitcast.at_ref, s32[8]{0:T(128)S(1)} %copy-done.3, f32[1,48]{1,0:T(1,128)S(1)} %bitcast.16, bf16[8,3,48,128]{3,2,1,0:T(8,128)(2,1)S(1)} %get-tuple-element.25.adjoint_ref, bf16[384,128]{1,0:T(8,128)(2,1)S(1)} %bitcast.12, bf16[400,128]{1,0:T(8,128)(2,1)S(1)} %collective-permute-done.refs_1_, ...), custom_call_target="tpu_custom_call" | custom-call | flops 509607936 | bytes 3047424 | tf_op jit(solution)/shard_map/grad_kernel/pallas_call | solution.py:286
  21.9 3.5 %all-to-all-start.1 = ((bf16[8,256,128]{2,1,0:T(8,128)(2,1)}), bf16[8,256,128]{2,1,0:T(8,128)(2,1)S(1)}, u32[]{:S(2)}, u32[]{:S(2)}) async-start(bf16[8,256,128]{2,1,0:T(8,128)(2,1)} %bitcast.5), calls=%async_computation.1 | async-start | bytes 1048576 | tf_op jit(solution)/shard_map/all_to_all | solution.py:302
  25.4 2.1 %part_kernel.1 = (f32[400,128]{1,0:T(8,128)S(1)}, bf16[400,128]{1,0:T(8,128)(2,1)S(1)}, bf16[400,128]{1,0:T(8,128)(2,1)S(1)}, bf16[400,128]{1,0:T(8,128)(2,1)S(1)}) custom-call(s32[1]{0:T(128)} %bitcast.at_ref, s32[8]{0:T(128)S(1)} %copy-done.3, f32[1,48]{1,0:T(1,128)S(1)} %bitcast.17, bf16[8,3,48,128]{3,2,1,0:T(8,128)(2,1)S(1)} %get-tuple-element.25.adjoint_ref, ...), custom_call_target="tpu_custom_call" | custom-call | flops 509607936 | bytes 3047424 | tf_op jit(solution)/shard_map/part_kernel/pallas_call | solution.py:308
  27.5 1.3 %collective-permute-start.3 = (bf16[400,128]{1,0:T(8,128)(2,1)S(1)}, bf16[400,128]{1,0:T(8,128)(2,1)S(1)}, u32[]{:S(2)}, u32[]{:S(2)}) collective-permute-start(bf16[400,128]{1,0:T(8,128)(2,1)S(1)} %get-tuple-element.18), channel_id=1, source_target_pairs={{0,1},{1,0},{2,3},{3,2},{4,5},{5,4},{6,7},{7,6},{8,9},{9,8},{10,11... | collective-permute-start | bytes 307208 | tf_op jit(solution)/shard_map/ppermute | solution.py:327
  28.9 2.9 %collective-permute-start.4 = (bf16[400,128]{1,0:T(8,128)(2,1)S(1)}, bf16[400,128]{1,0:T(8,128)(2,1)S(1)}, u32[]{:S(2)}, u32[]{:S(2)}) collective-permute-start(bf16[400,128]{1,0:T(8,128)(2,1)S(1)} %get-tuple-element.19), channel_id=1, source_target_pairs={{0,2},{1,3},{2,0},{3,1},{4,6},{5,7},{6,4},{7,5},{8,10},{9,11},{10,... | collective-permute-start | bytes 307208 | tf_op jit(solution)/shard_map/ppermute | solution.py:327
  31.8 0.2 collective-permute-start.5
  32.0 3.1 %all-to-all-done.1 = bf16[8,256,128]{2,1,0:T(8,128)(2,1)S(1)} async-done(((bf16[8,256,128]{2,1,0:T(8,128)(2,1)}), bf16[8,256,128]{2,1,0:T(8,128)(2,1)S(1)}, u32[]{:S(2)}, u32[]{:S(2)}) %all-to-all-start.1) | async-done | bytes 524320 | tf_op jit(solution)/shard_map/all_to_all | solution.py:302
  35.1 0.1 reduce_sum.12
  35.2 8.9 %all_gather.3.packed_ref = bf16[2048,128]{1,0:T(8,128)(2,1)S(1)} all-gather(bf16[256,128]{1,0:T(8,128)(2,1)S(1)} %reduce_sum.12), channel_id=1, replica_groups=mesh['rows'=8,'chan'=4] {'rows'}, dimensions={0}, use_global_device_ids=true | all-gather | bytes 589824 | tf_op jit(solution)/shard_map/all_gather | solution.py:329
  44.1 0.0 collective-permute-done.3.refs_1_
  44.1 0.0 collective-permute-done.4.refs_2_
  44.1 0.0 collective-permute-done.5.refs_3_
  44.1 1.2 %finish_kernel.1 = (bf16[8,48,128]{2,1,0:T(8,128)(2,1)}, f32[1296,192]{1,0:T(8,128)}) custom-call(bf16[2048,128]{1,0:T(8,128)(2,1)S(1)} %all_gather.3.packed_ref, bf16[384,128]{1,0:T(8,128)(2,1)S(1)} %bitcast.14, f32[400,128]{1,0:T(8,128)S(1)} %get-tuple-element.17.refs_0_, bf16[400,128]{1,0:T(8,128)(2,1)S(1)} %collective-permute-done.3.refs_1_, ...), custom_call_target="tpu_custom_call" | custom-call | tf_op jit(solution)/shard_map/finish_kernel/pallas_call | solution.py:330
  (7 shorter events, 0.0 us)
Async XLA Ops:
  0.6 18.4 %copy-start = (bf16[8,48,1,128]{3,1,2,0:T(8,128)(2,1)S(1)}, bf16[8,48,1,128]{3,1,2,0:T(8,128)(2,1)}, u32[]{:S(2)}) copy-start(bf16[8,48,1,128]{3,1,2,0:T(8,128)(2,1)} %param.9) | copy-start | bytes 294916
  0.6 18.4 %copy-start.1 = (f32[48]{0:T(128)S(1)}, f32[48]{0:T(128)}, u32[]{:S(2)}) copy-start(f32[48]{0:T(128)} %param.10) | copy-start | bytes 580
  0.7 18.4 %copy-start.3 = (s32[8]{0:T(128)S(1)}, s32[8]{0:T(128)}, u32[]{:S(2)}) copy-start(s32[8]{0:T(128)} %slot_ref.3) | copy-start | bytes 100
  2.4 16.7 %collective-permute-start.2 = (bf16[400,128]{1,0:T(8,128)(2,1)}, bf16[400,128]{1,0:T(8,128)(2,1)S(1)}, u32[]{:S(2)}, u32[]{:S(2)}) collective-permute-start(bf16[400,128]{1,0:T(8,128)(2,1)} %get-tuple-element.16), channel_id=1, source_target_pairs={{0,3},{1,2},{2,1},{3,0},{4,7},{5,6},{6,5},{7,4},{8,11},{9,10},{10,... | collective-permute-start | bytes 307208 | tf_op jit(solution)/shard_map/ppermute | solution.py:270
  7.4 11.6 %collective-permute-start.1 = (bf16[400,128]{1,0:T(8,128)(2,1)}, bf16[400,128]{1,0:T(8,128)(2,1)S(1)}, u32[]{:S(2)}, u32[]{:S(2)}) collective-permute-start(bf16[400,128]{1,0:T(8,128)(2,1)} %get-tuple-element.16), channel_id=1, source_target_pairs={{0,2},{1,3},{2,0},{3,1},{4,6},{5,7},{6,4},{7,5},{8,10},{9,11},{10,... | collective-permute-start | bytes 307208 | tf_op jit(solution)/shard_map/ppermute | solution.py:270
  7.4 11.6 %collective-permute-start = (bf16[400,128]{1,0:T(8,128)(2,1)}, bf16[400,128]{1,0:T(8,128)(2,1)S(1)}, u32[]{:S(2)}, u32[]{:S(2)}) collective-permute-start(bf16[400,128]{1,0:T(8,128)(2,1)} %get-tuple-element.16), channel_id=1, source_target_pairs={{0,1},{1,0},{2,3},{3,2},{4,5},{5,4},{6,7},{7,6},{8,9},{9,8},{10,11... | collective-permute-start | bytes 307208 | tf_op jit(solution)/shard_map/ppermute | solution.py:270
  19.1 6.4 %copy-start.2 = (bf16[27,48,192]{2,1,0:T(8,128)(2,1)S(1)}, bf16[27,48,192]{2,1,0:T(8,128)(2,1)}, u32[]{:S(2)}) copy-start(bf16[27,48,192]{2,1,0:T(8,128)(2,1)} %param.11) | copy-start | bytes 1492996
  21.9 13.2 %all-to-all-start.1 = ((bf16[8,256,128]{2,1,0:T(8,128)(2,1)}), bf16[8,256,128]{2,1,0:T(8,128)(2,1)S(1)}, u32[]{:S(2)}, u32[]{:S(2)}) async-start(bf16[8,256,128]{2,1,0:T(8,128)(2,1)} %bitcast.5), calls=%async_computation.1 | async-start | bytes 1048576 | tf_op jit(solution)/shard_map/all_to_all | solution.py:302
  27.5 16.5 %collective-permute-start.3 = (bf16[400,128]{1,0:T(8,128)(2,1)S(1)}, bf16[400,128]{1,0:T(8,128)(2,1)S(1)}, u32[]{:S(2)}, u32[]{:S(2)}) collective-permute-start(bf16[400,128]{1,0:T(8,128)(2,1)S(1)} %get-tuple-element.18), channel_id=1, source_target_pairs={{0,1},{1,0},{2,3},{3,2},{4,5},{5,4},{6,7},{7,6},{8,9},{9,8},{10,11... | collective-permute-start | bytes 307208 | tf_op jit(solution)/shard_map/ppermute | solution.py:327
  28.9 15.2 %collective-permute-start.4 = (bf16[400,128]{1,0:T(8,128)(2,1)S(1)}, bf16[400,128]{1,0:T(8,128)(2,1)S(1)}, u32[]{:S(2)}, u32[]{:S(2)}) collective-permute-start(bf16[400,128]{1,0:T(8,128)(2,1)S(1)} %get-tuple-element.19), channel_id=1, source_target_pairs={{0,2},{1,3},{2,0},{3,1},{4,6},{5,7},{6,4},{7,5},{8,10},{9,11},{10,... | collective-permute-start | bytes 307208 | tf_op jit(solution)/shard_map/ppermute | solution.py:327
  31.8 12.3 %collective-permute-start.5 = (bf16[400,128]{1,0:T(8,128)(2,1)S(1)}, bf16[400,128]{1,0:T(8,128)(2,1)S(1)}, u32[]{:S(2)}, u32[]{:S(2)}) collective-permute-start(bf16[400,128]{1,0:T(8,128)(2,1)S(1)} %get-tuple-element.20), channel_id=1, source_target_pairs={{0,3},{1,2},{2,1},{3,0},{4,7},{5,6},{6,5},{7,4},{8,11},{9,10},{10,... | collective-permute-start | bytes 307208 | tf_op jit(solution)/shard_map/ppermute | solution.py:327

commit v14 on v13

--- a/solution.py
+++ b/solution.py
@@ -136,7 +136,6 @@
     grad_ref, place, line, windows, hidden = refs[groups:]
     ins = groups * group
     width = adjoint_ref.shape[-1]
-    build_windows(frames, group, slot_ref, adjoint_ref, windows, place)
     gain = gains(gain_ref, line, x_refs, frames * group, group)
     for t in range(frames):
         scale, scaled = norm(x_refs, t, group)
@@ -146,6 +145,7 @@
             start = pl.multiple_of((at_ref[0] ^ s) * group, 16)
             hidden[pl.ds(start, group), pl.ds(t * width, width)] = value
 
+    build_windows(frames, group, slot_ref, adjoint_ref, windows, place)
     grad = lax.dot_general(
         windows[...], hidden[...], (((1,), (1,)), ((), ())), preferred_element_type=jnp.float32
     )

time: 45.6 us -> 45.6 us (level)
  no operation moved by 1% of the time
where the time goes in v14:
time: 45.6 us; the launch traced here: 45.3 us
  blocking collectives  19.9 us (44%)
  starting transfers between devices  13.6 us (30%)
  Pallas kernels  7.84 us (17%)
  waiting for transfers between devices  3.09 us (7%)
  between operations  0.72 us (2%)
    all_to_all x1, blocking collectives, shards(): lax.all_to_all(rows, 'rows', split_axis=0, concat_axis=0, tiled=True)  11 us
    all_gather x1, blocking collectives, shards(): whole = lax.all_gather(summed, 'rows', axis=0, tiled=True)  8.9 us
    ppermute x3, starting transfers between devices, shards(): lax.ppermute(payload, 'chan', partners[s])  5.62 us
    ppermute x3, starting transfers between devices, shards(): lax.ppermute(parts[s], 'chan', partners[s])  4.48 us
    all_to_all x1, starting transfers between devices, shards(): lax.all_to_all(packed.reshape(count, packed_rows // count, 128), 'rows',...  3.49 us
    all_to_all x1, waiting for transfers between devices, shards(): lax.all_to_all(packed.reshape(count, packed_rows // count, 128), 'rows',...  3.07 us
    pallas_call x1, Pallas kernels, shards(): pl.pallas_call(functools.partial(grad_kernel, frames, group, factor), out...  2.8 us
    pallas_call x1, Pallas kernels, shards(): pl.pallas_call(functools.partial(part_kernel, frames, group), out_shape=t...  2.11 us
  transfers between devices with their start and end apart: 7, of which 1 were waited for; matrix products, arithmetic and copies ran while one was open for 0% of the time, Pallas kernels for 5%

profile of v14, /device:TPU:0, one launch (start us, length us, event | category | flops | bytes accessed | tf_op | source)
XLA Modules:
  0.0 45.3 jit_solution(15055406040878292126)
XLA Ops:
  0.6 0.0 copy-start
  0.7 1.7 %prepare_kernel.1 = (bf16[8,3,48,128]{3,2,1,0:T(8,128)(2,1)S(1)}, bf16[400,128]{1,0:T(8,128)(2,1)}) custom-call(bf16[48,8,128]{2,1,0:T(8,128)(2,1)} %bitcast.19, bf16[8,48,128]{2,1,0:T(8,128)(2,1)} %bitcast.11, f32[1,48]{1,0:T(1,128)} %bitcast.15), custom_call_target="tpu_custom_call" | custom-call | tf_op jit(solution)/shard_map/prepare_kernel/pallas_call | solution.py:251
  2.4 5.0 %collective-permute-start.2 = (bf16[400,128]{1,0:T(8,128)(2,1)}, bf16[400,128]{1,0:T(8,128)(2,1)S(1)}, u32[]{:S(2)}, u32[]{:S(2)}) collective-permute-start(bf16[400,128]{1,0:T(8,128)(2,1)} %get-tuple-element.16), channel_id=1, source_target_pairs={{0,3},{1,2},{2,1},{3,0},{4,7},{5,6},{6,5},{7,4},{8,11},{9,10},{10,... | collective-permute-start | bytes 307208 | tf_op jit(solution)/shard_map/ppermute | solution.py:270
  7.4 0.0 collective-permute-start.1
  7.4 0.6 %collective-permute-start = (bf16[400,128]{1,0:T(8,128)(2,1)}, bf16[400,128]{1,0:T(8,128)(2,1)S(1)}, u32[]{:S(2)}, u32[]{:S(2)}) collective-permute-start(bf16[400,128]{1,0:T(8,128)(2,1)} %get-tuple-element.16), channel_id=1, source_target_pairs={{0,1},{1,0},{2,3},{3,2},{4,5},{5,4},{6,7},{7,6},{8,9},{9,8},{10,11... | collective-permute-start | bytes 307208 | tf_op jit(solution)/shard_map/ppermute | solution.py:270
  8.0 11.1 %conditional.1 = (bf16[8,3,48,128]{3,2,1,0:T(8,128)(2,1)S(1)}) conditional(s32[]{:T(128)} %convert_element_type.2, bf16[8,3,48,128]{3,2,1,0:T(8,128)(2,1)S(1)} %get-tuple-element.15, bf16[8,3,48,128]{3,2,1,0:T(8,128)(2,1)S(1)} %get-tuple-element.15), branch_computations={%region_0.1_spmd, %region_1.2_spmd} | conditional | bytes 1179656 | solution.py:272
  8.0 11.0 %all_to_all.9 = bf16[8,3,48,128]{3,2,1,0:T(8,128)(2,1)S(1)} all-to-all(bf16[8,3,48,128]{3,2,1,0:T(8,128)(2,1)S(1)} %copy.10), channel_id=1, replica_groups=mesh['rows'=8,'chan'=4] {'rows'}, dimensions={0} | all-to-all | bytes 589824 | tf_op jit(solution)/shard_map/cond/branch_1_fun/all_to_all | solution.py:274
  19.0 0.0 collective-permute-done.2.refs_3_
  19.0 0.0 collective-permute-done.1.refs_2_
  19.0 0.0 collective-permute-done.refs_1_
  19.1 0.0 copy-start.2
  19.1 2.8 %grad_kernel.1 = bf16[2048,128]{1,0:T(8,128)(2,1)} custom-call(s32[1]{0:T(128)} %bitcast.at_ref, s32[8]{0:T(128)S(1)} %copy-done.3, f32[1,48]{1,0:T(1,128)S(1)} %bitcast.16, bf16[8,3,48,128]{3,2,1,0:T(8,128)(2,1)S(1)} %get-tuple-element.25.adjoint_ref, bf16[384,128]{1,0:T(8,128)(2,1)S(1)} %bitcast.12, bf16[400,128]{1,0:T(8,128)(2,1)S(1)} %collective-permute-done.refs_1_, ...), custom_call_target="tpu_custom_call" | custom-call | flops 509607936 | bytes 3047424 | tf_op jit(solution)/shard_map/grad_kernel/pallas_call | solution.py:286
  21.9 3.5 %all-to-all-start.1 = ((bf16[8,256,128]{2,1,0:T(8,128)(2,1)}), bf16[8,256,128]{2,1,0:T(8,128)(2,1)S(1)}, u32[]{:S(2)}, u32[]{:S(2)}) async-start(bf16[8,256,128]{2,1,0:T(8,128)(2,1)} %bitcast.5), calls=%async_computation.1 | async-start | bytes 1048576 | tf_op jit(solution)/shard_map/all_to_all | solution.py:302
  25.4 2.1 %part_kernel.1 = (f32[400,128]{1,0:T(8,128)S(1)}, bf16[400,128]{1,0:T(8,128)(2,1)S(1)}, bf16[400,128]{1,0:T(8,128)(2,1)S(1)}, bf16[400,128]{1,0:T(8,128)(2,1)S(1)}) custom-call(s32[1]{0:T(128)} %bitcast.at_ref, s32[8]{0:T(128)S(1)} %copy-done.3, f32[1,48]{1,0:T(1,128)S(1)} %bitcast.17, bf16[8,3,48,128]{3,2,1,0:T(8,128)(2,1)S(1)} %get-tuple-element.25.adjoint_ref, ...), custom_call_target="tpu_custom_call" | custom-call | flops 509607936 | bytes 3047424 | tf_op jit(solution)/shard_map/part_kernel/pallas_call | solution.py:308
  27.5 1.3 %collective-permute-start.3 = (bf16[400,128]{1,0:T(8,128)(2,1)S(1)}, bf16[400,128]{1,0:T(8,128)(2,1)S(1)}, u32[]{:S(2)}, u32[]{:S(2)}) collective-permute-start(bf16[400,128]{1,0:T(8,128)(2,1)S(1)} %get-tuple-element.18), channel_id=1, source_target_pairs={{0,1},{1,0},{2,3},{3,2},{4,5},{5,4},{6,7},{7,6},{8,9},{9,8},{10,11... | collective-permute-start | bytes 307208 | tf_op jit(solution)/shard_map/ppermute | solution.py:327
  28.8 2.9 %collective-permute-start.4 = (bf16[400,128]{1,0:T(8,128)(2,1)S(1)}, bf16[400,128]{1,0:T(8,128)(2,1)S(1)}, u32[]{:S(2)}, u32[]{:S(2)}) collective-permute-start(bf16[400,128]{1,0:T(8,128)(2,1)S(1)} %get-tuple-element.19), channel_id=1, source_target_pairs={{0,2},{1,3},{2,0},{3,1},{4,6},{5,7},{6,4},{7,5},{8,10},{9,11},{10,... | collective-permute-start | bytes 307208 | tf_op jit(solution)/shard_map/ppermute | solution.py:327
  31.8 0.2 collective-permute-start.5
  32.0 3.1 %all-to-all-done.1 = bf16[8,256,128]{2,1,0:T(8,128)(2,1)S(1)} async-done(((bf16[8,256,128]{2,1,0:T(8,128)(2,1)}), bf16[8,256,128]{2,1,0:T(8,128)(2,1)S(1)}, u32[]{:S(2)}, u32[]{:S(2)}) %all-to-all-start.1) | async-done | bytes 524320 | tf_op jit(solution)/shard_map/all_to_all | solution.py:302
  35.1 0.1 reduce_sum.12
  35.1 8.9 %all_gather.3.packed_ref = bf16[2048,128]{1,0:T(8,128)(2,1)S(1)} all-gather(bf16[256,128]{1,0:T(8,128)(2,1)S(1)} %reduce_sum.12), channel_id=1, replica_groups=mesh['rows'=8,'chan'=4] {'rows'}, dimensions={0}, use_global_device_ids=true | all-gather | bytes 589824 | tf_op jit(solution)/shard_map/all_gather | solution.py:329
  44.0 0.0 collective-permute-done.3.refs_1_
  44.0 0.0 collective-permute-done.4.refs_2_
  44.1 0.0 collective-permute-done.5.refs_3_
  44.1 1.2 %finish_kernel.1 = (bf16[8,48,128]{2,1,0:T(8,128)(2,1)}, f32[1296,192]{1,0:T(8,128)}) custom-call(bf16[2048,128]{1,0:T(8,128)(2,1)S(1)} %all_gather.3.packed_ref, bf16[384,128]{1,0:T(8,128)(2,1)S(1)} %bitcast.14, f32[400,128]{1,0:T(8,128)S(1)} %get-tuple-element.17.refs_0_, bf16[400,128]{1,0:T(8,128)(2,1)S(1)} %collective-permute-done.3.refs_1_, ...), custom_call_target="tpu_custom_call" | custom-call | tf_op jit(solution)/shard_map/finish_kernel/pallas_call | solution.py:330
  (7 shorter events, 0.0 us)
Async XLA Ops:
  0.6 18.4 %copy-start = (bf16[8,48,1,128]{3,1,2,0:T(8,128)(2,1)S(1)}, bf16[8,48,1,128]{3,1,2,0:T(8,128)(2,1)}, u32[]{:S(2)}) copy-start(bf16[8,48,1,128]{3,1,2,0:T(8,128)(2,1)} %param.9) | copy-start | bytes 294916
  0.6 18.4 %copy-start.1 = (f32[48]{0:T(128)S(1)}, f32[48]{0:T(128)}, u32[]{:S(2)}) copy-start(f32[48]{0:T(128)} %param.10) | copy-start | bytes 580
  0.7 18.4 %copy-start.3 = (s32[8]{0:T(128)S(1)}, s32[8]{0:T(128)}, u32[]{:S(2)}) copy-start(s32[8]{0:T(128)} %slot_ref.3) | copy-start | bytes 100
  2.4 16.7 %collective-permute-start.2 = (bf16[400,128]{1,0:T(8,128)(2,1)}, bf16[400,128]{1,0:T(8,128)(2,1)S(1)}, u32[]{:S(2)}, u32[]{:S(2)}) collective-permute-start(bf16[400,128]{1,0:T(8,128)(2,1)} %get-tuple-element.16), channel_id=1, source_target_pairs={{0,3},{1,2},{2,1},{3,0},{4,7},{5,6},{6,5},{7,4},{8,11},{9,10},{10,... | collective-permute-start | bytes 307208 | tf_op jit(solution)/shard_map/ppermute | solution.py:270
  7.4 11.6 %collective-permute-start.1 = (bf16[400,128]{1,0:T(8,128)(2,1)}, bf16[400,128]{1,0:T(8,128)(2,1)S(1)}, u32[]{:S(2)}, u32[]{:S(2)}) collective-permute-start(bf16[400,128]{1,0:T(8,128)(2,1)} %get-tuple-element.16), channel_id=1, source_target_pairs={{0,2},{1,3},{2,0},{3,1},{4,6},{5,7},{6,4},{7,5},{8,10},{9,11},{10,... | collective-permute-start | bytes 307208 | tf_op jit(solution)/shard_map/ppermute | solution.py:270
  7.4 11.6 %collective-permute-start = (bf16[400,128]{1,0:T(8,128)(2,1)}, bf16[400,128]{1,0:T(8,128)(2,1)S(1)}, u32[]{:S(2)}, u32[]{:S(2)}) collective-permute-start(bf16[400,128]{1,0:T(8,128)(2,1)} %get-tuple-element.16), channel_id=1, source_target_pairs={{0,1},{1,0},{2,3},{3,2},{4,5},{5,4},{6,7},{7,6},{8,9},{9,8},{10,11... | collective-permute-start | bytes 307208 | tf_op jit(solution)/shard_map/ppermute | solution.py:270
  19.1 6.3 %copy-start.2 = (bf16[27,48,192]{2,1,0:T(8,128)(2,1)S(1)}, bf16[27,48,192]{2,1,0:T(8,128)(2,1)}, u32[]{:S(2)}) copy-start(bf16[27,48,192]{2,1,0:T(8,128)(2,1)} %param.11) | copy-start | bytes 1492996
  21.9 13.2 %all-to-all-start.1 = ((bf16[8,256,128]{2,1,0:T(8,128)(2,1)}), bf16[8,256,128]{2,1,0:T(8,128)(2,1)S(1)}, u32[]{:S(2)}, u32[]{:S(2)}) async-start(bf16[8,256,128]{2,1,0:T(8,128)(2,1)} %bitcast.5), calls=%async_computation.1 | async-start | bytes 1048576 | tf_op jit(solution)/shard_map/all_to_all | solution.py:302
  27.5 16.5 %collective-permute-start.3 = (bf16[400,128]{1,0:T(8,128)(2,1)S(1)}, bf16[400,128]{1,0:T(8,128)(2,1)S(1)}, u32[]{:S(2)}, u32[]{:S(2)}) collective-permute-start(bf16[400,128]{1,0:T(8,128)(2,1)S(1)} %get-tuple-element.18), channel_id=1, source_target_pairs={{0,1},{1,0},{2,3},{3,2},{4,5},{5,4},{6,7},{7,6},{8,9},{9,8},{10,11... | collective-permute-start | bytes 307208 | tf_op jit(solution)/shard_map/ppermute | solution.py:327
  28.8 15.2 %collective-permute-start.4 = (bf16[400,128]{1,0:T(8,128)(2,1)S(1)}, bf16[400,128]{1,0:T(8,128)(2,1)S(1)}, u32[]{:S(2)}, u32[]{:S(2)}) collective-permute-start(bf16[400,128]{1,0:T(8,128)(2,1)S(1)} %get-tuple-element.19), channel_id=1, source_target_pairs={{0,2},{1,3},{2,0},{3,1},{4,6},{5,7},{6,4},{7,5},{8,10},{9,11},{10,... | collective-permute-start | bytes 307208 | tf_op jit(solution)/shard_map/ppermute | solution.py:327
  31.8 12.3 %collective-permute-start.5 = (bf16[400,128]{1,0:T(8,128)(2,1)S(1)}, bf16[400,128]{1,0:T(8,128)(2,1)S(1)}, u32[]{:S(2)}, u32[]{:S(2)}) collective-permute-start(bf16[400,128]{1,0:T(8,128)(2,1)S(1)} %get-tuple-element.20), channel_id=1, source_target_pairs={{0,3},{1,2},{2,1},{3,0},{4,7},{5,6},{6,5},{7,4},{8,11},{9,10},{10,... | collective-permute-start | bytes 307208 | tf_op jit(solution)/shard_map/ppermute | solution.py:327

commit v15 on v13

--- a/solution.py
+++ b/solution.py
@@ -131,9 +131,9 @@
 
 
 def grad_kernel(frames, group, factor, at_ref, slot_ref, gain_ref, adjoint_ref, *refs):
-    groups = len(refs) - 5
+    groups = len(refs) - 7
     x_refs = refs[:groups]
-    grad_ref, place, line, windows, hidden = refs[groups:]
+    grad_ref, place, line, windows, hidden, packed, moved = refs[groups:]
     ins = groups * group
     width = adjoint_ref.shape[-1]
     build_windows(frames, group, slot_ref, adjoint_ref, windows, place)
@@ -146,30 +146,41 @@
             start = pl.multiple_of((at_ref[0] ^ s) * group, 16)
             hidden[pl.ds(start, group), pl.ds(t * width, width)] = value
 
-    grad = lax.dot_general(
-        windows[...], hidden[...], (((1,), (1,)), ((), ())), preferred_element_type=jnp.float32
-    )
-    grad = grad * factor
-    taps_out = grad.shape[0]
+    taps_out = windows.shape[0]
     blocks, rest, half, rows = packing(taps_out, ins, 1)
-    for block in range(blocks):
-        grad_ref[pl.ds(block * taps_out, taps_out), :] = grad[
-            :, block * 128 : block * 128 + 128
-        ].astype(jnp.bfloat16)
+    part = taps_out // 3
     base = blocks * taps_out
+    leaving = []
+    if packed.shape[0] > base + half:
+        tail = packed.shape[0] - base - half
+        packed[pl.ds(base + half, tail), :] = jnp.zeros((tail, 128), jnp.bfloat16)
     if rest:
-        left = grad[:half, blocks * 128 :]
-        right = grad[half:, blocks * 128 :]
-        right = jnp.concatenate(
-            [right, jnp.zeros((2 * half - taps_out, rest), jnp.float32)], axis=0
+        packed[pl.ds(base, half), :] = jnp.zeros((half, 128), jnp.bfloat16)
+    for p in range(3):
+        first = p * part
+        grad = factor * lax.dot_general(
+            windows[pl.ds(first, part), :], hidden[...], (((1,), (1,)), ((), ())),
+            preferred_element_type=jnp.float32,
         )
-        grad_ref[pl.ds(base, half), :] = jnp.concatenate([left, right], axis=1).astype(
-            jnp.bfloat16
-        )
-        base = base + half
-    tail = grad_ref.shape[0] - base
-    if tail:
-        grad_ref[pl.ds(base, tail), :] = jnp.zeros((tail, 128), jnp.bfloat16)
+        for block in range(blocks):
+            span = pl.ds(block * taps_out + first, part)
+            packed[span, :] = grad[:, block * 128 : block * 128 + 128].astype(jnp.bfloat16)
+            leaving.append((span, len(leaving)))
+            pltpu.make_async_copy(packed.at[span], grad_ref.at[span], moved.at[len(leaving) - 1]).start()
+        if rest:
+            for begin, end, low in ((0, half, 0), (half, taps_out, rest)):
+                begin, end = max(begin, first), min(end, first + part)
+                if begin < end:
+                    shift = half if low else 0
+                    packed[pl.ds(base + begin - shift, end - begin), pl.ds(low, rest)] = grad[
+                        begin - first : end - first, blocks * 128 :
+                    ].astype(jnp.bfloat16)
+    span = pl.ds(base, packed.shape[0] - base)
+    if packed.shape[0] > base:
+        leaving.append((span, len(leaving)))
+        pltpu.make_async_copy(packed.at[span], grad_ref.at[span], moved.at[len(leaving) - 1]).start()
+    for span, k in leaving:
+        pltpu.make_async_copy(packed.at[span], grad_ref.at[span], moved.at[k]).wait()
 
 
 def part_kernel(frames, group, at_ref, slot_ref, gain_ref, adjoint_ref, weight_ref, *refs):
@@ -287,12 +298,14 @@
         functools.partial(grad_kernel, frames, group, factor),
         out_shape=jax.ShapeDtypeStruct((packed_rows, 128), jnp.bfloat16),
         in_specs=[smem(), smem()] + [copied()] * (groups + 2),
-        out_specs=vmem(),
+        out_specs=pl.BlockSpec(memory_space=pl.ANY),
         scratch_shapes=[
             pltpu.SMEM((frames,), jnp.int32),
             pltpu.VMEM((8, 128), jnp.float32),
             pltpu.VMEM((taps_out, pixels), jnp.bfloat16),
             pltpu.VMEM((ins, pixels), jnp.bfloat16),
+            pltpu.VMEM((packed_rows, 128), jnp.bfloat16),
+            pltpu.SemaphoreType.DMA((3 * (ins // 128) + 1,)),
         ],
         compiler_params=limit(taps_out, pixels),
         cost_estimate=cost(taps_out, ins, pixels),

time: 45.6 us -> 45.6 us (level)
  no operation moved by 1% of the time
where the time goes in v15:
time: 45.6 us; the launch traced here: 45.3 us
  blocking collectives  19.9 us (44%)
  starting transfers between devices  13.6 us (30%)
  Pallas kernels  7.82 us (17%)
  waiting for transfers between devices  3.09 us (7%)
  between operations  0.73 us (2%)
    all_to_all x1, blocking collectives, shards(): lax.all_to_all(rows, 'rows', split_axis=0, concat_axis=0, tiled=True)  11 us
    all_gather x1, blocking collectives, shards(): whole = lax.all_gather(summed, 'rows', axis=0, tiled=True)  8.9 us
    ppermute x3, starting transfers between devices, shards(): lax.ppermute(payload, 'chan', partners[s])  5.62 us
    ppermute x3, starting transfers between devices, shards(): lax.ppermute(parts[s], 'chan', partners[s])  4.48 us
    all_to_all x1, starting transfers between devices, shards(): lax.all_to_all(packed.reshape(count, packed_rows // count, 128), 'rows',...  3.51 us
    all_to_all x1, waiting for transfers between devices, shards(): lax.all_to_all(packed.reshape(count, packed_rows // count, 128), 'rows',...  3.08 us
    pallas_call x1, Pallas kernels, shards(): pl.pallas_call(functools.partial(grad_kernel, frames, group, factor), out...  2.78 us
    pallas_call x1, Pallas kernels, shards(): pl.pallas_call(functools.partial(part_kernel, frames, group), out_shape=t...  2.1 us
  transfers between devices with their start and end apart: 7, of which 1 were waited for; matrix products, arithmetic and copies ran while one was open for 0% of the time, Pallas kernels for 5%

profile of v15, /device:TPU:0, one launch (start us, length us, event | category | flops | bytes accessed | tf_op | source)
XLA Modules:
  0.0 45.3 jit_solution(7399743987287441227)
XLA Ops:
  0.6 0.0 copy-start
  0.7 1.7 %prepare_kernel.1 = (bf16[8,3,48,128]{3,2,1,0:T(8,128)(2,1)S(1)}, bf16[400,128]{1,0:T(8,128)(2,1)}) custom-call(bf16[48,8,128]{2,1,0:T(8,128)(2,1)} %bitcast.19, bf16[8,48,128]{2,1,0:T(8,128)(2,1)} %bitcast.11, f32[1,48]{1,0:T(1,128)} %bitcast.15), custom_call_target="tpu_custom_call" | custom-call | tf_op jit(solution)/shard_map/prepare_kernel/pallas_call | solution.py:262
  2.4 5.0 %collective-permute-start.2 = (bf16[400,128]{1,0:T(8,128)(2,1)}, bf16[400,128]{1,0:T(8,128)(2,1)S(1)}, u32[]{:S(2)}, u32[]{:S(2)}) collective-permute-start(bf16[400,128]{1,0:T(8,128)(2,1)} %get-tuple-element.16), channel_id=1, source_target_pairs={{0,3},{1,2},{2,1},{3,0},{4,7},{5,6},{6,5},{7,4},{8,11},{9,10},{10,... | collective-permute-start | bytes 307208 | tf_op jit(solution)/shard_map/ppermute | solution.py:281
  7.4 0.0 collective-permute-start.1
  7.4 0.6 %collective-permute-start = (bf16[400,128]{1,0:T(8,128)(2,1)}, bf16[400,128]{1,0:T(8,128)(2,1)S(1)}, u32[]{:S(2)}, u32[]{:S(2)}) collective-permute-start(bf16[400,128]{1,0:T(8,128)(2,1)} %get-tuple-element.16), channel_id=1, source_target_pairs={{0,1},{1,0},{2,3},{3,2},{4,5},{5,4},{6,7},{7,6},{8,9},{9,8},{10,11... | collective-permute-start | bytes 307208 | tf_op jit(solution)/shard_map/ppermute | solution.py:281
  8.0 11.1 %conditional.1 = (bf16[8,3,48,128]{3,2,1,0:T(8,128)(2,1)S(1)}) conditional(s32[]{:T(128)} %convert_element_type.2, bf16[8,3,48,128]{3,2,1,0:T(8,128)(2,1)S(1)} %get-tuple-element.15, bf16[8,3,48,128]{3,2,1,0:T(8,128)(2,1)S(1)} %get-tuple-element.15), branch_computations={%region_0.1_spmd, %region_1.2_spmd} | conditional | bytes 1179656 | solution.py:283
  8.0 11.0 %all_to_all.9 = bf16[8,3,48,128]{3,2,1,0:T(8,128)(2,1)S(1)} all-to-all(bf16[8,3,48,128]{3,2,1,0:T(8,128)(2,1)S(1)} %copy.10), channel_id=1, replica_groups=mesh['rows'=8,'chan'=4] {'rows'}, dimensions={0} | all-to-all | bytes 589824 | tf_op jit(solution)/shard_map/cond/branch_1_fun/all_to_all | solution.py:285
  19.0 0.0 collective-permute-done.2.refs_3_
  19.0 0.0 collective-permute-done.1.refs_2_
  19.0 0.0 collective-permute-done.refs_1_
  19.1 0.0 copy-start.2
  19.1 2.8 %grad_kernel.1 = bf16[2048,128]{1,0:T(8,128)(2,1)} custom-call(s32[1]{0:T(128)} %bitcast.at_ref, s32[8]{0:T(128)S(1)} %copy-done.3, f32[1,48]{1,0:T(1,128)S(1)} %bitcast.16, bf16[8,3,48,128]{3,2,1,0:T(8,128)(2,1)S(1)} %get-tuple-element.25.adjoint_ref, bf16[384,128]{1,0:T(8,128)(2,1)S(1)} %bitcast.12, bf16[400,128]{1,0:T(8,128)(2,1)S(1)} %collective-permute-done.refs_1_, ...), custom_call_target="tpu_custom_call" | custom-call | flops 509607936 | bytes 3047424 | tf_op jit(solution)/shard_map/grad_kernel/pallas_call | solution.py:297
  21.9 3.5 %all-to-all-start.1 = ((bf16[8,256,128]{2,1,0:T(8,128)(2,1)}), bf16[8,256,128]{2,1,0:T(8,128)(2,1)S(1)}, u32[]{:S(2)}, u32[]{:S(2)}) async-start(bf16[8,256,128]{2,1,0:T(8,128)(2,1)} %bitcast.5), calls=%async_computation.1 | async-start | bytes 1048576 | tf_op jit(solution)/shard_map/all_to_all | solution.py:315
  25.4 2.1 %part_kernel.1 = (f32[400,128]{1,0:T(8,128)S(1)}, bf16[400,128]{1,0:T(8,128)(2,1)S(1)}, bf16[400,128]{1,0:T(8,128)(2,1)S(1)}, bf16[400,128]{1,0:T(8,128)(2,1)S(1)}) custom-call(s32[1]{0:T(128)} %bitcast.at_ref, s32[8]{0:T(128)S(1)} %copy-done.3, f32[1,48]{1,0:T(1,128)S(1)} %bitcast.17, bf16[8,3,48,128]{3,2,1,0:T(8,128)(2,1)S(1)} %get-tuple-element.25.adjoint_ref, ...), custom_call_target="tpu_custom_call" | custom-call | flops 509607936 | bytes 3047424 | tf_op jit(solution)/shard_map/part_kernel/pallas_call | solution.py:321
  27.5 1.3 %collective-permute-start.3 = (bf16[400,128]{1,0:T(8,128)(2,1)S(1)}, bf16[400,128]{1,0:T(8,128)(2,1)S(1)}, u32[]{:S(2)}, u32[]{:S(2)}) collective-permute-start(bf16[400,128]{1,0:T(8,128)(2,1)S(1)} %get-tuple-element.18), channel_id=1, source_target_pairs={{0,1},{1,0},{2,3},{3,2},{4,5},{5,4},{6,7},{7,6},{8,9},{9,8},{10,11... | collective-permute-start | bytes 307208 | tf_op jit(solution)/shard_map/ppermute | solution.py:340
  28.8 2.9 %collective-permute-start.4 = (bf16[400,128]{1,0:T(8,128)(2,1)S(1)}, bf16[400,128]{1,0:T(8,128)(2,1)S(1)}, u32[]{:S(2)}, u32[]{:S(2)}) collective-permute-start(bf16[400,128]{1,0:T(8,128)(2,1)S(1)} %get-tuple-element.19), channel_id=1, source_target_pairs={{0,2},{1,3},{2,0},{3,1},{4,6},{5,7},{6,4},{7,5},{8,10},{9,11},{10,... | collective-permute-start | bytes 307208 | tf_op jit(solution)/shard_map/ppermute | solution.py:340
  31.8 0.2 collective-permute-start.5
  32.0 3.1 %all-to-all-done.1 = bf16[8,256,128]{2,1,0:T(8,128)(2,1)S(1)} async-done(((bf16[8,256,128]{2,1,0:T(8,128)(2,1)}), bf16[8,256,128]{2,1,0:T(8,128)(2,1)S(1)}, u32[]{:S(2)}, u32[]{:S(2)}) %all-to-all-start.1) | async-done | bytes 524320 | tf_op jit(solution)/shard_map/all_to_all | solution.py:315
  35.1 0.1 reduce_sum.12
  35.1 8.9 %all_gather.3.packed_ref = bf16[2048,128]{1,0:T(8,128)(2,1)S(1)} all-gather(bf16[256,128]{1,0:T(8,128)(2,1)S(1)} %reduce_sum.12), channel_id=1, replica_groups=mesh['rows'=8,'chan'=4] {'rows'}, dimensions={0}, use_global_device_ids=true | all-gather | bytes 589824 | tf_op jit(solution)/shard_map/all_gather | solution.py:342
  44.0 0.0 collective-permute-done.3.refs_1_
  44.0 0.0 collective-permute-done.4.refs_2_
  44.1 0.0 collective-permute-done.5.refs_3_
  44.1 1.2 %finish_kernel.1 = (bf16[8,48,128]{2,1,0:T(8,128)(2,1)}, f32[1296,192]{1,0:T(8,128)}) custom-call(bf16[2048,128]{1,0:T(8,128)(2,1)S(1)} %all_gather.3.packed_ref, bf16[384,128]{1,0:T(8,128)(2,1)S(1)} %bitcast.14, f32[400,128]{1,0:T(8,128)S(1)} %get-tuple-element.17.refs_0_, bf16[400,128]{1,0:T(8,128)(2,1)S(1)} %collective-permute-done.3.refs_1_, ...), custom_call_target="tpu_custom_call" | custom-call | tf_op jit(solution)/shard_map/finish_kernel/pallas_call | solution.py:343
  (7 shorter events, 0.0 us)
Async XLA Ops:
  0.6 18.4 %copy-start = (bf16[8,48,1,128]{3,1,2,0:T(8,128)(2,1)S(1)}, bf16[8,48,1,128]{3,1,2,0:T(8,128)(2,1)}, u32[]{:S(2)}) copy-start(bf16[8,48,1,128]{3,1,2,0:T(8,128)(2,1)} %param.9) | copy-start | bytes 294916
  0.6 18.4 %copy-start.1 = (f32[48]{0:T(128)S(1)}, f32[48]{0:T(128)}, u32[]{:S(2)}) copy-start(f32[48]{0:T(128)} %param.10) | copy-start | bytes 580
  0.7 18.4 %copy-start.3 = (s32[8]{0:T(128)S(1)}, s32[8]{0:T(128)}, u32[]{:S(2)}) copy-start(s32[8]{0:T(128)} %slot_ref.3) | copy-start | bytes 100
  2.4 16.7 %collective-permute-start.2 = (bf16[400,128]{1,0:T(8,128)(2,1)}, bf16[400,128]{1,0:T(8,128)(2,1)S(1)}, u32[]{:S(2)}, u32[]{:S(2)}) collective-permute-start(bf16[400,128]{1,0:T(8,128)(2,1)} %get-tuple-element.16), channel_id=1, source_target_pairs={{0,3},{1,2},{2,1},{3,0},{4,7},{5,6},{6,5},{7,4},{8,11},{9,10},{10,... | collective-permute-start | bytes 307208 | tf_op jit(solution)/shard_map/ppermute | solution.py:281
  7.4 11.6 %collective-permute-start.1 = (bf16[400,128]{1,0:T(8,128)(2,1)}, bf16[400,128]{1,0:T(8,128)(2,1)S(1)}, u32[]{:S(2)}, u32[]{:S(2)}) collective-permute-start(bf16[400,128]{1,0:T(8,128)(2,1)} %get-tuple-element.16), channel_id=1, source_target_pairs={{0,2},{1,3},{2,0},{3,1},{4,6},{5,7},{6,4},{7,5},{8,10},{9,11},{10,... | collective-permute-start | bytes 307208 | tf_op jit(solution)/shard_map/ppermute | solution.py:281
  7.4 11.6 %collective-permute-start = (bf16[400,128]{1,0:T(8,128)(2,1)}, bf16[400,128]{1,0:T(8,128)(2,1)S(1)}, u32[]{:S(2)}, u32[]{:S(2)}) collective-permute-start(bf16[400,128]{1,0:T(8,128)(2,1)} %get-tuple-element.16), channel_id=1, source_target_pairs={{0,1},{1,0},{2,3},{3,2},{4,5},{5,4},{6,7},{7,6},{8,9},{9,8},{10,11... | collective-permute-start | bytes 307208 | tf_op jit(solution)/shard_map/ppermute | solution.py:281
  19.1 6.3 %copy-start.2 = (bf16[27,48,192]{2,1,0:T(8,128)(2,1)S(1)}, bf16[27,48,192]{2,1,0:T(8,128)(2,1)}, u32[]{:S(2)}) copy-start(bf16[27,48,192]{2,1,0:T(8,128)(2,1)} %param.11) | copy-start | bytes 1492996
  21.9 13.2 %all-to-all-start.1 = ((bf16[8,256,128]{2,1,0:T(8,128)(2,1)}), bf16[8,256,128]{2,1,0:T(8,128)(2,1)S(1)}, u32[]{:S(2)}, u32[]{:S(2)}) async-start(bf16[8,256,128]{2,1,0:T(8,128)(2,1)} %bitcast.5), calls=%async_computation.1 | async-start | bytes 1048576 | tf_op jit(solution)/shard_map/all_to_all | solution.py:315
  27.5 16.5 %collective-permute-start.3 = (bf16[400,128]{1,0:T(8,128)(2,1)S(1)}, bf16[400,128]{1,0:T(8,128)(2,1)S(1)}, u32[]{:S(2)}, u32[]{:S(2)}) collective-permute-start(bf16[400,128]{1,0:T(8,128)(2,1)S(1)} %get-tuple-element.18), channel_id=1, source_target_pairs={{0,1},{1,0},{2,3},{3,2},{4,5},{5,4},{6,7},{7,6},{8,9},{9,8},{10,11... | collective-permute-start | bytes 307208 | tf_op jit(solution)/shard_map/ppermute | solution.py:340
  28.8 15.2 %collective-permute-start.4 = (bf16[400,128]{1,0:T(8,128)(2,1)S(1)}, bf16[400,128]{1,0:T(8,128)(2,1)S(1)}, u32[]{:S(2)}, u32[]{:S(2)}) collective-permute-start(bf16[400,128]{1,0:T(8,128)(2,1)S(1)} %get-tuple-element.19), channel_id=1, source_target_pairs={{0,2},{1,3},{2,0},{3,1},{4,6},{5,7},{6,4},{7,5},{8,10},{9,11},{10,... | collective-permute-start | bytes 307208 | tf_op jit(solution)/shard_map/ppermute | solution.py:340
  31.8 12.3 %collective-permute-start.5 = (bf16[400,128]{1,0:T(8,128)(2,1)S(1)}, bf16[400,128]{1,0:T(8,128)(2,1)S(1)}, u32[]{:S(2)}, u32[]{:S(2)}) collective-permute-start(bf16[400,128]{1,0:T(8,128)(2,1)S(1)} %get-tuple-element.20), channel_id=1, source_target_pairs={{0,3},{1,2},{2,1},{3,0},{4,7},{5,6},{6,5},{7,4},{8,11},{9,10},{10,... | collective-permute-start | bytes 307208 | tf_op jit(solution)/shard_map/ppermute | solution.py:340
